TPU v7x, 32 devices: a whole 2x2x4 slice. The times are simulated.
32 devices in a mesh: groups: 2 (over y), plane: 4 (over z), span: 2 (over x), wall: 2 (over core).
Axes of the slice: x: 2, y: 2, z: 4, core: 2. Of those that a mesh axis runs over, the one named last changes fastest.
Arguments:
- velocity: float32 [6, 32, 128, 512], P('groups', 'wall', 'plane', 'span'), parts along dimension 0, may hold values from -5 to 5
- levels: int32 [256, 512], P(('groups', 'plane'), 'span'), parts along dimension 0, may hold values from 1 to 30
- fraction: float32 [256, 512], P(('groups', 'plane'), 'span'), parts along dimension 0, may hold values from 0.2 to 1
- bed_height: float32 [256, 512], P(('groups', 'plane', 'span', 'wall')), parts along dimension 0, may hold values from -4 to 4
Outputs:
- velocity_next: float32 [6, 32, 128, 512], P('groups', 'wall', 'plane', 'span'), parts along dimension 0
- bed_next: float32 [256, 512], P(('groups', 'plane'), 'span'), parts along dimension 0
There are 2 independent parts, one for each index of `groups`. A program takes and returns all parts, laid end to end along the dimension named above; each array names one. Nothing has to cross between parts.
All inputs are finite; a program needn't handle non-finite values.
Results may differ from a plain program's by a relative error of at most 0.00002.
Values sent between devices are 32-bit elements; how exact they have to be, the bound alone decides.
No kernel may reach another device: no remote copies, remote signals or barrier semaphores. Data moves between devices by JAX's collectives and lax.ppermute only.
A program may use at most 64 MiB of HBM per device.

v0:
```python
import jax
import jax.numpy as jnp
from jax import lax
from jax.sharding import PartitionSpec as P

time_step = 0.1
viscosity = 0.5
bed_step = 0.4
slope_rate = 0.25
threshold_sq = 0.25


def extended_2(x, sides, width):
    for axis, dim in sides:
        size, length = (lax.axis_size(axis), x.shape[dim])
        up = [(i, (i + 1) % size) for i in range(size - 1)]
        down = [(j, i) for i, j in up]
        last = lax.slice_in_dim(x, length - width, length, axis=dim)
        initial = lax.slice_in_dim(x, 0, width, axis=dim)
        before = lax.ppermute(last, axis, up)
        after = lax.ppermute(initial, axis, down)
        x = jnp.concatenate([before, x, after], axis=dim)
    return x


def openness(levels, fraction, layers):
    return jnp.where(
        layers == levels[None], fraction[None], jnp.where(layers > levels[None], 1.0, 0.0)
    )


def window(field, axis, offset):
    starts = [2, 2, 2]
    starts[axis] = starts[axis] + offset
    depth = field.shape[0] - 4
    rows = field.shape[1] - 4
    cols = field.shape[2] - 4
    return field[
        starts[0] : starts[0] + depth, starts[1] : starts[1] + rows, starts[2] : starts[2] + cols
    ]


def fourth_wide(field, axis):
    near = window(field, axis, 1) - window(field, axis, -1)
    far = window(field, axis, 2) - window(field, axis, -2)
    return (8.0 * near - far) / 12.0


def side_pad(field):
    return jnp.pad(field, ((0, 0), (1, 1)))


def tile_divergence(shear_rows):
    square = shear_rows[0] * shear_rows[0] + shear_rows[1] * shear_rows[1]
    factor = jnp.maximum(square - threshold_sq, 0.0) / (square + threshold_sq)
    load_x = side_pad(shear_rows[0] * factor)[1:-1]
    load_y = shear_rows[1] * factor
    return 0.5 * (load_x[:, 2:] - load_x[:, :-2]) + 0.5 * (load_y[2:] - load_y[:-2])


def tile_smooth(height_rows):
    padded = side_pad(height_rows[1:-1])
    centre = height_rows[1:-1]
    return height_rows[2:] + height_rows[:-2] + padded[:, 2:] + padded[:, :-2] - 4.0 * centre


def body(velocity, levels, fraction, bed_height):
    layers_dev = velocity.shape[1]
    rows_dev = velocity.shape[2]
    cols_dev = velocity.shape[3]
    wall_count = lax.axis_size("wall")
    span_count = lax.axis_size("span")
    tile_count = span_count * wall_count
    tile_rows = rows_dev // tile_count
    heights = lax.axis_index("wall") * layers_dev + jnp.arange(layers_dev, dtype=jnp.int32)
    own_open = openness(levels, fraction, heights[:, None, None])
    stacked = jnp.concatenate([velocity, own_open[None]], axis=0)
    extended = extended_2(stacked, (("wall", 1), ("plane", 2), ("span", 3)), 2)
    moving = extended[:3]
    open_wide = extended[3]
    carried = open_wide[None] * moving
    along = (2, 1, 0)
    updated = []
    for component in range(3):
        advect = fourth_wide(moving[0] * carried[component], along[0])
        advect = advect + fourth_wide(moving[1] * carried[component], along[1])
        advect = advect + fourth_wide(moving[2] * carried[component], along[2])
        centre = window(carried[component], 0, 0)
        diffuse = -6.0 * centre
        for axis in range(3):
            diffuse = (
                diffuse + window(carried[component], axis, 1) + window(carried[component], axis, -1)
            )
        change = -advect + viscosity * diffuse
        updated.append(velocity[component] + time_step * own_open * change)
    velocity_next = jnp.stack(updated)
    cutting = jnp.where(heights[:, None, None] == levels[None], 1.0, 0.0)
    scale = 1.0 / (0.5 + fraction)
    shear = jnp.stack(
        [
            jnp.sum(cutting * velocity_next[0], axis=0) * scale,
            jnp.sum(cutting * velocity_next[1], axis=0) * scale,
        ]
    )
    outgoing = shear.reshape(2, tile_count, tile_rows, cols_dev)
    arrived = lax.all_to_all(outgoing, ("span", "wall"), split_axis=1, concat_axis=3, tiled=True)
    tiles = arrived.reshape(2, tile_rows, span_count, wall_count, cols_dev).sum(axis=3)
    tiles = tiles.reshape(2, tile_rows, span_count * cols_dev)
    bundle = jnp.stack([tiles[0], tiles[1], bed_height])
    beside_all = extended_2(bundle, ((("plane", "span", "wall"), 1),), 1)
    divergence = tile_divergence(beside_all[:2])
    first = bed_height - bed_step * divergence + bed_step * slope_rate * tile_smooth(beside_all[2])
    first_wide = extended_2(first, ((("plane", "span", "wall"), 0),), 1)
    final = first - bed_step * divergence + bed_step * slope_rate * tile_smooth(first_wide)
    spread = jnp.broadcast_to(
        final.reshape(tile_rows, span_count, 1, cols_dev),
        (tile_rows, span_count, wall_count, cols_dev),
    )
    spread = spread.reshape(tile_rows, tile_count, cols_dev)
    returned = lax.all_to_all(spread, ("span", "wall"), split_axis=1, concat_axis=0, tiled=True)
    bed_next = returned.reshape(rows_dev, cols_dev)
    return (velocity_next, bed_next)


def solution(mesh):
    return jax.shard_map(
        body,
        mesh=mesh,
        in_specs=(
            P("groups", "wall", "plane", "span"),
            P(("groups", "plane"), "span"),
            P(("groups", "plane"), "span"),
            P(("groups", "plane", "span", "wall"), None),
        ),
        out_specs=(P("groups", "wall", "plane", "span"), P(("groups", "plane"), "span")),
        check_vma=False,
    )
```

profile of v0, /device:TPU:0, one launch (start us, length us, event | category | flops | bytes accessed | tf_op | source)
XLA Modules:
  0.0 91.9 jit_solution(13445004704585926178)
XLA Ops:
  0.7 1.0 %select_select_fusion = f32[1,16,32,256]{3,2,1,0:T(8,128)S(1)} fusion(f32[32,256]{1,0:T(8,128)} %param.6, s32[32,256]{1,0:T(8,128)} %param.5, s32[16]{0:T(128)S(1)} %iota_add_fusion), kind=kLoop, calls=%fused_computation.108 | loop fusion | flops 524288 | bytes 589888 | tf_op jit(solution)/shard_map/jit(_where)/select_n | solution.py:27
  1.7 1.1 %pad_maximum_fusion.4 = (f32[4,2,32,256]{3,2,1,0:T(8,128)S(1)}, f32[4,2,32,256]{3,2,1,0:T(8,128)S(1)}) fusion(f32[1,16,32,256]{3,2,1,0:T(8,128)S(1)} %select_select_fusion, f32[3,16,32,256]{3,2,1,0:T(8,128)} %param.4), kind=kLoop, calls=%fused_computation.110 | loop fusion | flops 131072 | bytes 2621440 | tf_op jit(solution)/shard_map/slice | solution.py:18
  2.8 2.4 %collective-permute-start = (f32[4,2,32,256]{3,2,1,0:T(8,128)S(1)}, f32[4,2,32,256]{3,2,1,0:T(8,128)S(1)}, u32[]{:S(2)}, u32[]{:S(2)}) collective-permute-start(f32[4,2,32,256]{3,2,1,0:T(8,128)S(1)} %get-tuple-element.26), channel_id=1, source_target_pairs={{0,1},{2,3},{4,5},{6,7},{8,9},{10,11},{12,13},{14,15},{16,17},{18,... | collective-permute-start | bytes 786440 | tf_op jit(solution)/shard_map/ppermute | solution.py:20
  5.1 1.3 %collective-permute-start.1 = (f32[4,2,32,256]{3,2,1,0:T(8,128)S(1)}, f32[4,2,32,256]{3,2,1,0:T(8,128)S(1)}, u32[]{:S(2)}, u32[]{:S(2)}) collective-permute-start(f32[4,2,32,256]{3,2,1,0:T(8,128)S(1)} %get-tuple-element.27), channel_id=1, source_target_pairs={{1,0},{3,2},{5,4},{7,6},{9,8},{11,10},{13,12},{15,14},{17,16},{19,... | collective-permute-start | bytes 786440 | tf_op jit(solution)/shard_map/ppermute | solution.py:21
  6.5 2.1 %collective-permute-done.1 = f32[4,2,32,256]{3,2,1,0:T(8,128)S(1)} collective-permute-done((f32[4,2,32,256]{3,2,1,0:T(8,128)S(1)}, f32[4,2,32,256]{3,2,1,0:T(8,128)S(1)}, u32[]{:S(2)}, u32[]{:S(2)}) %collective-permute-start.1) | collective-permute-done | bytes 262176 | tf_op jit(solution)/shard_map/ppermute | solution.py:21
  8.7 4.3 %collective-permute-start.2 = (f32[4,20,2,256]{3,2,1,0:T(2,128)S(1)}, f32[4,20,2,256]{3,2,1,0:T(2,128)S(1)}, u32[]{:S(2)}, u32[]{:S(2)}) collective-permute-start(f32[4,20,2,256]{3,2,1,0:T(2,128)S(1)} %get-tuple-element.24), channel_id=1, source_target_pairs={{0,4},{4,8},{8,12},{1,5},{5,9},{9,13},{2,6},{6,10},{10,14},{3,7},{... | collective-permute-start | bytes 491528 | tf_op jit(solution)/shard_map/ppermute | solution.py:20
  13.0 1.3 %collective-permute-start.3 = (f32[4,20,2,256]{3,2,1,0:T(2,128)S(1)}, f32[4,20,2,256]{3,2,1,0:T(2,128)S(1)}, u32[]{:S(2)}, u32[]{:S(2)}) collective-permute-start(f32[4,20,2,256]{3,2,1,0:T(2,128)S(1)} %get-tuple-element.25), channel_id=1, source_target_pairs={{4,0},{8,4},{12,8},{5,1},{9,5},{13,9},{6,2},{10,6},{14,10},{7,3},{... | collective-permute-start | bytes 491528 | tf_op jit(solution)/shard_map/ppermute | solution.py:21
  14.3 2.4 %collective-permute-done.2 = f32[4,20,2,256]{3,2,1,0:T(2,128)S(1)} collective-permute-done((f32[4,20,2,256]{3,2,1,0:T(2,128)S(1)}, f32[4,20,2,256]{3,2,1,0:T(2,128)S(1)}, u32[]{:S(2)}, u32[]{:S(2)}) %collective-permute-start.2) | collective-permute-done | bytes 163872 | tf_op jit(solution)/shard_map/ppermute | solution.py:20
  16.8 4.1 %collective-permute-done.3 = f32[4,20,2,256]{3,2,1,0:T(2,128)S(1)} collective-permute-done((f32[4,20,2,256]{3,2,1,0:T(2,128)S(1)}, f32[4,20,2,256]{3,2,1,0:T(2,128)S(1)}, u32[]{:S(2)}, u32[]{:S(2)}) %collective-permute-start.3) | collective-permute-done | bytes 163872 | tf_op jit(solution)/shard_map/ppermute | solution.py:21
  21.4 2.2 %fusion.77 = (f32[4,20,36,2]{3,2,1,0:T(8,128)}, f32[4,20,36,2]{3,2,1,0:T(8,128)}) fusion(f32[4,20,36,256]{3,2,1,0:T(8,128)S(1)} %pad_maximum_fusion.1), kind=kLoop, calls=%fused_computation.164 | loop fusion | bytes 92160 | tf_op jit(solution)/shard_map/slice | solution.py:18
  23.6 2.1 %copy.22 = f32[4,20,36,2]{2,0,3,1:T(4,128)S(1)} copy(f32[4,20,36,2]{3,2,1,0:T(8,128)} %get-tuple-element.22) | data formatting | bytes 46080 | tf_op jit(solution)/shard_map/slice | solution.py:18
  25.7 3.4 %collective-permute-start.4 = (f32[4,20,36,2]{2,0,3,1:T(4,128)S(1)}, f32[4,20,36,2]{2,0,3,1:T(4,128)S(1)}, u32[]{:S(2)}, u32[]{:S(2)}) collective-permute-start(f32[4,20,36,2]{2,0,3,1:T(4,128)S(1)} %copy.22), channel_id=1, source_target_pairs={{0,2},{1,3},{4,6},{5,7},{8,10},{9,11},{12,14},{13,15},{16,18},{17,... | collective-permute-start | bytes 69128 | tf_op jit(solution)/shard_map/ppermute | solution.py:20
  29.1 2.1 %copy.23 = f32[4,20,36,2]{2,0,3,1:T(4,128)S(1)} copy(f32[4,20,36,2]{3,2,1,0:T(8,128)} %get-tuple-element.23) | data formatting | bytes 46080 | tf_op jit(solution)/shard_map/slice | solution.py:19
  31.1 1.3 %collective-permute-start.5 = (f32[4,20,36,2]{2,0,3,1:T(4,128)S(1)}, f32[4,20,36,2]{2,0,3,1:T(4,128)S(1)}, u32[]{:S(2)}, u32[]{:S(2)}) collective-permute-start(f32[4,20,36,2]{2,0,3,1:T(4,128)S(1)} %copy.23), channel_id=1, source_target_pairs={{2,0},{3,1},{6,4},{7,5},{10,8},{11,9},{14,12},{15,13},{18,16},{19,... | collective-permute-start | bytes 69128 | tf_op jit(solution)/shard_map/ppermute | solution.py:21
  32.4 1.8 %copy.24 = f32[4,20,36,2]{3,2,1,0:T(8,128)} copy(f32[4,20,36,2]{2,0,3,1:T(4,128)S(1)} %collective-permute-done.4) | data formatting | bytes 46080 | tf_op jit(solution)/shard_map/ppermute | solution.py:20
  34.3 3.2 %collective-permute-done.5 = f32[4,20,36,2]{2,0,3,1:T(4,128)S(1)} collective-permute-done((f32[4,20,36,2]{2,0,3,1:T(4,128)S(1)}, f32[4,20,36,2]{2,0,3,1:T(4,128)S(1)}, u32[]{:S(2)}, u32[]{:S(2)}) %collective-permute-start.5) | collective-permute-done | bytes 23072 | tf_op jit(solution)/shard_map/ppermute | solution.py:21
  37.5 1.9 %copy.25 = f32[4,20,36,2]{3,2,1,0:T(8,128)} copy(f32[4,20,36,2]{2,0,3,1:T(4,128)S(1)} %collective-permute-done.5) | data formatting | bytes 46080 | tf_op jit(solution)/shard_map/ppermute | solution.py:21
  39.4 7.4 %pad_maximum_fusion = f32[4,20,36,260]{3,2,1,0:T(8,128)S(1)} fusion(f32[4,20,36,2]{3,2,1,0:T(8,128)} %copy.25, f32[4,20,2,256]{3,2,1,0:T(2,128)S(1)} %collective-permute-done.3, f32[4,2,32,256]{3,2,1,0:T(8,128)S(1)} %collective-permute-done.1, f32[1,16,32,256]{3,2,1,0:T(8,128)S(1)} %select_select_fusion, f32[3,16,32,256]{3,2,1,0:T(8,128)S(1)} %copy-done, ...), kind=kLoop, calls=%fused_computation | loop fusion | flops 5241600 | bytes 5990400 | tf_op jit(solution)/shard_map/concatenate | solution.py:22
  47.1 2.6 %fusion.1 = (f32[20,36,260]{2,1,0:T(8,128)S(1)}, f32[20,36,260]{2,1,0:T(8,128)S(1)}, f32[20,36,260]{2,1,0:T(8,128)}, f32[20,36,260]{2,1,0:T(8,128)S(1)}, f32[20,...) fusion(f32[4,20,36,260]{3,2,1,0:T(8,128)S(1)} %pad_maximum_fusi, ...), kind=kLoop, calls=%fused_computation.12 | loop fusion | flops 1684800 | bytes 11232000 | tf_op jit(solution)/shard_map/mul | solution.py:85
  50.5 8.2 %fusion.10 = (f32[32,256]{1,0:T(8,128)S(1)}, f32[32,256]{1,0:T(8,128)S(1)}, f32[16,32,256]{2,1,0:T(8,128)S(1)}, f32[16,32,256]{2,1,0:T(8,128)}) fusion(s32[32,256]{1,0:T(8,128)S(1)} %copy-done.7, s32[16]{0:T(128)S(1)} %iota_add_fusion, f32[20,36,260]{2,1,0:T(8,128)S(1)} %get-tuple-element.21, f32[20,36,260]{2,1,0:T(8,128)S(1)} %get-tuple-element.16, ...), kind=kLoop, calls=%fused_computation.24 | loop fusion | flops 8372224 | bytes 22151232 | tf_op jit(solution)/shard_map/reduce_sum | solution.py:101
  58.8 6.5 %all_to_all.30 = f32[2,4,8,256]{3,2,0,1:T(8,128)S(1)} all-to-all(f32[2,4,8,256]{3,2,0,1:T(8,128)S(1)} %pad_maximum_fusion.9), channel_id=1, replica_groups=mesh['groups'=2,'plane'=4,'span'=2,'wall'=2] {'span','wall'}, dimensions={1} | all-to-all | bytes 131072 | tf_op jit(solution)/shard_map/all_to_all | solution.py:106
  65.3 1.5 %collective-permute-start.6 = (f32[3,1,512]{2,1,0:T(1,128)S(1)}, f32[3,1,512]{2,1,0:T(1,128)S(1)}, u32[]{:S(2)}, u32[]{:S(2)}) collective-permute-start(f32[3,1,512]{2,1,0:T(1,128)S(1)} %get-tuple-element.29), channel_id=1, source_target_pairs={{0,1},{1,2},{2,3},{3,4},{4,5},{5,6},{6,7},{7,8},{8,9},{9,10},{10,1... | collective-permute-start | bytes 18440 | tf_op jit(solution)/shard_map/ppermute | solution.py:20
  66.9 1.3 %collective-permute-start.7 = (f32[3,1,512]{2,1,0:T(1,128)S(1)}, f32[3,1,512]{2,1,0:T(1,128)S(1)}, u32[]{:S(2)}, u32[]{:S(2)}) collective-permute-start(f32[3,1,512]{2,1,0:T(1,128)S(1)} %get-tuple-element.28), channel_id=1, source_target_pairs={{1,0},{2,1},{3,2},{4,3},{5,4},{6,5},{7,6},{8,7},{9,8},{10,9},{11,1... | collective-permute-start | bytes 18440 | tf_op jit(solution)/shard_map/ppermute | solution.py:21
  68.2 1.9 %collective-permute-done.7 = f32[3,1,512]{2,1,0:T(1,128)S(1)} collective-permute-done((f32[3,1,512]{2,1,0:T(1,128)S(1)}, f32[3,1,512]{2,1,0:T(1,128)S(1)}, u32[]{:S(2)}, u32[]{:S(2)}) %collective-permute-start.7) | collective-permute-done | bytes 6176 | tf_op jit(solution)/shard_map/ppermute | solution.py:21
  70.3 1.3 %collective-permute-start.8 = (f32[1,512]{1,0:T(1,128)S(1)}, f32[1,512]{1,0:T(1,128)S(1)}, u32[]{:S(2)}, u32[]{:S(2)}) collective-permute-start(f32[1,512]{1,0:T(1,128)S(1)} %get-tuple-element.34), channel_id=1, source_target_pairs={{1,0},{2,1},{3,2},{4,3},{5,4},{6,5},{7,6},{8,7},{9,8},{10,9},{11,1... | collective-permute-start | bytes 6152 | tf_op jit(solution)/shard_map/ppermute | solution.py:21
  71.6 5.1 %collective-permute-start.9 = (f32[1,512]{1,0:T(1,128)S(1)}, f32[1,512]{1,0:T(1,128)S(1)}, u32[]{:S(2)}, u32[]{:S(2)}) collective-permute-start(f32[1,512]{1,0:T(1,128)S(1)} %get-tuple-element.35), channel_id=1, source_target_pairs={{0,1},{1,2},{2,3},{3,4},{4,5},{5,6},{6,7},{7,8},{8,9},{9,10},{10,1... | collective-permute-start | bytes 6152 | tf_op jit(solution)/shard_map/ppermute | solution.py:20
  76.7 2.6 %fusion.16 = f32[1,16,32,256]{3,2,1,0:T(8,128)S(1)} fusion(f32[20,36,260]{2,1,0:T(8,128)S(1)} %get-tuple-element.20, f32[20,36,260]{2,1,0:T(8,128)S(1)} %copy-done.1, f32[20,36,260]{2,1,0:T(8,128)S(1)} %copy-done.2, f32[20,36,260]{2,1,0:T(8,128)S(1)} %copy-done.3, f32[3,16,32,256]{3,2,1,0:T(8,128)S(1)} %copy-done, f32[32,256]{1,0:T(8,128)S(1)} %copy-done.5, ...), kind=kLoop, calls=%fused_computation.31 | loop fusion | flops 4194304 | bytes 11075648 | tf_op jit(solution)/shard_map/stack | solution.py:96
  79.4 0.6 broadcast_in_dim.45
  80.0 7.3 %all-to-all-start.1 = ((f32[8,4,256]{2,0,1:T(8,128)}), f32[8,4,256]{2,0,1:T(8,128)S(1)}, u32[]{:S(2)}, u32[]{:S(2)}) async-start(f32[8,4,256]{2,0,1:T(8,128)} %bitcast.25), calls=%async_computation.1 | async-start | bytes 65536 | tf_op jit(solution)/shard_map/all_to_all | solution.py:120
  87.3 1.3 %pad_maximum_fusion.2 = f32[3,16,32,256]{3,2,1,0:T(8,128)} fusion(f32[1,16,32,256]{3,2,1,0:T(8,128)S(1)} %fusion.16, f32[1,16,32,256]{3,2,1,0:T(8,128)S(1)} %bitcast.99, f32[1,16,32,256]{3,2,1,0:T(8,128)S(1)} %bitcast.98), kind=kLoop, calls=%fused_computation.3 | loop fusion | flops 786432 | bytes 3145728 | tf_op jit(solution)/shard_map/stack | solution.py:96
  88.6 2.7 %all-to-all-done.1 = f32[8,4,256]{2,0,1:T(8,128)S(1)} async-done(((f32[8,4,256]{2,0,1:T(8,128)}), f32[8,4,256]{2,0,1:T(8,128)S(1)}, u32[]{:S(2)}, u32[]{:S(2)}) %all-to-all-start.1) | async-done | bytes 32800 | tf_op jit(solution)/shard_map/all_to_all | solution.py:120
  91.3 0.6 copy.27
  (37 shorter events, 2.1 us)
Async XLA Ops:
  0.6 7.9 %copy-start = (f32[3,16,32,256]{3,2,1,0:T(8,128)S(1)}, f32[3,16,32,256]{3,2,1,0:T(8,128)}, u32[]{:S(2)}) copy-start(f32[3,16,32,256]{3,2,1,0:T(8,128)} %param.4) | copy-start | bytes 4718596
  2.8 3.7 %collective-permute-start = (f32[4,2,32,256]{3,2,1,0:T(8,128)S(1)}, f32[4,2,32,256]{3,2,1,0:T(8,128)S(1)}, u32[]{:S(2)}, u32[]{:S(2)}) collective-permute-start(f32[4,2,32,256]{3,2,1,0:T(8,128)S(1)} %get-tuple-element.26), channel_id=1, source_target_pairs={{0,1},{2,3},{4,5},{6,7},{8,9},{10,11},{12,13},{14,15},{16,17},{18,... | collective-permute-start | bytes 786440 | tf_op jit(solution)/shard_map/ppermute | solution.py:20
  5.1 3.4 %collective-permute-start.1 = (f32[4,2,32,256]{3,2,1,0:T(8,128)S(1)}, f32[4,2,32,256]{3,2,1,0:T(8,128)S(1)}, u32[]{:S(2)}, u32[]{:S(2)}) collective-permute-start(f32[4,2,32,256]{3,2,1,0:T(8,128)S(1)} %get-tuple-element.27), channel_id=1, source_target_pairs={{1,0},{3,2},{5,4},{7,6},{9,8},{11,10},{13,12},{15,14},{17,16},{19,... | collective-permute-start | bytes 786440 | tf_op jit(solution)/shard_map/ppermute | solution.py:21
  8.7 8.1 %collective-permute-start.2 = (f32[4,20,2,256]{3,2,1,0:T(2,128)S(1)}, f32[4,20,2,256]{3,2,1,0:T(2,128)S(1)}, u32[]{:S(2)}, u32[]{:S(2)}) collective-permute-start(f32[4,20,2,256]{3,2,1,0:T(2,128)S(1)} %get-tuple-element.24), channel_id=1, source_target_pairs={{0,4},{4,8},{8,12},{1,5},{5,9},{9,13},{2,6},{6,10},{10,14},{3,7},{... | collective-permute-start | bytes 491528 | tf_op jit(solution)/shard_map/ppermute | solution.py:20
  13.0 7.9 %collective-permute-start.3 = (f32[4,20,2,256]{3,2,1,0:T(2,128)S(1)}, f32[4,20,2,256]{3,2,1,0:T(2,128)S(1)}, u32[]{:S(2)}, u32[]{:S(2)}) collective-permute-start(f32[4,20,2,256]{3,2,1,0:T(2,128)S(1)} %get-tuple-element.25), channel_id=1, source_target_pairs={{4,0},{8,4},{12,8},{5,1},{9,5},{13,9},{6,2},{10,6},{14,10},{7,3},{... | collective-permute-start | bytes 491528 | tf_op jit(solution)/shard_map/ppermute | solution.py:21
  25.7 6.8 %collective-permute-start.4 = (f32[4,20,36,2]{2,0,3,1:T(4,128)S(1)}, f32[4,20,36,2]{2,0,3,1:T(4,128)S(1)}, u32[]{:S(2)}, u32[]{:S(2)}) collective-permute-start(f32[4,20,36,2]{2,0,3,1:T(4,128)S(1)} %copy.22), channel_id=1, source_target_pairs={{0,2},{1,3},{4,6},{5,7},{8,10},{9,11},{12,14},{13,15},{16,18},{17,... | collective-permute-start | bytes 69128 | tf_op jit(solution)/shard_map/ppermute | solution.py:20
  31.1 6.3 %collective-permute-start.5 = (f32[4,20,36,2]{2,0,3,1:T(4,128)S(1)}, f32[4,20,36,2]{2,0,3,1:T(4,128)S(1)}, u32[]{:S(2)}, u32[]{:S(2)}) collective-permute-start(f32[4,20,36,2]{2,0,3,1:T(4,128)S(1)} %copy.23), channel_id=1, source_target_pairs={{2,0},{3,1},{6,4},{7,5},{10,8},{11,9},{14,12},{15,13},{18,16},{19,... | collective-permute-start | bytes 69128 | tf_op jit(solution)/shard_map/ppermute | solution.py:21
  49.7 0.8 copy-start.5
  49.7 0.8 copy-start.7
  50.5 14.8 %copy-start.6 = (f32[8,512]{1,0:T(8,128)S(1)}, f32[8,512]{1,0:T(8,128)}, u32[]{:S(2)}) copy-start(f32[8,512]{1,0:T(8,128)} %param.7) | copy-start | bytes 49156
  50.5 26.1 %copy-start.1 = (f32[20,36,260]{2,1,0:T(8,128)S(1)}, f32[20,36,260]{2,1,0:T(8,128)}, u32[]{:S(2)}) copy-start(f32[20,36,260]{2,1,0:T(8,128)} %get-tuple-element.12) | copy-start | bytes 2246404
  50.5 26.2 %copy-start.2 = (f32[20,36,260]{2,1,0:T(8,128)S(1)}, f32[20,36,260]{2,1,0:T(8,128)}, u32[]{:S(2)}) copy-start(f32[20,36,260]{2,1,0:T(8,128)} %get-tuple-element.14) | copy-start | bytes 2246404
  50.5 26.2 %copy-start.3 = (f32[20,36,260]{2,1,0:T(8,128)S(1)}, f32[20,36,260]{2,1,0:T(8,128)}, u32[]{:S(2)}) copy-start(f32[20,36,260]{2,1,0:T(8,128)} %get-tuple-element.15) | copy-start | bytes 2246404
  65.3 2.9 %collective-permute-start.6 = (f32[3,1,512]{2,1,0:T(1,128)S(1)}, f32[3,1,512]{2,1,0:T(1,128)S(1)}, u32[]{:S(2)}, u32[]{:S(2)}) collective-permute-start(f32[3,1,512]{2,1,0:T(1,128)S(1)} %get-tuple-element.29), channel_id=1, source_target_pairs={{0,1},{1,2},{2,3},{3,4},{4,5},{5,6},{6,7},{7,8},{8,9},{9,10},{10,1... | collective-permute-start | bytes 18440 | tf_op jit(solution)/shard_map/ppermute | solution.py:20
  66.9 3.2 %collective-permute-start.7 = (f32[3,1,512]{2,1,0:T(1,128)S(1)}, f32[3,1,512]{2,1,0:T(1,128)S(1)}, u32[]{:S(2)}, u32[]{:S(2)}) collective-permute-start(f32[3,1,512]{2,1,0:T(1,128)S(1)} %get-tuple-element.28), channel_id=1, source_target_pairs={{1,0},{2,1},{3,2},{4,3},{5,4},{6,5},{7,6},{8,7},{9,8},{10,9},{11,1... | collective-permute-start | bytes 18440 | tf_op jit(solution)/shard_map/ppermute | solution.py:21
  70.3 9.1 %collective-permute-start.8 = (f32[1,512]{1,0:T(1,128)S(1)}, f32[1,512]{1,0:T(1,128)S(1)}, u32[]{:S(2)}, u32[]{:S(2)}) collective-permute-start(f32[1,512]{1,0:T(1,128)S(1)} %get-tuple-element.34), channel_id=1, source_target_pairs={{1,0},{2,1},{3,2},{4,3},{5,4},{6,5},{7,6},{8,7},{9,8},{10,9},{11,1... | collective-permute-start | bytes 6152 | tf_op jit(solution)/shard_map/ppermute | solution.py:21
  71.6 7.8 %collective-permute-start.9 = (f32[1,512]{1,0:T(1,128)S(1)}, f32[1,512]{1,0:T(1,128)S(1)}, u32[]{:S(2)}, u32[]{:S(2)}) collective-permute-start(f32[1,512]{1,0:T(1,128)S(1)} %get-tuple-element.35), channel_id=1, source_target_pairs={{0,1},{1,2},{2,3},{3,4},{4,5},{5,6},{6,7},{7,8},{8,9},{9,10},{10,1... | collective-permute-start | bytes 6152 | tf_op jit(solution)/shard_map/ppermute | solution.py:20
  76.7 10.6 %copy-start.4 = (f32[16,32,256]{2,1,0:T(8,128)S(1)}, f32[16,32,256]{2,1,0:T(8,128)}, u32[]{:S(2)}) copy-start(f32[16,32,256]{2,1,0:T(8,128)} %get-tuple-element.9) | copy-start | bytes 1572868
  80.0 11.2 %all-to-all-start.1 = ((f32[8,4,256]{2,0,1:T(8,128)}), f32[8,4,256]{2,0,1:T(8,128)S(1)}, u32[]{:S(2)}, u32[]{:S(2)}) async-start(f32[8,4,256]{2,0,1:T(8,128)} %bitcast.25), calls=%async_computation.1 | async-start | bytes 65536 | tf_op jit(solution)/shard_map/all_to_all | solution.py:120
where the time goes:
time: 92.5 us; the launch traced here: 91.9 us
  starting transfers between devices  30.5 us (33%)
  other arithmetic  25.4 us (27%)
  waiting for transfers between devices  16.4 us (18%)
  local copies, waits for them, and re-layouts  12.2 us (13%)
  blocking collectives  6.49 us (7%)
    ppermute x5, starting transfers between devices, extended_2(): before = lax.ppermute(last, axis, up)  16.7 us
    ppermute x5, waiting for transfers between devices, extended_2(): after = lax.ppermute(initial, axis, down)  11.3 us
    reduce_sum x1, other arithmetic, body(): jnp.sum(cutting * velocity_next[0], axis=0) * scale  8.22 us
    concatenate x2, other arithmetic, extended_2(): x = jnp.concatenate([before, x, after], axis=dim)  7.89 us
    all_to_all x1, starting transfers between devices, body(): lax.all_to_all(spread, ('span', 'wall'), split_axis=1, concat_axis=0, til...  7.28 us
    all_to_all x1, blocking collectives, body(): lax.all_to_all(outgoing, ('span', 'wall'), split_axis=1, concat_axis=3, t...  6.49 us
    ppermute x5, starting transfers between devices, extended_2(): after = lax.ppermute(initial, axis, down)  6.46 us
    slice x2, local copies, waits for them, and re-layouts, extended_2(): last = lax.slice_in_dim(x, length - width, length, axis=dim)  4.28 us
  transfers between devices with their start and end apart: 11, of which 6 were waited for; matrix products, arithmetic and copies ran while one was open for 8% of the time, Pallas kernels for 0%

commit v1 on v0

v1 whole, which is shorter than its diff:
```python
import functools

import jax
import jax.numpy as jnp
from jax import lax
from jax.experimental import pallas as pl
from jax.experimental.pallas import tpu as pltpu
from jax.sharding import PartitionSpec as P

time_step = 0.1
bed_step = 0.4
slope_rate = 0.25
threshold_sq = 0.25
gain = time_step / 12.0
EDGE = 4
SUB = 8
LANE = 128
VMEM = pltpu.VMEM
MIB = 1024 * 1024


def call(kernel, outs, ins, scratch=(), any_inputs=(), flops=0, moved=0, limit=20, aliases=None):
    specs = [pl.BlockSpec(memory_space=pl.ANY if i in any_inputs else VMEM) for i in range(len(ins))]
    shapes = [jax.ShapeDtypeStruct(s, jnp.float32) for s in outs]
    return pl.pallas_call(
        kernel,
        out_shape=shapes,
        in_specs=specs,
        out_specs=[pl.BlockSpec(memory_space=VMEM) for _ in outs],
        scratch_shapes=list(scratch),
        input_output_aliases=aliases or {},
        cost_estimate=pl.CostEstimate(flops=flops, bytes_accessed=moved, transcendentals=0),
        compiler_params=pltpu.CompilerParams(vmem_limit_bytes=limit * MIB),
    )(*ins)


def iota(shape, dim):
    return lax.broadcasted_iota(jnp.int32, shape, dim)


def ahead(x, step, axis):
    return pltpu.roll(x, (-step) % x.shape[axis], axis)


def sweep(flux, b, axis):
    a = 8.0 * flux
    return ahead((b - a) + ahead(flux, 1, axis), 1, axis) + ahead((b + a) - ahead(flux, -1, axis), -1, axis)


def opened_at(level, fraction, layer):
    return jnp.where(level == layer, fraction, jnp.where(layer > level, 1.0, 0.0))


def even(axis):
    return lax.rem(lax.axis_index(axis), 2) == 0


def brick(read, level, fraction, base, layers, q_ref, f_ref, write):
    rows, cols = level.shape
    blank = jnp.zeros((rows, cols), jnp.float32)
    for c in range(3):
        for z in (0, 1, layers + 2, layers + 3):
            q_ref[c, z] = blank
            f_ref[c, z] = blank
    cut_gain = fraction * (gain / 1.0)
    scale = 1.0 / (0.5 + fraction)

    def prepare(z, carry):
        vel = [read(c, z) for c in range(3)]
        opened = opened_at(level, fraction, (base + z).astype(jnp.float32))
        for c in range(3):
            q = opened * vel[c]
            q_ref[c, z + 2] = q
            f_ref[c, z + 2] = vel[2] * q
        return carry

    lax.fori_loop(0, layers, prepare, 0, unroll=2)

    def vertical(c, z):
        near = f_ref[c, z + 3] - f_ref[c, z + 1]
        both = q_ref[c, z + 3] + q_ref[c, z + 1]
        return 6.0 * both - 8.0 * near + (f_ref[c, z + 4] - f_ref[c, z])

    def outside(z):
        hit = level == (base + z).astype(jnp.float32)
        found = []
        for c in range(2):
            total = blank
            if z + 3 <= layers + 3 and z + 1 >= 0:
                low, high = (z + 1, z + 3)
            for offset, weight_f, weight_q in ((1, -8.0, 6.0), (-1, 8.0, 6.0), (2, 1.0, 0.0), (-2, -1.0, 0.0)):
                at = z + offset
                if 0 <= at < layers:
                    total = total + weight_f * f_ref[c, at + 2]
                    if weight_q:
                        total = total + weight_q * q_ref[c, at + 2]
            found.append(jnp.where(hit, cut_gain * total, 0.0))
        return found

    sums = [blank, blank]
    for z in (-2, -1, layers, layers + 1):
        found = outside(z)
        sums = [s + f for s, f in zip(sums, found)]

    def update(z, sums):
        vel = [read(c, z) for c in range(3)]
        q = [q_ref[c, z + 2] for c in range(3)]
        layer = (base + z).astype(jnp.float32)
        opened = opened_at(level, fraction, layer)
        hit = level == layer
        weight = gain * opened
        cross = vel[0] * q[1]
        along_x = (vel[0] * q[0], cross, f_ref[0, z + 2])
        along_y = (cross, vel[1] * q[1], f_ref[1, z + 2])
        sums = list(sums)
        for c in range(3):
            b = 6.0 * q[c]
            total = vertical(c, z) - 6.0 * b
            total = total + sweep(along_x[c], b, 1) + sweep(along_y[c], b, 0)
            fresh = vel[c] + weight * total
            write(c, z, fresh)
            if c < 2:
                sums[c] = sums[c] + jnp.where(hit, fresh, 0.0)
        return tuple(sums)

    sums = lax.fori_loop(0, layers, update, tuple(sums))
    return [s * scale for s in sums]


def pack_kernel(layers, bed_in, vel, lev, frac, bed, a_ref, b_ref, z_ref, top, bottom, sems):
    rows = lev.shape[0]
    wall = lax.axis_index("wall")
    start = jnp.where(wall == 0, layers - 2, 0)
    copies = [
        pltpu.make_async_copy(vel.at[:, :, pl.ds(0, SUB), :], top, sems.at[0]),
        pltpu.make_async_copy(vel.at[:, :, pl.ds(rows - SUB, SUB), :], bottom, sems.at[1]),
        pltpu.make_async_copy(vel.at[:, pl.ds(start, 2)], z_ref, sems.at[2]),
    ]
    for copy in copies:
        copy.start()
    cols = lev.shape[1]
    half = iota((SUB, cols), 0) < EDGE
    is_even = even("plane")

    def put(n, low, high):
        a_ref[n] = jnp.where(is_even, low, high)
        b_ref[n] = jnp.where(is_even, high, low)

    levels = lev[...].astype(jnp.float32)
    count = 3 * layers // 2
    put(
        count,
        jnp.where(half, pltpu.roll(levels[-SUB:], EDGE, 0), frac[-SUB:]),
        jnp.where(half, levels[:SUB], pltpu.roll(frac[:SUB], EDGE, 0)),
    )
    if bed_in:
        for i in range(bed.shape[1] // cols):
            tile = bed[:, i * cols : (i + 1) * cols]
            put(count + 1 + i, tile, tile)
    for copy in copies:
        copy.wait()
    for c in range(3):
        for k in range(layers // 2):
            low = jnp.where(half, pltpu.roll(bottom[c, 2 * k], EDGE, 0), bottom[c, 2 * k + 1])
            high = jnp.where(half, top[c, 2 * k], pltpu.roll(top[c, 2 * k + 1], EDGE, 0))
            put(c * (layers // 2) + k, low, high)


def gather_edges(read, layers, rows, cols, put):
    lane = iota((rows, LANE), 1)
    column = lax.rem(lane, 2 * EDGE)
    for c in range(3):
        right = jnp.zeros((rows, LANE), jnp.float32)
        left = right
        for z in range(layers):
            group = (lane // (2 * EDGE)) == z
            field = read(c, z)
            last = field[:, cols - LANE :]
            first = field[:, :LANE]
            at = 2 * EDGE * z
            right = jnp.where(group, pltpu.roll(last, (at - (LANE - EDGE)) % LANE, 1), right)
            left = jnp.where(group, pltpu.roll(first, (at + EDGE) % LANE, 1), left)
        put(0, c, jnp.where(column < EDGE, right, 0.0))
        put(1, c, jnp.where(column >= EDGE, left, 0.0))


def repeat_edges(field, rows, cols):
    lane = iota((rows, LANE), 1)
    right = jnp.where(lane < EDGE, pltpu.roll(field[:, cols - LANE :], EDGE, 1), 0.0)
    left = pltpu.roll(jnp.where(lane < EDGE, field[:, :LANE], 0.0), EDGE, 1)
    step = 2 * EDGE
    while step < LANE:
        right = right + pltpu.roll(right, step, 1)
        left = left + pltpu.roll(left, step, 1)
        step *= 2
    return right, left


def inner_kernel(layers, vel, lev, frac, new_ref, shear_ref, edge_ref, q_ref, f_ref):
    rows, cols = lev.shape
    base = lax.axis_index("wall") * layers
    levels = lev[...].astype(jnp.float32)
    fraction = frac[...]

    def write(c, z, value):
        new_ref[c, z] = value

    sums = brick(lambda c, z: vel[c, z], levels, fraction, base, layers, q_ref, f_ref, write)
    shear_ref[0] = sums[0]
    shear_ref[1] = sums[1]

    def put(side, n, value):
        edge_ref[side, n] = value.reshape(rows // SUB, SUB, LANE)

    gather_edges(lambda c, z: vel[c, z], layers, rows, cols, put)
    for n, field in ((3, levels), (4, fraction)):
        right, left = repeat_edges(field, rows, cols)
        put(0, n, right)
        put(1, n, left)


def unpack_kernel(layers, count, bed_in, got_a, got_b, edge, bed, halo_ref, flat_ref, full_ref, *messages):
    cols = halo_ref.shape[3]
    tiles = edge.shape[2]
    half = iota((SUB, cols), 0) < EDGE
    is_even = even("plane")

    def sides(n):
        one, two = got_a[n], got_b[n]
        return jnp.where(is_even, one, two), jnp.where(is_even, two, one)

    for c in range(3):
        for k in range(layers // 2):
            low, high = sides(c * (layers // 2) + k)
            halo_ref[c, 2 * k] = jnp.where(half, low, pltpu.roll(high, EDGE, 0))
            halo_ref[c, 2 * k + 1] = jnp.where(half, pltpu.roll(low, EDGE, 0), high)
    low, high = sides(3 * layers // 2)
    levels = jnp.where(half, low, pltpu.roll(high, EDGE, 0))
    fraction = jnp.where(half, pltpu.roll(low, EDGE, 0), high)
    flat_ref[0] = levels
    flat_ref[1] = fraction

    def put(side, n, value):
        full_ref[side, n * (tiles + 1) + tiles] = value

    gather_edges(lambda c, z: halo_ref[c, z], layers, SUB, cols, put)
    for n, field in ((3, levels), (4, fraction)):
        right, left = repeat_edges(field, SUB, cols)
        put(0, n, right)
        put(1, n, left)
    for side in range(2):
        for n in range(5):
            for t in range(tiles):
                full_ref[side, n * (tiles + 1) + t] = edge[side, n, t]
    used = 5 * (tiles + 1)
    right_first = even("span")
    for i, message in enumerate(messages):
        is_right = right_first if i == 0 else jnp.logical_not(right_first)
        for n in range(used):
            message[n] = jnp.where(is_right, full_ref[0, n], full_ref[1, n])
    if bed_in:
        parts = bed.shape[1] // LANE
        for i in range(parts):
            messages[0][used + i] = bed[:, i * LANE : (i + 1) * LANE]
        per = cols // LANE
        for i in range(bed.shape[1] // cols):
            low, high = sides(3 * layers // 2 + 1 + i)
            tile = jnp.where(half, low, high)
            for j in range(per):
                messages[0][used + parts + i * per + j] = tile[:, j * LANE : (j + 1) * LANE]


def strip_kernel(layers, vel, lev, frac, halo, flat, top_ref, bottom_ref, shear_ref, top, bottom, q_ref, f_ref, sems):
    rows, cols = lev.shape
    copies = [
        pltpu.make_async_copy(vel.at[:, :, pl.ds(0, SUB), :], top, sems.at[0]),
        pltpu.make_async_copy(vel.at[:, :, pl.ds(rows - SUB, SUB), :], bottom, sems.at[1]),
    ]
    for copy in copies:
        copy.start()
    base = lax.axis_index("wall") * layers
    half = iota((SUB, cols), 0) < EDGE
    for copy in copies:
        copy.wait()
    for side, own, new in ((0, top, top_ref), (1, bottom, bottom_ref)):
        inside = half if side == 0 else jnp.logical_not(half)
        first = 0 if side == 0 else rows - SUB
        levels = jnp.where(inside, lev[first : first + SUB].astype(jnp.float32), flat[0])
        fraction = jnp.where(inside, frac[first : first + SUB], flat[1])

        def read(c, z):
            return jnp.where(inside, own[c, z], halo[c, z])

        def write(c, z, value):
            new[c, z] = value

        sums = brick(read, levels, fraction, base, layers, q_ref, f_ref, write)
        shear_ref[side, 0] = sums[0]
        shear_ref[side, 1] = sums[1]


def column_strip(vel, levels, fraction, base, layers):
    shape = levels.shape
    width = 2 * EDGE
    here = iota(shape, 1) // width
    layer = (here + base).astype(jnp.float32)
    opened = opened_at(levels, fraction, layer)
    hit = levels == layer
    hit_down = levels == layer - layers
    hit_up = levels == layer + layers
    scale = 1.0 / (0.5 + fraction)
    fresh, shear = [], []
    for c in range(3):
        q = opened * vel[c]
        b = 6.0 * q
        total = sweep(vel[0] * q, b, 1) + sweep(vel[1] * q, b, 0) - 6.0 * b
        flux = vel[2] * q
        plus = ahead(b - 8.0 * flux, width, 1)
        minus = ahead(b + 8.0 * flux, -width, 1)
        plus_far = ahead(flux, 2 * width, 1)
        minus_far = ahead(flux, -2 * width, 1)
        total = total + jnp.where(here <= layers - 2, plus, 0.0) + jnp.where(here <= layers - 3, plus_far, 0.0)
        total = total + jnp.where(here >= 1, minus, 0.0) - jnp.where(here >= 2, minus_far, 0.0)
        value = vel[c] + gain * opened * total
        fresh.append(value)
        if c < 2:
            down = jnp.where(here > layers - 2, plus, 0.0) + jnp.where(here > layers - 3, plus_far, 0.0)
            up = jnp.where(here < 1, minus, 0.0) - jnp.where(here < 2, minus_far, 0.0)
            part = jnp.where(hit, value, 0.0)
            part = part + gain * fraction * (jnp.where(hit_down, down, 0.0) + jnp.where(hit_up, up, 0.0))
            step = LANE // 2
            while step >= width:
                part = part + pltpu.roll(part, step, 1)
                step //= 2
            shear.append(part * scale)
    return fresh, shear


def side_kernel(layers, spans, bed_in, full, shear, strips, *rest):
    got = rest[:spans]
    rest = rest[spans:]
    own_message = rest[0]
    fresh_ref, out_ref = rest[1:]
    _, rows, cols = shear.shape
    tiles = rows // SUB
    tall = tiles + 1
    base = lax.axis_index("wall") * layers
    right_first = even("span")
    results = []
    for side in range(2):
        fields = []
        for n in range(5):
            at = slice(n * tall, (n + 1) * tall)
            own = full[side, at]
            first = right_first if side == 0 else jnp.logical_not(right_first)
            other = jnp.where(first, got[0][at], got[1][at] if spans > 1 else 0.0)
            fields.append((own + other).reshape(tall * SUB, LANE))
        fresh, edge_shear = column_strip(fields[:3], fields[3], fields[4], base, layers)
        for c in range(3):
            fresh_ref[side, c] = fresh[c]
        results.append(edge_shear)
    lane = iota((SUB, LANE), 1)
    sub = iota((SUB, LANE), 0)
    lanes = cols // LANE
    for c in range(2):
        right, left = results[0][c], results[1][c]
        for t in range(tall):
            at = slice(t * SUB, (t + 1) * SUB)
            for k in range(lanes):
                cut = slice(k * LANE, (k + 1) * LANE)
                if t == tiles:
                    piece = jnp.where(sub < EDGE, strips[1, c, :, cut], strips[0, c, :, cut])
                    piece = jnp.where((sub < 2) | (sub >= SUB - 2), piece, 0.0)
                else:
                    piece = shear[c, at, cut]
                    if t == 0:
                        piece = jnp.where(sub < 2, strips[0, c, :, cut], piece)
                    if t == tiles - 1:
                        piece = jnp.where(sub >= SUB - 2, strips[1, c, :, cut], piece)
                if k == 0:
                    piece = jnp.where(lane < 2, pltpu.roll(left[at], LANE - EDGE, 1), piece)
                if k == lanes - 1:
                    piece = jnp.where(lane >= LANE - 2, pltpu.roll(right[at], LANE - EDGE, 1), piece)
                out_ref[(c * tall + t) * (lanes + 1) + k] = piece
            beyond = jnp.where(lane < 2, pltpu.roll(right[at], LANE - EDGE, 1), 0.0)
            beyond = jnp.where(lane >= LANE - 2, pltpu.roll(left[at], LANE - EDGE, 1), beyond)
            out_ref[(c * tall + t) * (lanes + 1) + lanes] = beyond
    if bed_in:
        used = 2 * tall * (lanes + 1)
        start = 5 * tall
        count = own_message.shape[0] - start
        for i in range(count):
            out_ref[used + i] = own_message[start + i]
            out_ref[used + count + i] = got[0][start + i]


def merge_kernel(layers, new, strip_top, strip_bottom, fresh, far, lev, frac, out_ref):
    rows, cols = lev.shape
    tiles = rows // SUB
    lanes = cols // LANE
    wall = lax.axis_index("wall")
    lower = wall == 0
    sub = iota((SUB, cols), 0)
    lane = iota((rows, LANE), 1)
    levels = lev[...].astype(jnp.float32)
    fraction = frac[...]
    for c in range(3):
        right, left = fresh[0, c, :rows], fresh[1, c, :rows]

        def layer_step(z, carry):
            shift = 2 * EDGE * z
            block = new[c, z]
            first = jnp.where(sub < 2, strip_top[c, z], block[:SUB])
            last = jnp.where(sub >= SUB - 2, strip_bottom[c, z], block[rows - SUB :])
            block = jnp.concatenate([first, block[SUB : rows - SUB], last], axis=0)
            pieces = [block[:, k * LANE : (k + 1) * LANE] for k in range(lanes)]
            at_left = pltpu.roll(left, lax.rem(2 * LANE - EDGE - shift, LANE), 1)
            at_right = pltpu.roll(right, lax.rem(2 * LANE - EDGE - shift, LANE), 1)
            pieces[0] = jnp.where(lane < 2, at_left, pieces[0])
            pieces[-1] = jnp.where(lane >= LANE - 2, at_right, pieces[-1])
            for k in range(lanes):
                out_ref[c, z, :, k * LANE : (k + 1) * LANE] = pieces[k]
            return carry

        lax.fori_loop(0, layers, layer_step, 0, unroll=4)
    base = wall * layers
    near_from = jnp.where(lower, 0, 1)
    far_from = 1 - near_from
    near_to = jnp.where(lower, layers - 1, 0)
    far_to = jnp.where(lower, layers - 2, 1)
    sign = jnp.where(lower, -1.0, 1.0)
    other = jnp.where(lower, layers, 0)
    near_open = opened_at(levels, fraction, (other + jnp.where(lower, 0, layers - 1)).astype(jnp.float32))
    far_open = opened_at(levels, fraction, (other + jnp.where(lower, 1, layers - 2)).astype(jnp.float32))
    near_gain = gain * opened_at(levels, fraction, (base + near_to).astype(jnp.float32))
    far_gain = gain * opened_at(levels, fraction, (base + far_to).astype(jnp.float32))
    near_w, far_w = far[2, near_from], far[2, far_from]
    for c in range(3):
        near_q = near_open * far[c, near_from]
        near_f = sign * (near_w * near_q)
        far_f = sign * (far_w * (far_open * far[c, far_from]))
        out_ref[c, near_to] = out_ref[c, near_to] + near_gain * (6.0 * near_q + 8.0 * near_f - far_f)
        out_ref[c, far_to] = out_ref[c, far_to] - far_gain * near_f


def bed_kernel(tall, lanes, bed_in, mine, theirs, *rest):
    out_ref = rest[-1]
    rows = (tall - 1) * SUB
    wide = (lanes + 1) * LANE
    span = lax.axis_index("span")
    wall = lax.axis_index("wall")
    plane = lax.axis_index("plane")

    def sheared(c):
        whole = []
        for t in range(tall):
            first = (c * tall + t) * (lanes + 1)
            whole.append(
                jnp.concatenate([mine[first + k] + theirs[first + k] for k in range(lanes + 1)], axis=1)
            )
        return jnp.concatenate(whole, axis=0)

    shear_x, shear_y = sheared(0), sheared(1)
    if bed_in:
        used = 2 * tall * (lanes + 1)
        parts = 2 * lanes

        def tile_of(s, w, which):
            pieces = []
            for k in range(parts):
                own = used + which * parts + k
                across = own + 2 * parts
                from_mine = jnp.where(span == s, mine[own], mine[across])
                from_theirs = jnp.where(span == s, theirs[own], theirs[across])
                pieces.append(jnp.where(wall == w, from_mine, from_theirs))
            return pieces

        def window(pieces):
            lane = iota((SUB, LANE), 1)
            low = span == 0
            inside = [jnp.where(low, pieces[k], pieces[lanes + k]) for k in range(lanes)]
            beyond = jnp.where(
                low,
                jnp.where(lane < LANE // 2, pieces[lanes], 0.0),
                jnp.where(lane < LANE // 2, 0.0, pieces[lanes - 1]),
            )
            return jnp.concatenate(inside + [beyond], axis=1)

        sub = iota((SUB, LANE), 0)
        whole = [window(tile_of(s, w, 0)) for s in range(2) for w in range(2)]
        after = tile_of(0, 0, 1)
        before = tile_of(1, 1, 1)
        whole.append(window([jnp.where(sub < EDGE, a, b) for a, b in zip(after, before)]))
        bed = jnp.concatenate(whole, axis=0)
    else:
        bed = rest[0][...]
    square = shear_x * shear_x + shear_y * shear_y
    factor = jnp.maximum(square - threshold_sq, 0.0) / (square + threshold_sq)
    load_x = shear_x * factor
    load_y = shear_y * factor
    divergence = 0.5 * (ahead(load_x, 1, 1) - ahead(load_x, -1, 1)) + 0.5 * (
        ahead(load_y, 1, 0) - ahead(load_y, -1, 0)
    )
    row = iota((tall * SUB, wide), 0)
    col = iota((tall * SUB, wide), 1)
    last_plane = plane == lax.axis_size("plane") - 1
    last_span = span == lax.axis_size("span") - 1
    row_low = jnp.where(last_plane, rows, rows + EDGE)
    row_high = jnp.where(plane == 0, rows + SUB, rows + EDGE)
    col_low = jnp.where(last_span, wide - LANE, wide - LANE // 2)
    col_high = jnp.where(span == 0, wide, wide - LANE // 2)
    valid = ((row < row_low) | (row >= row_high)) & ((col < col_low) | (col >= col_high))

    def step(height):
        around = ahead(height, 1, 0) + ahead(height, -1, 0) + ahead(height, 1, 1) + ahead(height, -1, 1)
        return height - bed_step * divergence + bed_step * slope_rate * (around - 4.0 * height)

    first = jnp.where(valid, step(bed), 0.0)
    out_ref[...] = step(first)[:rows, : lanes * LANE]


def pairings(axis):
    size = lax.axis_size(axis)
    lists = []
    for start in (0, 1):
        found = []
        for i in range(start, size - 1, 2):
            found += [(i, i + 1), (i + 1, i)]
        lists.append(found)
    return lists


def bed_around(bed_height, rows, cols):
    spans = lax.axis_size("span")
    whole = lax.all_gather(bed_height, ("span", "wall"), axis=0, tiled=True)
    padded = jnp.pad(whole, ((0, 0), (EDGE, EDGE)))
    piece = lax.dynamic_slice_in_dim(padded, lax.axis_index("span") * cols, cols + 2 * EDGE, axis=1)
    size = lax.axis_size("plane")
    up = [(i, i + 1) for i in range(size - 1)]
    before = lax.ppermute(piece[-EDGE:], "plane", up)
    after = lax.ppermute(piece[:EDGE], "plane", [(j, i) for i, j in up])
    tall = jnp.concatenate([piece, after, before], axis=0)
    gap = jnp.zeros((tall.shape[0], LANE - 2 * EDGE), jnp.float32)
    return jnp.concatenate([tall[:, EDGE:], gap, tall[:, :EDGE]], axis=1)


def body(velocity, levels, fraction, bed_height):
    _, layers, rows, cols = velocity.shape
    tiles = rows // SUB
    tall = tiles + 1
    lanes = cols // LANE
    spans = lax.axis_size("span")
    walls = lax.axis_size("wall")
    assert walls == 2 and layers * 2 * EDGE == LANE
    bed_in = spans == 2 and bed_height.shape == (SUB, 2 * cols)
    count = 3 * layers // 2 + 1 + (bed_height.shape[1] // cols if bed_in else 0)
    dma = pltpu.SemaphoreType.DMA
    sheet = (3, layers, SUB, cols)
    send_a, send_b, send_z = call(
        functools.partial(pack_kernel, layers, bed_in),
        [(count, SUB, cols), (count, SUB, cols), (3, 2, rows, cols)],
        [velocity, levels, fraction, bed_height],
        [pltpu.VMEM(sheet, jnp.float32), pltpu.VMEM(sheet, jnp.float32), dma((3,))],
        any_inputs=(0,),
        flops=1,
        moved=1_000_000,
        limit=10,
    )
    plane_a, plane_b = pairings("plane")
    got_a = lax.ppermute(send_a, "plane", plane_a)
    got_b = lax.ppermute(send_b, "plane", plane_b)
    got_z = lax.ppermute(send_z, "wall", pairings("wall")[0])
    deep = (3, layers + 4, rows, cols)
    new, shear, edge = call(
        functools.partial(inner_kernel, layers),
        [velocity.shape, (2, rows, cols), (2, 5, tiles, SUB, LANE)],
        [velocity, levels, fraction],
        [pltpu.VMEM(deep, jnp.float32), pltpu.VMEM(deep, jnp.float32)],
        flops=20_000_000,
        moved=3_000_000,
    )
    span_lists = [p for p in pairings("span") if p]
    message = (5 * tall + (4 * lanes if bed_in else 0), SUB, LANE)
    unpacked = call(
        functools.partial(unpack_kernel, layers, count, bed_in),
        [sheet, (2, SUB, cols), (2, 5 * tall, SUB, LANE)] + [message] * len(span_lists),
        [got_a, got_b, edge, bed_height],
        moved=1_000_000,
        limit=10,
    )
    halo, flat, full = unpacked[:3]
    messages = unpacked[3:]
    got = [lax.ppermute(m, "span", pairs) for m, pairs in zip(messages, span_lists)]
    shallow = (3, layers + 4, SUB, cols)
    new_top, new_bottom, strip_shear = call(
        functools.partial(strip_kernel, layers),
        [sheet, sheet, (2, 2, SUB, cols)],
        [velocity, levels, fraction, halo, flat],
        [pltpu.VMEM(sheet, jnp.float32)] * 2 + [pltpu.VMEM(shallow, jnp.float32)] * 2 + [dma((2,))],
        any_inputs=(0,),
        flops=10_000_000,
        moved=2_000_000,
    )
    shear_count = 2 * tall * (lanes + 1)
    out_count = shear_count + (8 * lanes if bed_in else 0)
    fresh, mine = call(
        functools.partial(side_kernel, layers, len(got), bed_in),
        [(2, 3, tall * SUB, LANE), (out_count, SUB, LANE)],
        [full, shear, strip_shear] + got + [messages[0]],
        moved=1_000_000,
        limit=10,
    )
    theirs = lax.ppermute(mine, "wall", pairings("wall")[0])
    (velocity_next,) = call(
        functools.partial(merge_kernel, layers),
        [velocity.shape],
        [new, new_top, new_bottom, fresh, got_z, levels, fraction],
        flops=2_000_000,
        moved=4_000_000,
    )
    extra = [] if bed_in else [bed_around(bed_height, rows, cols)]
    (bed_next,) = call(
        functools.partial(bed_kernel, tall, lanes, bed_in),
        [(rows, cols)],
        [mine, theirs] + extra,
        moved=1_000_000,
        limit=10,
    )
    return velocity_next, bed_next


def solution(mesh):
    return jax.shard_map(
        body,
        mesh=mesh,
        in_specs=(
            P("groups", "wall", "plane", "span"),
            P(("groups", "plane"), "span"),
            P(("groups", "plane"), "span"),
            P(("groups", "plane", "span", "wall"), None),
        ),
        out_specs=(P("groups", "wall", "plane", "span"), P(("groups", "plane"), "span")),
        check_vma=False,
    )
```

time: 92.5 us -> 27.7 us (0.30)
  the two profiles are of different devices: /device:TPU:0 before, /device:TPU:17 now
where the time goes in v1:
time: 27.7 us; the launch traced here: 27.3 us
  Pallas kernels  14.9 us (54%)
  starting transfers between devices  6.74 us (24%)
  local copies, waits for them, and re-layouts  3.65 us (13%)
  waiting for transfers between devices  1.26 us (5%)
  between operations  0.74 us (3%)
    pallas_call x7, Pallas kernels, call(): pl.pallas_call(kernel, out_shape=shapes, in_specs=specs, out_specs=[pl.Bl...  14.9 us
    unnamed x16, local copies, waits for them, and re-layouts  3.65 us
    ppermute x1, starting transfers between devices, body(): got_z = lax.ppermute(send_z, 'wall', pairings('wall')[0])  2.14 us
    ppermute x1, starting transfers between devices, body(): got_b = lax.ppermute(send_b, 'plane', plane_b)  1.91 us
    ppermute x1, starting transfers between devices, body(): got_a = lax.ppermute(send_a, 'plane', plane_a)  1.36 us
    ppermute x1, starting transfers between devices, body(): lax.ppermute(m, 'span', pairs)  1.25 us
    ppermute x1, waiting for transfers between devices, body(): got_b = lax.ppermute(send_b, 'plane', plane_b)  1.25 us
  transfers between devices with their start and end apart: 5, of which 1 were waited for; matrix products, arithmetic and copies ran while one was open for 0% of the time, Pallas kernels for 49%

profile of v1, /device:TPU:17, one launch (start us, length us, event | category | flops | bytes accessed | tf_op | source)
XLA Modules:
  0.0 27.3 jit_solution(10582578245922971617)
XLA Ops:
  0.6 0.0 copy-start
  0.6 1.4 %copy-done = f32[3,16,32,256]{3,2,1,0:T(8,128)S(1)} copy-done((f32[3,16,32,256]{3,2,1,0:T(8,128)S(1)}, f32[3,16,32,256]{3,2,1,0:T(8,128)}, u32[]{:S(2)}) %copy-start) | copy-done | bytes 1572888
  2.0 0.0 copy-start.2
  2.0 0.8 %copy-done.2 = s32[32,256]{1,0:T(8,128)S(1)} copy-done((s32[32,256]{1,0:T(8,128)S(1)}, s32[32,256]{1,0:T(8,128)}, u32[]{:S(2)}) %copy-start.2) | copy-done | bytes 32792
  2.8 0.0 copy-start.4
  2.8 0.8 %copy-done.4 = f32[32,256]{1,0:T(8,128)S(1)} copy-done((f32[32,256]{1,0:T(8,128)S(1)}, f32[32,256]{1,0:T(8,128)}, u32[]{:S(2)}) %copy-start.4) | copy-done | bytes 32792
  3.6 0.0 copy-start.6
  3.6 0.7 %copy-done.6 = f32[8,512]{1,0:T(8,128)S(1)} copy-done((f32[8,512]{1,0:T(8,128)S(1)}, f32[8,512]{1,0:T(8,128)}, u32[]{:S(2)}) %copy-start.6) | copy-done | bytes 16408
  4.3 0.0 copy-start.1
  4.3 0.0 copy-start.3
  4.3 0.0 copy-start.5
  4.3 0.2 shard_map.60
  4.5 1.4 %collective-permute-start = (f32[27,8,256]{2,1,0:T(8,128)S(1)}, f32[27,8,256]{2,1,0:T(8,128)S(1)}, u32[]{:S(2)}, u32[]{:S(2)}) collective-permute-start(f32[27,8,256]{2,1,0:T(8,128)S(1)} %get-tuple-element.18), channel_id=1, source_target_pairs={{0,4},{4,0},{8,12},{12,8},{1,5},{5,1},{9,13},{13,9},{2,6},{6,2},{1... | collective-permute-start | bytes 663560 | tf_op jit(solution)/shard_map/ppermute | solution.py:570
  5.9 1.9 %collective-permute-start.1 = (f32[27,8,256]{2,1,0:T(8,128)S(1)}, f32[27,8,256]{2,1,0:T(8,128)S(1)}, u32[]{:S(2)}, u32[]{:S(2)}) collective-permute-start(f32[27,8,256]{2,1,0:T(8,128)S(1)} %get-tuple-element.19), channel_id=1, source_target_pairs={{4,8},{8,4},{5,9},{9,5},{6,10},{10,6},{7,11},{11,7},{20,24},{24,20... | collective-permute-start | bytes 663560 | tf_op jit(solution)/shard_map/ppermute | solution.py:571
  7.8 0.0 copy-done.1
  7.8 0.0 copy-done.3
  7.8 0.0 copy-done.5
  7.8 4.6 %shard_map.59 = (f32[3,16,32,256]{3,2,1,0:T(8,128)S(1)}, f32[2,32,256]{2,1,0:T(8,128)S(1)}, f32[2,5,4,8,128]{4,3,2,1,0:T(8,128)S(1)}) custom-call(f32[3,16,32,256]{3,2,1,0:T(8,128)S(1)} %copy-done.1, s32[32,256]{1,0:T(8,128)S(1)} %copy-done.3, f32[32,256]{1,0:T(8,128)S(1)} %copy-done.5), custom_call_target="tpu_custom_call" | custom-call | flops 20000000 | bytes 3000000 | tf_op jit(solution)/shard_map/pallas_call | solution.py:25
  12.5 0.0 collective-permute-done.got_a
  12.5 1.2 %collective-permute-done.1.got_b = f32[27,8,256]{2,1,0:T(8,128)S(1)} collective-permute-done((f32[27,8,256]{2,1,0:T(8,128)S(1)}, f32[27,8,256]{2,1,0:T(8,128)S(1)}, u32[]{:S(2)}, u32[]{:S(2)}) %collective-permute-start.1) | collective-permute-done | bytes 221216 | tf_op jit(solution)/shard_map/ppermute | solution.py:571
  13.7 0.0 copy-done.7
  13.8 0.3 %shard_map.61 = (f32[3,16,8,256]{3,2,1,0:T(8,128)S(1)}, f32[2,8,256]{2,1,0:T(8,128)S(1)}, f32[2,25,8,128]{3,2,1,0:T(8,128)S(1)}, f32[33,8,128]{2,1,0:T(8,128)S(1)}) custom-call(f32[27,8,256]{2,1,0:T(8,128)S(1)} %collective-permute-done.got_a, f32[27,8,256]{2,1,0:T(8,128)S(1)} %collective-permute-done.1.got_b, ...), custom_call_target="tpu_custom_call" | custom-call | bytes 1000000 | tf_op jit(solution)/shard_map/pallas_call | solution.py:25
  14.1 1.2 %collective-permute-start.2 = (f32[33,8,128]{2,1,0:T(8,128)S(1)}, f32[33,8,128]{2,1,0:T(8,128)S(1)}, u32[]{:S(2)}, u32[]{:S(2)}) collective-permute-start(f32[33,8,128]{2,1,0:T(8,128)S(1)} %get-tuple-element.28.rest_1_), channel_id=1, source_target_pairs={{0,2},{2,0},{1,3},{3,1},{4,6},{6,4},{5,7},{7,5},{8,10},{10,8},{9,1... | collective-permute-start | bytes 405512 | tf_op jit(solution)/shard_map/ppermute | solution.py:593
  15.3 2.1 %collective-permute-start.3 = (f32[3,2,32,256]{3,2,1,0:T(8,128)S(1)}, f32[3,2,32,256]{3,2,1,0:T(8,128)S(1)}, u32[]{:S(2)}, u32[]{:S(2)}) collective-permute-start(f32[3,2,32,256]{3,2,1,0:T(8,128)S(1)} %get-tuple-element.30), channel_id=1, source_target_pairs={{0,1},{1,0},{2,3},{3,2},{4,5},{5,4},{6,7},{7,6},{8,9},{9,8},{10,11... | collective-permute-start | bytes 589832 | tf_op jit(solution)/shard_map/ppermute | solution.py:572
  17.5 5.6 %shard_map.62 = (f32[3,16,8,256]{3,2,1,0:T(8,128)S(1)}, f32[3,16,8,256]{3,2,1,0:T(8,128)S(1)}, f32[2,2,8,256]{3,2,1,0:T(8,128)S(1)}) custom-call(f32[3,16,32,256]{3,2,1,0:T(8,128)S(1)} %copy-done.1, s32[32,256]{1,0:T(8,128)S(1)} %copy-done.3, f32[32,256]{1,0:T(8,128)S(1)} %copy-done.5, f32[3,16,8,256]{3,2,1,0:T(8,128)S(1)} %get-tuple-element.21.halo, ...), custom_call_target="tpu_custom_call" | custom-call | flops 10000000 | bytes 2000000 | tf_op jit(solution)/shard_map/pallas_call | solution.py:25
  23.1 0.0 collective-permute-done.2.rest_0_
  23.1 0.8 %shard_map.63 = (f32[2,3,40,128]{3,2,1,0:T(8,128)S(1)}, f32[46,8,128]{2,1,0:T(8,128)S(1)}) custom-call(f32[2,25,8,128]{3,2,1,0:T(8,128)S(1)} %get-tuple-element.25.full, f32[2,32,256]{2,1,0:T(8,128)S(1)} %get-tuple-element.26.shear, f32[2,2,8,256]{3,2,1,0:T(8,128)S(1)} %get-tuple-element.27.strips, f32[33,8,128]{2,1,0:T(8,128)S(1)} %collective-permute-done.2.rest_0_, ...), custom_call_target="tpu_custom_call" | custom-call | bytes 1000000 | tf_op jit(solution)/shard_map/pallas_call | solution.py:25
  23.9 0.1 collective-permute-start.4
  24.0 0.0 collective-permute-done.3.far
  24.0 2.4 %shard_map.64 = f32[3,16,32,256]{3,2,1,0:T(8,128)} custom-call(f32[3,16,32,256]{3,2,1,0:T(8,128)S(1)} %get-tuple-element.17.new, f32[3,16,8,256]{3,2,1,0:T(8,128)S(1)} %get-tuple-element.23.strip_top, f32[3,16,8,256]{3,2,1,0:T(8,128)S(1)} %get-tuple-element.24.strip_bottom, f32[2,3,40,128]{3,2,1,0:T(8,128)S(1)} %get-tuple-element.29.fresh, ...), custom_call_target="tpu_custom_call" | custom-call | flops 2000000 | bytes 4000000 | tf_op jit(solution)/shard_map/pallas_call | solution.py:25
  26.5 0.0 collective-permute-done.4.theirs
  26.5 0.9 %shard_map.65 = f32[32,256]{1,0:T(8,128)} custom-call(f32[46,8,128]{2,1,0:T(8,128)S(1)} %get-tuple-element.31.mine, f32[46,8,128]{2,1,0:T(8,128)S(1)} %collective-permute-done.4.theirs), custom_call_target="tpu_custom_call" | custom-call | bytes 1000000 | tf_op jit(solution)/shard_map/pallas_call | solution.py:25
  (1 shorter events, 0.0 us)
Async XLA Ops:
  0.6 1.4 %copy-start = (f32[3,16,32,256]{3,2,1,0:T(8,128)S(1)}, f32[3,16,32,256]{3,2,1,0:T(8,128)}, u32[]{:S(2)}) copy-start(f32[3,16,32,256]{3,2,1,0:T(8,128)} %vel.5) | copy-start | bytes 4718596
  2.0 0.8 %copy-start.2 = (s32[32,256]{1,0:T(8,128)S(1)}, s32[32,256]{1,0:T(8,128)}, u32[]{:S(2)}) copy-start(s32[32,256]{1,0:T(8,128)} %lev.7) | copy-start | bytes 98308
  2.8 0.8 %copy-start.4 = (f32[32,256]{1,0:T(8,128)S(1)}, f32[32,256]{1,0:T(8,128)}, u32[]{:S(2)}) copy-start(f32[32,256]{1,0:T(8,128)} %frac.7) | copy-start | bytes 98308
  3.6 0.7 %copy-start.6 = (f32[8,512]{1,0:T(8,128)S(1)}, f32[8,512]{1,0:T(8,128)}, u32[]{:S(2)}) copy-start(f32[8,512]{1,0:T(8,128)} %bed.3) | copy-start | bytes 49156
  4.3 3.5 %copy-start.1 = (f32[3,16,32,256]{3,2,1,0:T(8,128)S(1)}, f32[3,16,32,256]{3,2,1,0:T(8,128)}, u32[]{:S(2)}) copy-start(f32[3,16,32,256]{3,2,1,0:T(8,128)} %vel.5) | copy-start | bytes 4718596
  4.3 3.5 %copy-start.3 = (s32[32,256]{1,0:T(8,128)S(1)}, s32[32,256]{1,0:T(8,128)}, u32[]{:S(2)}) copy-start(s32[32,256]{1,0:T(8,128)} %lev.7) | copy-start | bytes 98308
  4.3 3.5 %copy-start.5 = (f32[32,256]{1,0:T(8,128)S(1)}, f32[32,256]{1,0:T(8,128)}, u32[]{:S(2)}) copy-start(f32[32,256]{1,0:T(8,128)} %frac.7) | copy-start | bytes 98308
  4.3 9.5 %copy-start.7 = (f32[8,512]{1,0:T(8,128)S(1)}, f32[8,512]{1,0:T(8,128)}, u32[]{:S(2)}) copy-start(f32[8,512]{1,0:T(8,128)} %bed.3) | copy-start | bytes 49156
  4.5 8.0 %collective-permute-start = (f32[27,8,256]{2,1,0:T(8,128)S(1)}, f32[27,8,256]{2,1,0:T(8,128)S(1)}, u32[]{:S(2)}, u32[]{:S(2)}) collective-permute-start(f32[27,8,256]{2,1,0:T(8,128)S(1)} %get-tuple-element.18), channel_id=1, source_target_pairs={{0,4},{4,0},{8,12},{12,8},{1,5},{5,1},{9,13},{13,9},{2,6},{6,2},{1... | collective-permute-start | bytes 663560 | tf_op jit(solution)/shard_map/ppermute | solution.py:570
  5.9 7.9 %collective-permute-start.1 = (f32[27,8,256]{2,1,0:T(8,128)S(1)}, f32[27,8,256]{2,1,0:T(8,128)S(1)}, u32[]{:S(2)}, u32[]{:S(2)}) collective-permute-start(f32[27,8,256]{2,1,0:T(8,128)S(1)} %get-tuple-element.19), channel_id=1, source_target_pairs={{4,8},{8,4},{5,9},{9,5},{6,10},{10,6},{7,11},{11,7},{20,24},{24,20... | collective-permute-start | bytes 663560 | tf_op jit(solution)/shard_map/ppermute | solution.py:571
  14.1 9.0 %collective-permute-start.2 = (f32[33,8,128]{2,1,0:T(8,128)S(1)}, f32[33,8,128]{2,1,0:T(8,128)S(1)}, u32[]{:S(2)}, u32[]{:S(2)}) collective-permute-start(f32[33,8,128]{2,1,0:T(8,128)S(1)} %get-tuple-element.28.rest_1_), channel_id=1, source_target_pairs={{0,2},{2,0},{1,3},{3,1},{4,6},{6,4},{5,7},{7,5},{8,10},{10,8},{9,1... | collective-permute-start | bytes 405512 | tf_op jit(solution)/shard_map/ppermute | solution.py:593
  15.3 8.6 %collective-permute-start.3 = (f32[3,2,32,256]{3,2,1,0:T(8,128)S(1)}, f32[3,2,32,256]{3,2,1,0:T(8,128)S(1)}, u32[]{:S(2)}, u32[]{:S(2)}) collective-permute-start(f32[3,2,32,256]{3,2,1,0:T(8,128)S(1)} %get-tuple-element.30), channel_id=1, source_target_pairs={{0,1},{1,0},{2,3},{3,2},{4,5},{5,4},{6,7},{7,6},{8,9},{9,8},{10,11... | collective-permute-start | bytes 589832 | tf_op jit(solution)/shard_map/ppermute | solution.py:572
  23.9 2.5 %collective-permute-start.4 = (f32[46,8,128]{2,1,0:T(8,128)S(1)}, f32[46,8,128]{2,1,0:T(8,128)S(1)}, u32[]{:S(2)}, u32[]{:S(2)}) collective-permute-start(f32[46,8,128]{2,1,0:T(8,128)S(1)} %get-tuple-element.31.mine), channel_id=1, source_target_pairs={{0,1},{1,0},{2,3},{3,2},{4,5},{5,4},{6,7},{7,6},{8,9},{9,8},{10,11... | collective-permute-start | bytes 565256 | tf_op jit(solution)/shard_map/ppermute | solution.py:613

commit v2 on v1

--- a/solution.py
+++ b/solution.py
@@ -19,14 +19,14 @@
 MIB = 1024 * 1024
 
 
-def call(kernel, outs, ins, scratch=(), any_inputs=(), flops=0, moved=0, limit=20, aliases=None):
+def call(kernel, outs, ins, scratch=(), any_inputs=(), any_outputs=(), flops=0, moved=0, limit=20, aliases=None):
     specs = [pl.BlockSpec(memory_space=pl.ANY if i in any_inputs else VMEM) for i in range(len(ins))]
     shapes = [jax.ShapeDtypeStruct(s, jnp.float32) for s in outs]
     return pl.pallas_call(
         kernel,
         out_shape=shapes,
         in_specs=specs,
-        out_specs=[pl.BlockSpec(memory_space=VMEM) for _ in outs],
+        out_specs=[pl.BlockSpec(memory_space=pl.ANY if i in any_outputs else VMEM) for i in range(len(outs))],
         scratch_shapes=list(scratch),
         input_output_aliases=aliases or {},
         cost_estimate=pl.CostEstimate(flops=flops, bytes_accessed=moved, transcendentals=0),
@@ -55,14 +55,14 @@
     return lax.rem(lax.axis_index(axis), 2) == 0
 
 
-def brick(read, level, fraction, base, layers, q_ref, f_ref, write):
+def brick(read, level, fraction, base, layers, q_ref, f_ref, write, extra, unroll):
     rows, cols = level.shape
     blank = jnp.zeros((rows, cols), jnp.float32)
     for c in range(3):
         for z in (0, 1, layers + 2, layers + 3):
             q_ref[c, z] = blank
             f_ref[c, z] = blank
-    cut_gain = fraction * (gain / 1.0)
+    cut_gain = fraction * gain
     scale = 1.0 / (0.5 + fraction)
 
     def prepare(z, carry):
@@ -74,7 +74,7 @@
             f_ref[c, z + 2] = vel[2] * q
         return carry
 
-    lax.fori_loop(0, layers, prepare, 0, unroll=2)
+    lax.fori_loop(0, layers, prepare, 0, unroll=4)
 
     def vertical(c, z):
         near = f_ref[c, z + 3] - f_ref[c, z + 1]
@@ -86,8 +86,6 @@
         found = []
         for c in range(2):
             total = blank
-            if z + 3 <= layers + 3 and z + 1 >= 0:
-                low, high = (z + 1, z + 3)
             for offset, weight_f, weight_q in ((1, -8.0, 6.0), (-1, 8.0, 6.0), (2, 1.0, 0.0), (-2, -1.0, 0.0)):
                 at = z + offset
                 if 0 <= at < layers:
@@ -97,7 +95,7 @@
             found.append(jnp.where(hit, cut_gain * total, 0.0))
         return found
 
-    sums = [blank, blank]
+    sums = extra
     for z in (-2, -1, layers, layers + 1):
         found = outside(z)
         sums = [s + f for s, f in zip(sums, found)]
@@ -123,47 +121,93 @@
                 sums[c] = sums[c] + jnp.where(hit, fresh, 0.0)
         return tuple(sums)
 
-    sums = lax.fori_loop(0, layers, update, tuple(sums))
+    sums = lax.fori_loop(0, layers, update, tuple(sums), unroll=unroll)
     return [s * scale for s in sums]
 
 
-def pack_kernel(layers, bed_in, vel, lev, frac, bed, a_ref, b_ref, z_ref, top, bottom, sems):
-    rows = lev.shape[0]
+def beyond_terms(tile, level, fraction, base, layers, forward):
+    near = pltpu.roll(level, SUB - 1, 0) if forward else pltpu.roll(level, 1, 0)
+    far = pltpu.roll(level, SUB - 2, 0) if forward else pltpu.roll(level, 2, 0)
+    sign = 1.0 if forward else -1.0
+    one = [jnp.zeros(level.shape, jnp.float32)] * 2
+    two = list(one)
+    for z in range(layers):
+        layer = (base + z).astype(jnp.float32)
+        opened = opened_at(level, fraction, layer)
+        near_hit, far_hit = near == layer, far == layer
+        for c in range(2):
+            q = opened * tile[c, z]
+            flux = sign * (tile[1, z] * q)
+            one[c] = one[c] + jnp.where(near_hit, 6.0 * q + 8.0 * flux, 0.0)
+            two[c] = two[c] - jnp.where(far_hit, flux, 0.0)
+    sub = iota(level.shape, 0)
+    source = SUB - 3 if forward else 2
+    past = source - 1 if forward else source + 1
+    shift = 1 if forward else SUB - 1
+    shift_two = 2 if forward else SUB - 2
+    found = []
+    for c in range(2):
+        a = pltpu.roll(jnp.where(sub == source, one[c], 0.0), shift, 0)
+        b = pltpu.roll(jnp.where((sub == source) | (sub == past), two[c], 0.0), shift_two, 0)
+        found.append(a + b)
+    return found
+
+
+def pack_kernel(layers, bed_in, vel_in, lev_in, frac_in, bed_from, a_ref, b_ref, z_ref, vel, flat, bed, lev, sems):
+    _, rows, cols = flat.shape
     wall = lax.axis_index("wall")
-    start = jnp.where(wall == 0, layers - 2, 0)
-    copies = [
-        pltpu.make_async_copy(vel.at[:, :, pl.ds(0, SUB), :], top, sems.at[0]),
-        pltpu.make_async_copy(vel.at[:, :, pl.ds(rows - SUB, SUB), :], bottom, sems.at[1]),
-        pltpu.make_async_copy(vel.at[:, pl.ds(start, 2)], z_ref, sems.at[2]),
+    base = wall * layers
+    small = [
+        pltpu.make_async_copy(lev_in, lev, sems.at[0]),
+        pltpu.make_async_copy(frac_in, flat.at[1], sems.at[1]),
+        pltpu.make_async_copy(bed_from, bed, sems.at[2]),
     ]
-    for copy in copies:
+    pieces = []
+    for i, (start, size) in enumerate(((0, SUB), (rows - SUB, SUB), (SUB, rows - 2 * SUB))):
+        at = pl.ds(start, size)
+        pieces.append(pltpu.make_async_copy(vel_in.at[:, :, at, :], vel.at[:, :, at, :], sems.at[3 + i]))
+    for copy in small + pieces:
         copy.start()
-    cols = lev.shape[1]
-    half = iota((SUB, cols), 0) < EDGE
+    sub = iota((SUB, cols), 0)
+    pair = sub // 2
     is_even = even("plane")
 
     def put(n, low, high):
         a_ref[n] = jnp.where(is_even, low, high)
         b_ref[n] = jnp.where(is_even, high, low)
 
-    levels = lev[...].astype(jnp.float32)
-    count = 3 * layers // 2
-    put(
-        count,
-        jnp.where(half, pltpu.roll(levels[-SUB:], EDGE, 0), frac[-SUB:]),
-        jnp.where(half, levels[:SUB], pltpu.roll(frac[:SUB], EDGE, 0)),
-    )
+    def stack(fields, place):
+        tile = jnp.zeros((SUB, cols), jnp.float32)
+        for i, field in enumerate(fields):
+            tile = jnp.where(pair == i, pltpu.roll(field, (2 * i + place) % SUB, 0), tile)
+        return tile
+
+    for copy in small:
+        copy.wait()
+    flat[0] = lev[...].astype(jnp.float32)
+    low_lev, low_frac = flat[0, rows - SUB :], flat[1, rows - SUB :]
+    high_lev, high_frac = flat[0, :SUB], flat[1, :SUB]
+    count = 3 * layers // 4
     if bed_in:
-        for i in range(bed.shape[1] // cols):
-            tile = bed[:, i * cols : (i + 1) * cols]
-            put(count + 1 + i, tile, tile)
-    for copy in copies:
+        halves = [bed[:, i * cols : (i + 1) * cols] for i in range(bed.shape[1] // cols)]
+        put(count + 1, stack(halves, 2), stack(halves, 0))
+    for copy in pieces[:2]:
         copy.wait()
-    for c in range(3):
-        for k in range(layers // 2):
-            low = jnp.where(half, pltpu.roll(bottom[c, 2 * k], EDGE, 0), bottom[c, 2 * k + 1])
-            high = jnp.where(half, top[c, 2 * k], pltpu.roll(top[c, 2 * k + 1], EDGE, 0))
-            put(c * (layers // 2) + k, low, high)
+    top = vel.at[:, :, pl.ds(0, SUB), :]
+    bottom = vel.at[:, :, pl.ds(rows - SUB, SUB), :]
+    for c in range(3):
+        for k in range(layers // 4):
+            low = stack([bottom[c, 4 * k + i] for i in range(4)], 2)
+            high = stack([top[c, 4 * k + i] for i in range(4)], 0)
+            put(c * (layers // 4) + k, low, high)
+    low_far = beyond_terms(bottom, low_lev, low_frac, base, layers, True)
+    high_far = beyond_terms(top, high_lev, high_frac, base, layers, False)
+    put(count, stack([low_lev, low_frac] + low_far, 2), stack([high_lev, high_frac] + high_far, 0))
+    pieces[2].wait()
+    start = jnp.where(wall == 0, layers - 2, 0)
+    for c in range(3):
+        for z in range(2):
+            z_ref[c, z] = vel[c, start + z]
 
 
 def gather_edges(read, layers, rows, cols, put):
@@ -196,110 +240,197 @@
     return right, left
 
 
-def inner_kernel(layers, vel, lev, frac, new_ref, shear_ref, edge_ref, q_ref, f_ref):
-    rows, cols = lev.shape
+def inner_kernel(layers, vel, flat, new_ref, shear_ref, edge_ref, q_ref, f_ref, split_ref, band_ref, x_ref):
+    _, rows, cols = flat.shape
     base = lax.axis_index("wall") * layers
-    levels = lev[...].astype(jnp.float32)
-    fraction = frac[...]
-
-    def write(c, z, value):
-        new_ref[c, z] = value
-
-    sums = brick(lambda c, z: vel[c, z], levels, fraction, base, layers, q_ref, f_ref, write)
-    shear_ref[0] = sums[0]
-    shear_ref[1] = sums[1]
+    lanes = cols // LANE
+    tall = iota((cols, cols), 0) - iota((cols, cols), 1)
+    flux_band = jnp.where(tall == 1, -8.0, jnp.where(tall == -1, 8.0, 0.0))
+    flux_band = flux_band + jnp.where(tall == 2, 1.0, jnp.where(tall == -2, -1.0, 0.0))
+    field_band = jnp.where(jnp.abs(tall) == 1, 6.0, jnp.where(tall == 0, -36.0, 0.0))
+    for i, band in enumerate((flux_band, flux_band, field_band, field_band)):
+        band_ref[i * cols : (i + 1) * cols] = band.astype(jnp.bfloat16)
+    blank = jnp.zeros((rows, cols), jnp.float32)
+    for c in range(3):
+        for z in (0, 1, layers + 2, layers + 3):
+            q_ref[c, z] = blank
+            f_ref[c, z] = blank
+
+    def halves(x):
+        high = x.astype(jnp.bfloat16)
+        return high, (x - high.astype(jnp.float32)).astype(jnp.bfloat16)
+
+    def prepare(z, carry):
+        layer = (base + z).astype(jnp.float32)
+        at = pl.ds(pl.multiple_of(z * rows, rows), rows)
+        for k in range(lanes):
+            cut = slice(k * LANE, (k + 1) * LANE)
+            opened = opened_at(flat[0, :, cut], flat[1, :, cut], layer)
+            vel_x, vel_z = vel[0, z, :, cut], vel[2, z, :, cut]
+            for c in range(3):
+                q = opened * vel[c, z, :, cut]
+                q_ref[c, z + 2, :, cut] = q
+                f_ref[c, z + 2, :, cut] = vel_z * q
+                parts = halves(vel_x * q) + halves(q)
+                for i, part in enumerate(parts):
+                    split_ref[c, at, i * cols + k * LANE : i * cols + (k + 1) * LANE] = part
+        return carry
+
+    lax.fori_loop(0, layers, prepare, 0)
+    for c in range(3):
+        x_ref[c] = jnp.dot(split_ref[c], band_ref[...], preferred_element_type=jnp.float32)
+
+    def outside(z, c, cut):
+        total = jnp.zeros((rows, LANE), jnp.float32)
+        for offset, weight in ((1, -8.0), (-1, 8.0), (2, 1.0), (-2, -1.0)):
+            at = z + offset
+            if 0 <= at < layers:
+                total = total + weight * f_ref[c, at + 2, :, cut]
+                if abs(offset) == 1:
+                    total = total + 6.0 * q_ref[c, at + 2, :, cut]
+        hit = flat[0, :, cut] == (base + z).astype(jnp.float32)
+        return jnp.where(hit, gain * flat[1, :, cut] * total, 0.0)
+
+    sums = []
+    for k in range(lanes):
+        for c in range(2):
+            sums.append(sum(outside(z, c, slice(k * LANE, (k + 1) * LANE)) for z in (-2, -1, layers, layers + 1)))
+
+    def update(z, sums):
+        sums = list(sums)
+        layer = (base + z).astype(jnp.float32)
+        at = pl.ds(pl.multiple_of(z * rows, rows), rows)
+        for k in range(lanes):
+            cut = slice(k * LANE, (k + 1) * LANE)
+            level = flat[0, :, cut]
+            weight = gain * opened_at(level, flat[1, :, cut], layer)
+            hit = level == layer
+            vel_y = vel[1, z, :, cut]
+            for c in range(3):
+                q = q_ref[c, z + 2, :, cut]
+                flux = f_ref[1, z + 2, :, cut] if c == 2 else vel_y * q
+                total = x_ref[c, at, cut] + sweep(flux, 6.0 * q, 0)
+                near = f_ref[c, z + 3, :, cut] - f_ref[c, z + 1, :, cut]
+                both = q_ref[c, z + 3, :, cut] + q_ref[c, z + 1, :, cut]
+                total = total + (6.0 * both - 8.0 * near + (f_ref[c, z + 4, :, cut] - f_ref[c, z, :, cut]))
+                fresh = vel[c, z, :, cut] + weight * total
+                new_ref[c, z, :, cut] = fresh
+                if c < 2:
+                    sums[2 * k + c] = sums[2 * k + c] + jnp.where(hit, fresh, 0.0)
+        return tuple(sums)
+
+    sums = lax.fori_loop(0, layers, update, tuple(sums))
+    for k in range(lanes):
+        cut = slice(k * LANE, (k + 1) * LANE)
+        scale = 1.0 / (0.5 + flat[1, :, cut])
+        for c in range(2):
+            shear_ref[c, :, cut] = sums[2 * k + c] * scale
 
     def put(side, n, value):
         edge_ref[side, n] = value.reshape(rows // SUB, SUB, LANE)
 
     gather_edges(lambda c, z: vel[c, z], layers, rows, cols, put)
-    for n, field in ((3, levels), (4, fraction)):
-        right, left = repeat_edges(field, rows, cols)
-        put(0, n, right)
-        put(1, n, left)
-
-
-def unpack_kernel(layers, count, bed_in, got_a, got_b, edge, bed, halo_ref, flat_ref, full_ref, *messages):
+    for n in range(2):
+        right, left = repeat_edges(flat[n], rows, cols)
+        put(0, 3 + n, right)
+        put(1, 3 + n, left)
+
+
+def unpack_kernel(layers, bed_in, got_a, got_b, edge, bed, got_z, halo_ref, beside_ref, full_ref, far_ref, *messages):
     cols = halo_ref.shape[3]
     tiles = edge.shape[2]
-    half = iota((SUB, cols), 0) < EDGE
+    tall = tiles + 1
+    sub = iota((SUB, cols), 0)
     is_even = even("plane")
 
     def sides(n):
         one, two = got_a[n], got_b[n]
         return jnp.where(is_even, one, two), jnp.where(is_even, two, one)
 
-    for c in range(3):
-        for k in range(layers // 2):
-            low, high = sides(c * (layers // 2) + k)
-            halo_ref[c, 2 * k] = jnp.where(half, low, pltpu.roll(high, EDGE, 0))
-            halo_ref[c, 2 * k + 1] = jnp.where(half, pltpu.roll(low, EDGE, 0), high)
-    low, high = sides(3 * layers // 2)
-    levels = jnp.where(half, low, pltpu.roll(high, EDGE, 0))
-    fraction = jnp.where(half, pltpu.roll(low, EDGE, 0), high)
-    flat_ref[0] = levels
-    flat_ref[1] = fraction
+    def spread(n, fields):
+        low, high = sides(n)
+        found = []
+        for i in range(fields):
+            above = pltpu.roll(high, (SUB - 2 - 2 * i) % SUB, 0)
+            below = pltpu.roll(low, (-2 * i) % SUB, 0)
+            found.append(jnp.where(sub < 2, below, jnp.where(sub >= SUB - 2, above, 0.0)))
+        return found
+
+    for c in range(3):
+        for k in range(layers // 4):
+            for i, tile in enumerate(spread(c * (layers // 4) + k, 4)):
+                halo_ref[c, 4 * k + i] = tile
+    count = 3 * layers // 4
+    beside = spread(count, 4)
+    for i, tile in enumerate(beside):
+        beside_ref[i] = tile
 
     def put(side, n, value):
-        full_ref[side, n * (tiles + 1) + tiles] = value
+        full_ref[side, n * tall + tiles] = value
 
     gather_edges(lambda c, z: halo_ref[c, z], layers, SUB, cols, put)
-    for n, field in ((3, levels), (4, fraction)):
-        right, left = repeat_edges(field, SUB, cols)
-        put(0, n, right)
-        put(1, n, left)
+    for n in range(2):
+        right, left = repeat_edges(beside[n], SUB, cols)
+        put(0, 3 + n, right)
+        put(1, 3 + n, left)
     for side in range(2):
         for n in range(5):
             for t in range(tiles):
-                full_ref[side, n * (tiles + 1) + t] = edge[side, n, t]
-    used = 5 * (tiles + 1)
+                full_ref[side, n * tall + t] = edge[side, n, t]
+    lane = iota((SUB, LANE), 1)
+    group = lane // (2 * EDGE)
+    far_right = [repeat_edges(tile, SUB, cols) for tile in beside[2:]]
+    for side in range(2):
+        far_ref[side] = jnp.where(group == 0, far_right[0][side], jnp.where(group == 1, far_right[1][side], 0.0))
     right_first = even("span")
+    packed = []
+    for side, shift in ((0, EDGE), (1, LANE - EDGE)):
+        for t in range(tall):
+            u, v, w, level, fraction = [full_ref[side, n * tall + t] for n in range(5)]
+            last = jnp.where(group == 0, level, jnp.where(group == 1, fraction, 0.0))
+            packed.append(u + pltpu.roll(v, shift, 1))
+            packed.append(w + pltpu.roll(last, shift, 1))
     for i, message in enumerate(messages):
         is_right = right_first if i == 0 else jnp.logical_not(right_first)
-        for n in range(used):
-            message[n] = jnp.where(is_right, full_ref[0, n], full_ref[1, n])
+        for n in range(2 * tall):
+            message[n] = jnp.where(is_right, packed[n], packed[2 * tall + n])
+        message[2 * tall] = jnp.where(is_right, far_ref[0], far_ref[1])
     if bed_in:
+        used = 2 * tall + 1
         parts = bed.shape[1] // LANE
         for i in range(parts):
             messages[0][used + i] = bed[:, i * LANE : (i + 1) * LANE]
         per = cols // LANE
-        for i in range(bed.shape[1] // cols):
-            low, high = sides(3 * layers // 2 + 1 + i)
-            tile = jnp.where(half, low, high)
+        for i, tile in enumerate(spread(count + 1, bed.shape[1] // cols)):
             for j in range(per):
                 messages[0][used + parts + i * per + j] = tile[:, j * LANE : (j + 1) * LANE]
 
 
-def strip_kernel(layers, vel, lev, frac, halo, flat, top_ref, bottom_ref, shear_ref, top, bottom, q_ref, f_ref, sems):
-    rows, cols = lev.shape
-    copies = [
-        pltpu.make_async_copy(vel.at[:, :, pl.ds(0, SUB), :], top, sems.at[0]),
-        pltpu.make_async_copy(vel.at[:, :, pl.ds(rows - SUB, SUB), :], bottom, sems.at[1]),
-    ]
-    for copy in copies:
-        copy.start()
+def strip_kernel(layers, vel, flat, halo, beside, top_ref, bottom_ref, shear_ref, q_ref, f_ref):
+    _, rows, cols = flat.shape
     base = lax.axis_index("wall") * layers
-    half = iota((SUB, cols), 0) < EDGE
-    for copy in copies:
-        copy.wait()
-    for side, own, new in ((0, top, top_ref), (1, bottom, bottom_ref)):
-        inside = half if side == 0 else jnp.logical_not(half)
+    sub = iota((SUB, cols), 0)
+    for side, new in ((0, top_ref), (1, bottom_ref)):
+        inside = sub < EDGE if side == 0 else sub >= EDGE
+        outer = sub >= SUB - 2 if side == 0 else sub < 2
         first = 0 if side == 0 else rows - SUB
-        levels = jnp.where(inside, lev[first : first + SUB].astype(jnp.float32), flat[0])
-        fraction = jnp.where(inside, frac[first : first + SUB], flat[1])
+        at = slice(first, first + SUB)
+        levels = jnp.where(inside, flat[0, at], beside[0])
+        fraction = jnp.where(inside, flat[1, at], beside[1])
+        extra = [jnp.where(outer, gain * fraction * beside[2 + c], 0.0) for c in range(2)]
 
         def read(c, z):
-            return jnp.where(inside, own[c, z], halo[c, z])
+            return jnp.where(inside, vel[c, z, at], halo[c, z])
 
         def write(c, z, value):
             new[c, z] = value
 
-        sums = brick(read, levels, fraction, base, layers, q_ref, f_ref, write)
+        sums = brick(read, levels, fraction, base, layers, q_ref, f_ref, write, extra, 4)
         shear_ref[side, 0] = sums[0]
         shear_ref[side, 1] = sums[1]
 
 
-def column_strip(vel, levels, fraction, base, layers):
+def column_strip(vel, levels, fraction, extra, base, layers):
     shape = levels.shape
     width = 2 * EDGE
     here = iota(shape, 1) // width
@@ -332,11 +463,22 @@
             while step >= width:
                 part = part + pltpu.roll(part, step, 1)
                 step //= 2
-            shear.append(part * scale)
+            more = extra if c == 0 else ahead(extra, width, 1)
+            more = jnp.concatenate([jnp.zeros((shape[0] - SUB, LANE), jnp.float32), more], axis=0)
+            shear.append((part + gain * fraction * more) * scale)
     return fresh, shear
 
 
-def side_kernel(layers, spans, bed_in, full, shear, strips, *rest):
+def everywhere(x):
+    step = 2 * EDGE
+    x = jnp.where(iota(x.shape, 1) < step, x, 0.0)
+    while step < LANE:
+        x = x + pltpu.roll(x, step, 1)
+        step *= 2
+    return x
+
+
+def side_kernel(layers, spans, bed_in, full, far, shear, strips, *rest):
     got = rest[:spans]
     rest = rest[spans:]
     own_message = rest[0]
@@ -347,18 +489,30 @@
     base = lax.axis_index("wall") * layers
     right_first = even("span")
     results = []
+    column = lax.rem(iota((tall * SUB, LANE), 1), 2 * EDGE)
+    fresh_sides = []
     for side in range(2):
+        first = right_first if side == 0 else jnp.logical_not(right_first)
+
+        def other(n):
+            return jnp.where(first, got[0][n], got[1][n] if spans > 1 else 0.0)
+
+        given = column >= EDGE if side == 0 else column < EDGE
+        back = EDGE if side == 0 else LANE - EDGE
+        both = [jnp.concatenate([other(2 * t + i) for t in range(tall)], axis=0) for i in range(2)]
+        turned = [jnp.where(given, pltpu.roll(b, back, 1), 0.0) for b in both]
+        theirs = [jnp.where(given, both[0], 0.0), turned[0], jnp.where(given, both[1], 0.0)]
+        theirs += [everywhere(turned[1]), everywhere(ahead(turned[1], 2 * EDGE, 1))]
         fields = []
         for n in range(5):
-            at = slice(n * tall, (n + 1) * tall)
-            own = full[side, at]
-            first = right_first if side == 0 else jnp.logical_not(right_first)
-            other = jnp.where(first, got[0][at], got[1][at] if spans > 1 else 0.0)
-            fields.append((own + other).reshape(tall * SUB, LANE))
-        fresh, edge_shear = column_strip(fields[:3], fields[3], fields[4], base, layers)
-        for c in range(3):
-            fresh_ref[side, c] = fresh[c]
+            own = full[side, n * tall : (n + 1) * tall].reshape(tall * SUB, LANE)
+            fields.append(own + theirs[n])
+        extra = far[side] + other(2 * tall)
+        fresh, edge_shear = column_strip(fields[:3], fields[3], fields[4], extra, base, layers)
+        fresh_sides.append(fresh)
         results.append(edge_shear)
+    for c in range(3):
+        fresh_ref[c] = jnp.where(column < EDGE, fresh_sides[0][c], fresh_sides[1][c])[:rows]
     lane = iota((SUB, LANE), 1)
     sub = iota((SUB, LANE), 0)
     lanes = cols // LANE
@@ -387,42 +541,22 @@
             out_ref[(c * tall + t) * (lanes + 1) + lanes] = beyond
     if bed_in:
         used = 2 * tall * (lanes + 1)
-        start = 5 * tall
+        start = 2 * tall + 1
         count = own_message.shape[0] - start
         for i in range(count):
             out_ref[used + i] = own_message[start + i]
             out_ref[used + count + i] = got[0][start + i]
 
 
-def merge_kernel(layers, new, strip_top, strip_bottom, fresh, far, lev, frac, out_ref):
-    rows, cols = lev.shape
-    tiles = rows // SUB
+def merge_kernel(layers, new, strip_top, strip_bottom, fresh, far, flat, final, out_ref, sems):
+    _, rows, cols = flat.shape
     lanes = cols // LANE
     wall = lax.axis_index("wall")
     lower = wall == 0
-    sub = iota((SUB, cols), 0)
-    lane = iota((rows, LANE), 1)
-    levels = lev[...].astype(jnp.float32)
-    fraction = frac[...]
-    for c in range(3):
-        right, left = fresh[0, c, :rows], fresh[1, c, :rows]
-
-        def layer_step(z, carry):
-            shift = 2 * EDGE * z
-            block = new[c, z]
-            first = jnp.where(sub < 2, strip_top[c, z], block[:SUB])
-            last = jnp.where(sub >= SUB - 2, strip_bottom[c, z], block[rows - SUB :])
-            block = jnp.concatenate([first, block[SUB : rows - SUB], last], axis=0)
-            pieces = [block[:, k * LANE : (k + 1) * LANE] for k in range(lanes)]
-            at_left = pltpu.roll(left, lax.rem(2 * LANE - EDGE - shift, LANE), 1)
-            at_right = pltpu.roll(right, lax.rem(2 * LANE - EDGE - shift, LANE), 1)
-            pieces[0] = jnp.where(lane < 2, at_left, pieces[0])
-            pieces[-1] = jnp.where(lane >= LANE - 2, at_right, pieces[-1])
-            for k in range(lanes):
-                out_ref[c, z, :, k * LANE : (k + 1) * LANE] = pieces[k]
-            return carry
-
-        lax.fori_loop(0, layers, layer_step, 0, unroll=4)
+    sub = iota((SUB, LANE), 0)
+    lane = iota((SUB, LANE), 1)
+    levels = flat[0]
+    fraction = flat[1]
     base = wall * layers
     near_from = jnp.where(lower, 0, 1)
     far_from = 1 - near_from
@@ -435,12 +569,36 @@
     near_gain = gain * opened_at(levels, fraction, (base + near_to).astype(jnp.float32))
     far_gain = gain * opened_at(levels, fraction, (base + far_to).astype(jnp.float32))
     near_w, far_w = far[2, near_from], far[2, far_from]
-    for c in range(3):
+    copies = []
+    for c in range(3):
+        for z in range(layers):
+            for t in range(rows // SUB):
+                at = slice(t * SUB, (t + 1) * SUB)
+                side = pltpu.roll(fresh[c, at], (LANE - EDGE - 2 * EDGE * z) % LANE, 1)
+                for k in range(lanes):
+                    cut = slice(k * LANE, (k + 1) * LANE)
+                    piece = new[c, z, at, cut]
+                    if t == 0:
+                        piece = jnp.where(sub < 2, strip_top[c, z, :, cut], piece)
+                    if t == rows // SUB - 1:
+                        piece = jnp.where(sub >= SUB - 2, strip_bottom[c, z, :, cut], piece)
+                    if k == 0:
+                        piece = jnp.where(lane < 2, side, piece)
+                    if k == lanes - 1:
+                        piece = jnp.where(lane >= LANE - 2, side, piece)
+                    out_ref[c, z, at, cut] = piece
         near_q = near_open * far[c, near_from]
         near_f = sign * (near_w * near_q)
         far_f = sign * (far_w * (far_open * far[c, far_from]))
         out_ref[c, near_to] = out_ref[c, near_to] + near_gain * (6.0 * near_q + 8.0 * near_f - far_f)
         out_ref[c, far_to] = out_ref[c, far_to] - far_gain * near_f
+        part = layers // 4
+        for i in range(4):
+            at = pl.ds(i * part, part)
+            copies.append(pltpu.make_async_copy(out_ref.at[c, at], final.at[c, at], sems.at[4 * c + i]))
+            copies[-1].start()
+    for copy in copies:
+        copy.wait()
 
 
 def bed_kernel(tall, lanes, bed_in, mine, theirs, *rest):
@@ -553,16 +711,15 @@
     walls = lax.axis_size("wall")
     assert walls == 2 and layers * 2 * EDGE == LANE
     bed_in = spans == 2 and bed_height.shape == (SUB, 2 * cols)
-    count = 3 * layers // 2 + 1 + (bed_height.shape[1] // cols if bed_in else 0)
+    count = 3 * layers // 4 + (2 if bed_in else 1)
     dma = pltpu.SemaphoreType.DMA
     sheet = (3, layers, SUB, cols)
-    send_a, send_b, send_z = call(
+    send_a, send_b, send_z, vel, flat, bed = call(
         functools.partial(pack_kernel, layers, bed_in),
-        [(count, SUB, cols), (count, SUB, cols), (3, 2, rows, cols)],
-        [velocity, levels, fraction, bed_height],
-        [pltpu.VMEM(sheet, jnp.float32), pltpu.VMEM(sheet, jnp.float32), dma((3,))],
-        any_inputs=(0,),
-        flops=1,
+        [(count, SUB, cols), (count, SUB, cols), (3, 2, rows, cols), velocity.shape, (2, rows, cols), bed_height.shape],
+        [pltpu.with_memory_space_constraint(x, pltpu.HBM) for x in (velocity, levels, fraction, bed_height)],
+        [pltpu.VMEM(levels.shape, jnp.int32), dma((6,))],
+        any_inputs=(0, 1, 2, 3),
         moved=1_000_000,
         limit=10,
     )
@@ -570,34 +727,35 @@
     got_a = lax.ppermute(send_a, "plane", plane_a)
     got_b = lax.ppermute(send_b, "plane", plane_b)
     got_z = lax.ppermute(send_z, "wall", pairings("wall")[0])
-    deep = (3, layers + 4, rows, cols)
+    deep = pltpu.VMEM((3, layers + 4, rows, cols), jnp.float32)
     new, shear, edge = call(
         functools.partial(inner_kernel, layers),
         [velocity.shape, (2, rows, cols), (2, 5, tiles, SUB, LANE)],
-        [velocity, levels, fraction],
-        [pltpu.VMEM(deep, jnp.float32), pltpu.VMEM(deep, jnp.float32)],
+        [vel, flat],
+        [deep, deep, pltpu.VMEM((3, layers * rows, 4 * cols), jnp.bfloat16), pltpu.VMEM((4 * cols, cols), jnp.bfloat16)]
+        + [pltpu.VMEM((3, layers * rows, cols), jnp.float32)],
         flops=20_000_000,
         moved=3_000_000,
     )
     span_lists = [p for p in pairings("span") if p]
-    message = (5 * tall + (4 * lanes if bed_in else 0), SUB, LANE)
+    message = (2 * tall + 1 + (4 * lanes if bed_in else 0), SUB, LANE)
     unpacked = call(
-        functools.partial(unpack_kernel, layers, count, bed_in),
-        [sheet, (2, SUB, cols), (2, 5 * tall, SUB, LANE)] + [message] * len(span_lists),
-        [got_a, got_b, edge, bed_height],
+        functools.partial(unpack_kernel, layers, bed_in),
+        [sheet, (4, SUB, cols), (2, 5 * tall, SUB, LANE), (2, SUB, LANE)] + [message] * len(span_lists),
+        [got_a, got_b, edge, bed, got_z],
+        any_inputs=(4,),
         moved=1_000_000,
         limit=10,
     )
-    halo, flat, full = unpacked[:3]
-    messages = unpacked[3:]
+    halo, beside, full, far = unpacked[:4]
+    messages = unpacked[4:]
     got = [lax.ppermute(m, "span", pairs) for m, pairs in zip(messages, span_lists)]
-    shallow = (3, layers + 4, SUB, cols)
+    shallow = pltpu.VMEM((3, layers + 4, SUB, cols), jnp.float32)
     new_top, new_bottom, strip_shear = call(
         functools.partial(strip_kernel, layers),
         [sheet, sheet, (2, 2, SUB, cols)],
-        [velocity, levels, fraction, halo, flat],
-        [pltpu.VMEM(sheet, jnp.float32)] * 2 + [pltpu.VMEM(shallow, jnp.float32)] * 2 + [dma((2,))],
-        any_inputs=(0,),
+        [vel, flat, halo, beside],
+        [shallow, shallow],
         flops=10_000_000,
         moved=2_000_000,
     )
@@ -605,8 +763,8 @@
     out_count = shear_count + (8 * lanes if bed_in else 0)
     fresh, mine = call(
         functools.partial(side_kernel, layers, len(got), bed_in),
-        [(2, 3, tall * SUB, LANE), (out_count, SUB, LANE)],
-        [full, shear, strip_shear] + got + [messages[0]],
+        [(3, rows, LANE), (out_count, SUB, LANE)],
+        [full, far, shear, strip_shear] + got + [messages[0]],
         moved=1_000_000,
         limit=10,
     )
@@ -614,7 +772,9 @@
     (velocity_next,) = call(
         functools.partial(merge_kernel, layers),
         [velocity.shape],
-        [new, new_top, new_bottom, fresh, got_z, levels, fraction],
+        [new, new_top, new_bottom, fresh, got_z, flat],
+        [pltpu.VMEM(velocity.shape, jnp.float32), dma((12,))],
+        any_outputs=(0,),
         flops=2_000_000,
         moved=4_000_000,
     )

time: 27.7 us -> 20.8 us (0.75)
  the two profiles are of different devices: /device:TPU:17 before, /device:TPU:11 now
where the time goes in v2:
time: 20.8 us; the launch traced here: 20.7 us
  Pallas kernels  11.5 us (55%)
  starting transfers between devices  7.39 us (36%)
  waiting for transfers between devices  1.07 us (5%)
  between operations  0.71 us (3%)
    pallas_call x7, Pallas kernels, call(): pl.pallas_call(kernel, out_shape=shapes, in_specs=specs, out_specs=[pl.Bl...  11.5 us
    ppermute x1, starting transfers between devices, body(): got_b = lax.ppermute(send_b, 'plane', plane_b)  4.32 us
    ppermute x1, starting transfers between devices, body(): theirs = lax.ppermute(mine, 'wall', pairings('wall')[0])  1.85 us
    ppermute x1, waiting for transfers between devices, body(): lax.ppermute(m, 'span', pairs)  1.06 us
    ppermute x1, starting transfers between devices, body(): got_z = lax.ppermute(send_z, 'wall', pairings('wall')[0])  0.74 us
  transfers between devices with their start and end apart: 5, of which 1 were waited for; matrix products, arithmetic and copies ran while one was open for 0% of the time, Pallas kernels for 37%

profile of v2, /device:TPU:11, one launch (start us, length us, event | category | flops | bytes accessed | tf_op | source)
XLA Modules:
  0.0 20.7 jit_solution(13316896614171718085)
XLA Ops:
  0.6 1.5 %shard_map.59 = (f32[14,8,256]{2,1,0:T(8,128)S(1)}, f32[14,8,256]{2,1,0:T(8,128)S(1)}, f32[3,2,32,256]{3,2,1,0:T(8,128)S(1)}, f32[3,16,32,256]{3,2,1,0:T(8,128)S...) custom-call(f32[3,16,32,256]{3,2,1,0:T(8,128)} %vel_in.1, s32[32,256]{1,0:T(8,128)} %lev_in.1, f32[32,256]{1,0:T(8,128)} %frac_in.1, ...), custom_call_target="tpu_custom_call" | custom-call | bytes 1000000 | tf_op jit(solution)/shard_map/pallas_call | solution.py:25
  2.2 0.7 %collective-permute-start.2 = (f32[3,2,32,256]{3,2,1,0:T(8,128)S(1)}, f32[3,2,32,256]{3,2,1,0:T(8,128)S(1)}, u32[]{:S(2)}, u32[]{:S(2)}) collective-permute-start(f32[3,2,32,256]{3,2,1,0:T(8,128)S(1)} %get-tuple-element.28), channel_id=1, source_target_pairs={{0,1},{1,0},{2,3},{3,2},{4,5},{5,4},{6,7},{7,6},{8,9},{9,8},{10,11... | collective-permute-start | bytes 589832 | tf_op jit(solution)/shard_map/ppermute | solution.py:729
  2.9 0.2 collective-permute-start
  3.1 4.3 %collective-permute-start.1 = (f32[14,8,256]{2,1,0:T(8,128)S(1)}, f32[14,8,256]{2,1,0:T(8,128)S(1)}, u32[]{:S(2)}, u32[]{:S(2)}) collective-permute-start(f32[14,8,256]{2,1,0:T(8,128)S(1)} %get-tuple-element.25), channel_id=1, source_target_pairs={{4,8},{8,4},{5,9},{9,5},{6,10},{10,6},{7,11},{11,7},{20,24},{24,20... | collective-permute-start | bytes 344072 | tf_op jit(solution)/shard_map/ppermute | solution.py:728
  7.4 4.3 %shard_map.60 = (f32[3,16,32,256]{3,2,1,0:T(8,128)S(1)}, f32[2,32,256]{2,1,0:T(8,128)S(1)}, f32[2,5,4,8,128]{4,3,2,1,0:T(8,128)S(1)}) custom-call(f32[3,16,32,256]{3,2,1,0:T(8,128)S(1)} %get-tuple-element.21.vel, f32[2,32,256]{2,1,0:T(8,128)S(1)} %get-tuple-element.22.flat), custom_call_target="tpu_custom_call" | custom-call | flops 20000000 | bytes 3000000 | tf_op jit(solution)/shard_map/pallas_call | solution.py:25
  11.7 0.0 collective-permute-done.got_a
  11.7 0.0 collective-permute-done.1.got_b
  11.7 0.0 collective-permute-done.2.got_z.far
  11.8 0.4 %shard_map.61 = (f32[3,16,8,256]{3,2,1,0:T(8,128)S(1)}, f32[4,8,256]{2,1,0:T(8,128)S(1)}, f32[2,25,8,128]{3,2,1,0:T(8,128)S(1)}, f32[2,8,128]{2,1,0:T(8,128)S(1)}, f32[19,8,128]{2,1,0:T(8,128)S(1)}) custom-call(f32[14,8,256]{2,1,0:T(8,128)S(1)} %collective-permute-done.got_a, f32[14,8,256]{2,1,0:T(8,128)S(1)} %collective-permute-done.1.got_b, ...), custom_call_target="tpu_custom_call" | custom-call | bytes 1000000 | tf_op jit(solution)/shard_map/pallas_call | solution.py:25
  12.2 0.3 %collective-permute-start.3 = (f32[19,8,128]{2,1,0:T(8,128)S(1)}, f32[19,8,128]{2,1,0:T(8,128)S(1)}, u32[]{:S(2)}, u32[]{:S(2)}) collective-permute-start(f32[19,8,128]{2,1,0:T(8,128)S(1)} %get-tuple-element.37.rest_1_), channel_id=1, source_target_pairs={{0,2},{2,0},{1,3},{3,1},{4,6},{6,4},{5,7},{7,5},{8,10},{10,8},{9,1... | collective-permute-start | bytes 233480 | tf_op jit(solution)/shard_map/ppermute | solution.py:752
  12.5 1.9 %shard_map.62 = (f32[3,16,8,256]{3,2,1,0:T(8,128)S(1)}, f32[3,16,8,256]{3,2,1,0:T(8,128)S(1)}, f32[2,2,8,256]{3,2,1,0:T(8,128)S(1)}) custom-call(f32[3,16,32,256]{3,2,1,0:T(8,128)S(1)} %get-tuple-element.21.vel, f32[2,32,256]{2,1,0:T(8,128)S(1)} %get-tuple-element.22.flat, f32[3,16,8,256]{3,2,1,0:T(8,128)S(1)} %get-tuple-element.29.halo, ...), custom_call_target="tpu_custom_call" | custom-call | flops 10000000 | bytes 2000000 | tf_op jit(solution)/shard_map/pallas_call | solution.py:25
  14.4 1.1 %collective-permute-done.3.rest_0_ = f32[19,8,128]{2,1,0:T(8,128)S(1)} collective-permute-done((f32[19,8,128]{2,1,0:T(8,128)S(1)}, f32[19,8,128]{2,1,0:T(8,128)S(1)}, u32[]{:S(2)}, u32[]{:S(2)}) %collective-permute-start.3) | collective-permute-done | bytes 77856 | tf_op jit(solution)/shard_map/ppermute | solution.py:752
  15.5 1.1 %shard_map.63 = (f32[3,32,128]{2,1,0:T(8,128)S(1)}, f32[46,8,128]{2,1,0:T(8,128)S(1)}) custom-call(f32[2,25,8,128]{3,2,1,0:T(8,128)S(1)} %get-tuple-element.33.full, f32[2,8,128]{2,1,0:T(8,128)S(1)} %get-tuple-element.34.far, f32[2,32,256]{2,1,0:T(8,128)S(1)} %get-tuple-element.35.shear, f32[2,2,8,256]{3,2,1,0:T(8,128)S(1)} %get-tuple-element.36.strips, ...), custom_call_target="tpu_custom_call" | custom-call | bytes 1000000 | tf_op jit(solution)/shard_map/pallas_call | solution.py:25
  16.6 1.8 %collective-permute-start.4 = (f32[46,8,128]{2,1,0:T(8,128)S(1)}, f32[46,8,128]{2,1,0:T(8,128)S(1)}, u32[]{:S(2)}, u32[]{:S(2)}) collective-permute-start(f32[46,8,128]{2,1,0:T(8,128)S(1)} %get-tuple-element.39.mine), channel_id=1, source_target_pairs={{0,1},{1,0},{2,3},{3,2},{4,5},{5,4},{6,7},{7,6},{8,9},{9,8},{10,11... | collective-permute-start | bytes 565256 | tf_op jit(solution)/shard_map/ppermute | solution.py:771
  18.4 1.4 %shard_map.64 = f32[3,16,32,256]{3,2,1,0:T(8,128)} custom-call(f32[3,16,32,256]{3,2,1,0:T(8,128)S(1)} %get-tuple-element.23.new, f32[3,16,8,256]{3,2,1,0:T(8,128)S(1)} %get-tuple-element.31.strip_top, f32[3,16,8,256]{3,2,1,0:T(8,128)S(1)} %get-tuple-element.32.strip_bottom, f32[3,32,128]{2,1,0:T(8,128)S(1)} %get-tuple-element.38.fresh, ...), custom_call_target="tpu_custom_call" | custom-call | flops 2000000 | bytes 4000000 | tf_op jit(solution)/shard_map/pallas_call | solution.py:25
  19.8 0.0 collective-permute-done.4.theirs
  19.8 0.9 %shard_map.65 = f32[32,256]{1,0:T(8,128)} custom-call(f32[46,8,128]{2,1,0:T(8,128)S(1)} %get-tuple-element.39.mine, f32[46,8,128]{2,1,0:T(8,128)S(1)} %collective-permute-done.4.theirs), custom_call_target="tpu_custom_call" | custom-call | bytes 1000000 | tf_op jit(solution)/shard_map/pallas_call | solution.py:25
Async XLA Ops:
  2.2 9.6 %collective-permute-start.2 = (f32[3,2,32,256]{3,2,1,0:T(8,128)S(1)}, f32[3,2,32,256]{3,2,1,0:T(8,128)S(1)}, u32[]{:S(2)}, u32[]{:S(2)}) collective-permute-start(f32[3,2,32,256]{3,2,1,0:T(8,128)S(1)} %get-tuple-element.28), channel_id=1, source_target_pairs={{0,1},{1,0},{2,3},{3,2},{4,5},{5,4},{6,7},{7,6},{8,9},{9,8},{10,11... | collective-permute-start | bytes 589832 | tf_op jit(solution)/shard_map/ppermute | solution.py:729
  2.9 8.8 %collective-permute-start = (f32[14,8,256]{2,1,0:T(8,128)S(1)}, f32[14,8,256]{2,1,0:T(8,128)S(1)}, u32[]{:S(2)}, u32[]{:S(2)}) collective-permute-start(f32[14,8,256]{2,1,0:T(8,128)S(1)} %get-tuple-element.24), channel_id=1, source_target_pairs={{0,4},{4,0},{8,12},{12,8},{1,5},{5,1},{9,13},{13,9},{2,6},{6,2},{1... | collective-permute-start | bytes 344072 | tf_op jit(solution)/shard_map/ppermute | solution.py:727
  3.1 8.7 %collective-permute-start.1 = (f32[14,8,256]{2,1,0:T(8,128)S(1)}, f32[14,8,256]{2,1,0:T(8,128)S(1)}, u32[]{:S(2)}, u32[]{:S(2)}) collective-permute-start(f32[14,8,256]{2,1,0:T(8,128)S(1)} %get-tuple-element.25), channel_id=1, source_target_pairs={{4,8},{8,4},{5,9},{9,5},{6,10},{10,6},{7,11},{11,7},{20,24},{24,20... | collective-permute-start | bytes 344072 | tf_op jit(solution)/shard_map/ppermute | solution.py:728
  12.2 3.3 %collective-permute-start.3 = (f32[19,8,128]{2,1,0:T(8,128)S(1)}, f32[19,8,128]{2,1,0:T(8,128)S(1)}, u32[]{:S(2)}, u32[]{:S(2)}) collective-permute-start(f32[19,8,128]{2,1,0:T(8,128)S(1)} %get-tuple-element.37.rest_1_), channel_id=1, source_target_pairs={{0,2},{2,0},{1,3},{3,1},{4,6},{6,4},{5,7},{7,5},{8,10},{10,8},{9,1... | collective-permute-start | bytes 233480 | tf_op jit(solution)/shard_map/ppermute | solution.py:752
  16.6 3.2 %collective-permute-start.4 = (f32[46,8,128]{2,1,0:T(8,128)S(1)}, f32[46,8,128]{2,1,0:T(8,128)S(1)}, u32[]{:S(2)}, u32[]{:S(2)}) collective-permute-start(f32[46,8,128]{2,1,0:T(8,128)S(1)} %get-tuple-element.39.mine), channel_id=1, source_target_pairs={{0,1},{1,0},{2,3},{3,2},{4,5},{5,4},{6,7},{7,6},{8,9},{9,8},{10,11... | collective-permute-start | bytes 565256 | tf_op jit(solution)/shard_map/ppermute | solution.py:771

commit v3 on v2

--- a/solution.py
+++ b/solution.py
@@ -153,7 +153,7 @@
     return found
 
 
-def pack_kernel(layers, bed_in, vel_in, lev_in, frac_in, bed_from, a_ref, b_ref, z_ref, vel, flat, bed, lev, sems):
+def pack_kernel(layers, bed_in, vel_in, lev_in, frac_in, bed_from, a_ref, b_ref, vel, flat, bed, lev, sems):
     _, rows, cols = flat.shape
     wall = lax.axis_index("wall")
     base = wall * layers
@@ -204,10 +204,6 @@
     high_far = beyond_terms(top, high_lev, high_frac, base, layers, False)
     put(count, stack([low_lev, low_frac] + low_far, 2), stack([high_lev, high_frac] + high_far, 0))
     pieces[2].wait()
-    start = jnp.where(wall == 0, layers - 2, 0)
-    for c in range(3):
-        for z in range(2):
-            z_ref[c, z] = vel[c, start + z]
 
 
 def gather_edges(read, layers, rows, cols, put):
@@ -240,7 +236,10 @@
     return right, left
 
 
-def inner_kernel(layers, vel, flat, new_ref, shear_ref, edge_ref, q_ref, f_ref, split_ref, band_ref, x_ref):
+def inner_kernel(layers, comps, vel, flat, *refs):
+    with_shear = 0 in comps
+    new_ref = refs[0]
+    q_ref, f_ref, split_ref, band_ref, x_ref = refs[-5:]
     _, rows, cols = flat.shape
     base = lax.axis_index("wall") * layers
     lanes = cols // LANE
@@ -251,10 +250,10 @@
     for i, band in enumerate((flux_band, flux_band, field_band, field_band)):
         band_ref[i * cols : (i + 1) * cols] = band.astype(jnp.bfloat16)
     blank = jnp.zeros((rows, cols), jnp.float32)
-    for c in range(3):
+    for n in range(len(comps)):
         for z in (0, 1, layers + 2, layers + 3):
-            q_ref[c, z] = blank
-            f_ref[c, z] = blank
+            q_ref[n, z] = blank
+            f_ref[n, z] = blank
 
     def halves(x):
         high = x.astype(jnp.bfloat16)
@@ -267,18 +266,18 @@
             cut = slice(k * LANE, (k + 1) * LANE)
             opened = opened_at(flat[0, :, cut], flat[1, :, cut], layer)
             vel_x, vel_z = vel[0, z, :, cut], vel[2, z, :, cut]
-            for c in range(3):
+            for n, c in enumerate(comps):
                 q = opened * vel[c, z, :, cut]
-                q_ref[c, z + 2, :, cut] = q
-                f_ref[c, z + 2, :, cut] = vel_z * q
+                q_ref[n, z + 2, :, cut] = q
+                f_ref[n, z + 2, :, cut] = vel_z * q
                 parts = halves(vel_x * q) + halves(q)
                 for i, part in enumerate(parts):
-                    split_ref[c, at, i * cols + k * LANE : i * cols + (k + 1) * LANE] = part
+                    split_ref[n, at, i * cols + k * LANE : i * cols + (k + 1) * LANE] = part
         return carry
 
     lax.fori_loop(0, layers, prepare, 0)
-    for c in range(3):
-        x_ref[c] = jnp.dot(split_ref[c], band_ref[...], preferred_element_type=jnp.float32)
+    for n in range(len(comps)):
+        x_ref[n] = jnp.dot(split_ref[n], band_ref[...], preferred_element_type=jnp.float32)
 
     def outside(z, c, cut):
         total = jnp.zeros((rows, LANE), jnp.float32)
@@ -292,9 +291,11 @@
         return jnp.where(hit, gain * flat[1, :, cut] * total, 0.0)
 
     sums = []
-    for k in range(lanes):
-        for c in range(2):
-            sums.append(sum(outside(z, c, slice(k * LANE, (k + 1) * LANE)) for z in (-2, -1, layers, layers + 1)))
+    if with_shear:
+        for k in range(lanes):
+            cut = slice(k * LANE, (k + 1) * LANE)
+            for c in range(2):
+                sums.append(sum(outside(z, c, cut) for z in (-2, -1, layers, layers + 1)))
 
     def update(z, sums):
         sums = list(sums)
@@ -306,20 +307,22 @@
             weight = gain * opened_at(level, flat[1, :, cut], layer)
             hit = level == layer
             vel_y = vel[1, z, :, cut]
-            for c in range(3):
-                q = q_ref[c, z + 2, :, cut]
-                flux = f_ref[1, z + 2, :, cut] if c == 2 else vel_y * q
-                total = x_ref[c, at, cut] + sweep(flux, 6.0 * q, 0)
-                near = f_ref[c, z + 3, :, cut] - f_ref[c, z + 1, :, cut]
-                both = q_ref[c, z + 3, :, cut] + q_ref[c, z + 1, :, cut]
-                total = total + (6.0 * both - 8.0 * near + (f_ref[c, z + 4, :, cut] - f_ref[c, z, :, cut]))
+            for n, c in enumerate(comps):
+                q = q_ref[n, z + 2, :, cut]
+                total = x_ref[n, at, cut] + sweep(vel_y * q, 6.0 * q, 0)
+                near = f_ref[n, z + 3, :, cut] - f_ref[n, z + 1, :, cut]
+                both = q_ref[n, z + 3, :, cut] + q_ref[n, z + 1, :, cut]
+                total = total + (6.0 * both - 8.0 * near + (f_ref[n, z + 4, :, cut] - f_ref[n, z, :, cut]))
                 fresh = vel[c, z, :, cut] + weight * total
-                new_ref[c, z, :, cut] = fresh
-                if c < 2:
+                new_ref[n, z, :, cut] = fresh
+                if with_shear:
                     sums[2 * k + c] = sums[2 * k + c] + jnp.where(hit, fresh, 0.0)
         return tuple(sums)
 
     sums = lax.fori_loop(0, layers, update, tuple(sums))
+    if not with_shear:
+        return
+    shear_ref, edge_ref = refs[1:3]
     for k in range(lanes):
         cut = slice(k * LANE, (k + 1) * LANE)
         scale = 1.0 / (0.5 + flat[1, :, cut])
@@ -336,7 +339,7 @@
         put(1, 3 + n, left)
 
 
-def unpack_kernel(layers, bed_in, got_a, got_b, edge, bed, got_z, halo_ref, beside_ref, full_ref, far_ref, *messages):
+def unpack_kernel(layers, bed_in, got_a, got_b, edge, bed, halo_ref, beside_ref, full_ref, far_ref, *messages):
     cols = halo_ref.shape[3]
     tiles = edge.shape[2]
     tall = tiles + 1
@@ -406,7 +409,7 @@
                 messages[0][used + parts + i * per + j] = tile[:, j * LANE : (j + 1) * LANE]
 
 
-def strip_kernel(layers, vel, flat, halo, beside, top_ref, bottom_ref, shear_ref, q_ref, f_ref):
+def strip_kernel(layers, vel, flat, halo, beside, top_ref, bottom_ref, shear_ref, z_ref, q_ref, f_ref):
     _, rows, cols = flat.shape
     base = lax.axis_index("wall") * layers
     sub = iota((SUB, cols), 0)
@@ -428,6 +431,10 @@
         sums = brick(read, levels, fraction, base, layers, q_ref, f_ref, write, extra, 4)
         shear_ref[side, 0] = sums[0]
         shear_ref[side, 1] = sums[1]
+    start = jnp.where(lax.axis_index("wall") == 0, layers - 2, 0)
+    for c in range(3):
+        for z in range(2):
+            z_ref[c, z] = vel[c, start + z]
 
 
 def column_strip(vel, levels, fraction, extra, base, layers):
@@ -482,7 +489,7 @@
     got = rest[:spans]
     rest = rest[spans:]
     own_message = rest[0]
-    fresh_ref, out_ref = rest[1:]
+    fresh_ref, out_ref = rest[2:]
     _, rows, cols = shear.shape
     tiles = rows // SUB
     tall = tiles + 1
@@ -548,7 +555,7 @@
             out_ref[used + count + i] = got[0][start + i]
 
 
-def merge_kernel(layers, new, strip_top, strip_bottom, fresh, far, flat, final, out_ref, sems):
+def merge_kernel(layers, new, new_z, strip_top, strip_bottom, fresh, far, flat, final, out_ref, sems):
     _, rows, cols = flat.shape
     lanes = cols // LANE
     wall = lax.axis_index("wall")
@@ -577,7 +584,7 @@
                 side = pltpu.roll(fresh[c, at], (LANE - EDGE - 2 * EDGE * z) % LANE, 1)
                 for k in range(lanes):
                     cut = slice(k * LANE, (k + 1) * LANE)
-                    piece = new[c, z, at, cut]
+                    piece = new[c, z, at, cut] if c < 2 else new_z[0, z, at, cut]
                     if t == 0:
                         piece = jnp.where(sub < 2, strip_top[c, z, :, cut], piece)
                     if t == rows // SUB - 1:
@@ -714,9 +721,9 @@
     count = 3 * layers // 4 + (2 if bed_in else 1)
     dma = pltpu.SemaphoreType.DMA
     sheet = (3, layers, SUB, cols)
-    send_a, send_b, send_z, vel, flat, bed = call(
+    send_a, send_b, vel, flat, bed = call(
         functools.partial(pack_kernel, layers, bed_in),
-        [(count, SUB, cols), (count, SUB, cols), (3, 2, rows, cols), velocity.shape, (2, rows, cols), bed_height.shape],
+        [(count, SUB, cols), (count, SUB, cols), velocity.shape, (2, rows, cols), bed_height.shape],
         [pltpu.with_memory_space_constraint(x, pltpu.HBM) for x in (velocity, levels, fraction, bed_height)],
         [pltpu.VMEM(levels.shape, jnp.int32), dma((6,))],
         any_inputs=(0, 1, 2, 3),
@@ -724,26 +731,29 @@
         limit=10,
     )
     plane_a, plane_b = pairings("plane")
+    got_b = lax.ppermute(send_b, "plane", plane_b)
     got_a = lax.ppermute(send_a, "plane", plane_a)
-    got_b = lax.ppermute(send_b, "plane", plane_b)
-    got_z = lax.ppermute(send_z, "wall", pairings("wall")[0])
-    deep = pltpu.VMEM((3, layers + 4, rows, cols), jnp.float32)
-    new, shear, edge = call(
-        functools.partial(inner_kernel, layers),
-        [velocity.shape, (2, rows, cols), (2, 5, tiles, SUB, LANE)],
-        [vel, flat],
-        [deep, deep, pltpu.VMEM((3, layers * rows, 4 * cols), jnp.bfloat16), pltpu.VMEM((4 * cols, cols), jnp.bfloat16)]
-        + [pltpu.VMEM((3, layers * rows, cols), jnp.float32)],
-        flops=20_000_000,
-        moved=3_000_000,
-    )
+
+    def inner(comps, more, flops):
+        count = len(comps)
+        deep = pltpu.VMEM((count, layers + 4, rows, cols), jnp.float32)
+        return call(
+            functools.partial(inner_kernel, layers, comps),
+            [(count, layers, rows, cols)] + more,
+            [vel, flat],
+            [deep, deep, pltpu.VMEM((count, layers * rows, 4 * cols), jnp.bfloat16)]
+            + [pltpu.VMEM((4 * cols, cols), jnp.bfloat16), pltpu.VMEM((count, layers * rows, cols), jnp.float32)],
+            flops=flops,
+            moved=3_000_000,
+        )
+
+    new, shear, edge = inner((0, 1), [(2, rows, cols), (2, 5, tiles, SUB, LANE)], 20_000_000)
     span_lists = [p for p in pairings("span") if p]
     message = (2 * tall + 1 + (4 * lanes if bed_in else 0), SUB, LANE)
     unpacked = call(
         functools.partial(unpack_kernel, layers, bed_in),
         [sheet, (4, SUB, cols), (2, 5 * tall, SUB, LANE), (2, SUB, LANE)] + [message] * len(span_lists),
-        [got_a, got_b, edge, bed, got_z],
-        any_inputs=(4,),
+        [got_a, got_b, edge, bed],
         moved=1_000_000,
         limit=10,
     )
@@ -751,20 +761,23 @@
     messages = unpacked[4:]
     got = [lax.ppermute(m, "span", pairs) for m, pairs in zip(messages, span_lists)]
     shallow = pltpu.VMEM((3, layers + 4, SUB, cols), jnp.float32)
-    new_top, new_bottom, strip_shear = call(
+    new_top, new_bottom, strip_shear, send_z = call(
         functools.partial(strip_kernel, layers),
-        [sheet, sheet, (2, 2, SUB, cols)],
+        [sheet, sheet, (2, 2, SUB, cols), (3, 2, rows, cols)],
         [vel, flat, halo, beside],
         [shallow, shallow],
         flops=10_000_000,
         moved=2_000_000,
     )
+    got_z = lax.ppermute(send_z, "wall", pairings("wall")[0])
     shear_count = 2 * tall * (lanes + 1)
     out_count = shear_count + (8 * lanes if bed_in else 0)
+    (new_z,) = inner((2,), [], 10_000_000)
     fresh, mine = call(
         functools.partial(side_kernel, layers, len(got), bed_in),
         [(3, rows, LANE), (out_count, SUB, LANE)],
-        [full, far, shear, strip_shear] + got + [messages[0]],
+        [full, far, shear, strip_shear] + got + [messages[0], new_z],
+        any_inputs=(5 + len(got),),
         moved=1_000_000,
         limit=10,
     )
@@ -772,7 +785,7 @@
     (velocity_next,) = call(
         functools.partial(merge_kernel, layers),
         [velocity.shape],
-        [new, new_top, new_bottom, fresh, got_z, flat],
+        [new, new_z, new_top, new_bottom, fresh, got_z, flat],
         [pltpu.VMEM(velocity.shape, jnp.float32), dma((12,))],
         any_outputs=(0,),
         flops=2_000_000,

time: 20.8 us -> 20.5 us (0.986)
  the two profiles are of different devices: /device:TPU:11 before, /device:TPU:17 now
where the time goes in v3:
time: 20.5 us; the launch traced here: 20.1 us
  Pallas kernels  12.1 us (59%)
  starting transfers between devices  7.06 us (34%)
  between operations  0.71 us (3%)
  waiting for transfers between devices  0.26 us (1%)
    pallas_call x8, Pallas kernels, call(): pl.pallas_call(kernel, out_shape=shapes, in_specs=specs, out_specs=[pl.Bl...  12.1 us
    ppermute x1, starting transfers between devices, body(): got_z = lax.ppermute(send_z, 'wall', pairings('wall')[0])  2.45 us
    ppermute x1, starting transfers between devices, body(): got_b = lax.ppermute(send_b, 'plane', plane_b)  1.91 us
    ppermute x1, starting transfers between devices, body(): got_a = lax.ppermute(send_a, 'plane', plane_a)  1.36 us
    ppermute x1, starting transfers between devices, body(): lax.ppermute(m, 'span', pairs)  1.26 us
  transfers between devices with their start and end apart: 5, of which 1 were waited for; matrix products, arithmetic and copies ran while one was open for 0% of the time, Pallas kernels for 46%

profile of v3, /device:TPU:17, one launch (start us, length us, event | category | flops | bytes accessed | tf_op | source)
XLA Modules:
  0.0 20.1 jit_solution(10190790558756143681)
XLA Ops:
  0.6 1.5 %shard_map.59 = (f32[14,8,256]{2,1,0:T(8,128)S(1)}, f32[14,8,256]{2,1,0:T(8,128)S(1)}, f32[3,16,32,256]{3,2,1,0:T(8,128)S(1)}, f32[2,32,256]{2,1,0:T(8,128)S(1)}, f32[8,512]{1,0:T(8,128)S(1)}) custom-call(f32[3,16,32,256]{3,2,1,0:T(8,128)} %vel_in.1, s32[32,256]{1,0:T(8,128)} %lev_in.1, f32[32,256]{1,0:T(8,128)} %frac_in.1, f32[8,512]{1,0:T(8,128)} %bed_from.1), custom_call_target="tpu_custom_call" | custom-call | bytes 1000000 | tf_op jit(solution)/shard_map/pallas_call | solution.py:25
  2.1 1.4 %collective-permute-start = (f32[14,8,256]{2,1,0:T(8,128)S(1)}, f32[14,8,256]{2,1,0:T(8,128)S(1)}, u32[]{:S(2)}, u32[]{:S(2)}) collective-permute-start(f32[14,8,256]{2,1,0:T(8,128)S(1)} %get-tuple-element.24), channel_id=1, source_target_pairs={{0,4},{4,0},{8,12},{12,8},{1,5},{5,1},{9,13},{13,9},{2,6},{6,2},{1... | collective-permute-start | bytes 344072 | tf_op jit(solution)/shard_map/ppermute | solution.py:735
  3.5 1.9 %collective-permute-start.1 = (f32[14,8,256]{2,1,0:T(8,128)S(1)}, f32[14,8,256]{2,1,0:T(8,128)S(1)}, u32[]{:S(2)}, u32[]{:S(2)}) collective-permute-start(f32[14,8,256]{2,1,0:T(8,128)S(1)} %get-tuple-element.25), channel_id=1, source_target_pairs={{4,8},{8,4},{5,9},{9,5},{6,10},{10,6},{7,11},{11,7},{20,24},{24,20... | collective-permute-start | bytes 344072 | tf_op jit(solution)/shard_map/ppermute | solution.py:734
  5.4 3.3 %shard_map.60 = (f32[2,16,32,256]{3,2,1,0:T(8,128)S(1)}, f32[2,32,256]{2,1,0:T(8,128)S(1)}, f32[2,5,4,8,128]{4,3,2,1,0:T(8,128)S(1)}) custom-call(f32[3,16,32,256]{3,2,1,0:T(8,128)S(1)} %get-tuple-element.21.vel, f32[2,32,256]{2,1,0:T(8,128)S(1)} %get-tuple-element.22.flat), custom_call_target="tpu_custom_call" | custom-call | flops 20000000 | bytes 3000000 | tf_op jit(solution)/shard_map/pallas_call | solution.py:25
  8.8 0.0 collective-permute-done.got_a
  8.8 0.3 %collective-permute-done.1.got_b = f32[14,8,256]{2,1,0:T(8,128)S(1)} collective-permute-done((f32[14,8,256]{2,1,0:T(8,128)S(1)}, f32[14,8,256]{2,1,0:T(8,128)S(1)}, u32[]{:S(2)}, u32[]{:S(2)}) %collective-permute-start.1) | collective-permute-done | bytes 114720 | tf_op jit(solution)/shard_map/ppermute | solution.py:734
  9.0 0.4 %shard_map.62 = (f32[3,16,8,256]{3,2,1,0:T(8,128)S(1)}, f32[4,8,256]{2,1,0:T(8,128)S(1)}, f32[2,25,8,128]{3,2,1,0:T(8,128)S(1)}, f32[2,8,128]{2,1,0:T(8,128)S(1)}, f32[19,8,128]{2,1,0:T(8,128)S(1)}) custom-call(f32[14,8,256]{2,1,0:T(8,128)S(1)} %collective-permute-done.got_a, f32[14,8,256]{2,1,0:T(8,128)S(1)} %collective-permute-done.1.got_b, ...), custom_call_target="tpu_custom_call" | custom-call | bytes 1000000 | tf_op jit(solution)/shard_map/pallas_call | solution.py:25
  9.4 1.3 %collective-permute-start.2 = (f32[19,8,128]{2,1,0:T(8,128)S(1)}, f32[19,8,128]{2,1,0:T(8,128)S(1)}, u32[]{:S(2)}, u32[]{:S(2)}) collective-permute-start(f32[19,8,128]{2,1,0:T(8,128)S(1)} %get-tuple-element.36.rest_1_), channel_id=1, source_target_pairs={{0,2},{2,0},{1,3},{3,1},{4,6},{6,4},{5,7},{7,5},{8,10},{10,8},{9,1... | collective-permute-start | bytes 233480 | tf_op jit(solution)/shard_map/ppermute | solution.py:762
  10.7 1.9 %shard_map.63 = (f32[3,16,8,256]{3,2,1,0:T(8,128)S(1)}, f32[3,16,8,256]{3,2,1,0:T(8,128)S(1)}, f32[2,2,8,256]{3,2,1,0:T(8,128)S(1)}, f32[3,2,32,256]{3,2,1,0:T(8,128)S(1)}) custom-call(f32[3,16,32,256]{3,2,1,0:T(8,128)S(1)} %get-tuple-element.21.vel, f32[2,32,256]{2,1,0:T(8,128)S(1)} %get-tuple-element.22.flat, ...), custom_call_target="tpu_custom_call" | custom-call | flops 10000000 | bytes 2000000 | tf_op jit(solution)/shard_map/pallas_call | solution.py:25
  12.7 2.5 %collective-permute-start.3 = (f32[3,2,32,256]{3,2,1,0:T(8,128)S(1)}, f32[3,2,32,256]{3,2,1,0:T(8,128)S(1)}, u32[]{:S(2)}, u32[]{:S(2)}) collective-permute-start(f32[3,2,32,256]{3,2,1,0:T(8,128)S(1)} %get-tuple-element.38), channel_id=1, source_target_pairs={{0,1},{1,0},{2,3},{3,2},{4,5},{5,4},{6,7},{7,6},{8,9},{9,8},{10,11... | collective-permute-start | bytes 589832 | tf_op jit(solution)/shard_map/ppermute | solution.py:772
  15.1 1.5 %shard_map.61.rest_2_.new_z = f32[1,16,32,256]{3,2,1,0:T(8,128)S(1)} custom-call(f32[3,16,32,256]{3,2,1,0:T(8,128)S(1)} %get-tuple-element.21.vel, f32[2,32,256]{2,1,0:T(8,128)S(1)} %get-tuple-element.22.flat), custom_call_target="tpu_custom_call" | custom-call | flops 10000000 | bytes 3000000 | tf_op jit(solution)/shard_map/pallas_call | solution.py:25
  16.6 0.0 collective-permute-done.2.rest_0_
  16.7 1.1 %shard_map.64 = (f32[3,32,128]{2,1,0:T(8,128)S(1)}, f32[46,8,128]{2,1,0:T(8,128)S(1)}) custom-call(f32[2,25,8,128]{3,2,1,0:T(8,128)S(1)} %get-tuple-element.32.full, f32[2,8,128]{2,1,0:T(8,128)S(1)} %get-tuple-element.33.far, f32[2,32,256]{2,1,0:T(8,128)S(1)} %get-tuple-element.34.shear, f32[2,2,8,256]{3,2,1,0:T(8,128)S(1)} %get-tuple-element.35.strips, ...), custom_call_target="tpu_custom_call" | custom-call | bytes 1000000 | tf_op jit(solution)/shard_map/pallas_call | solution.py:25
  17.8 0.1 collective-permute-start.4
  17.8 0.0 collective-permute-done.3.far
  17.9 1.4 %shard_map.65 = f32[3,16,32,256]{3,2,1,0:T(8,128)} custom-call(f32[2,16,32,256]{3,2,1,0:T(8,128)S(1)} %get-tuple-element.23.new, f32[1,16,32,256]{3,2,1,0:T(8,128)S(1)} %shard_map.61.rest_2_.new_z, f32[3,16,8,256]{3,2,1,0:T(8,128)S(1)} %get-tuple-element.30.strip_top, f32[3,16,8,256]{3,2,1,0:T(8,128)S(1)} %get-tuple-element.31.strip_bottom, ...), custom_call_target="tpu_custom_call" | custom-call | flops 2000000 | bytes 4000000 | tf_op jit(solution)/shard_map/pallas_call | solution.py:25
  19.3 0.0 collective-permute-done.4.theirs
  19.3 0.9 %shard_map.66 = f32[32,256]{1,0:T(8,128)} custom-call(f32[46,8,128]{2,1,0:T(8,128)S(1)} %get-tuple-element.39.mine, f32[46,8,128]{2,1,0:T(8,128)S(1)} %collective-permute-done.4.theirs), custom_call_target="tpu_custom_call" | custom-call | bytes 1000000 | tf_op jit(solution)/shard_map/pallas_call | solution.py:25
Async XLA Ops:
  2.1 6.6 %collective-permute-start = (f32[14,8,256]{2,1,0:T(8,128)S(1)}, f32[14,8,256]{2,1,0:T(8,128)S(1)}, u32[]{:S(2)}, u32[]{:S(2)}) collective-permute-start(f32[14,8,256]{2,1,0:T(8,128)S(1)} %get-tuple-element.24), channel_id=1, source_target_pairs={{0,4},{4,0},{8,12},{12,8},{1,5},{5,1},{9,13},{13,9},{2,6},{6,2},{1... | collective-permute-start | bytes 344072 | tf_op jit(solution)/shard_map/ppermute | solution.py:735
  3.5 5.5 %collective-permute-start.1 = (f32[14,8,256]{2,1,0:T(8,128)S(1)}, f32[14,8,256]{2,1,0:T(8,128)S(1)}, u32[]{:S(2)}, u32[]{:S(2)}) collective-permute-start(f32[14,8,256]{2,1,0:T(8,128)S(1)} %get-tuple-element.25), channel_id=1, source_target_pairs={{4,8},{8,4},{5,9},{9,5},{6,10},{10,6},{7,11},{11,7},{20,24},{24,20... | collective-permute-start | bytes 344072 | tf_op jit(solution)/shard_map/ppermute | solution.py:734
  9.4 7.2 %collective-permute-start.2 = (f32[19,8,128]{2,1,0:T(8,128)S(1)}, f32[19,8,128]{2,1,0:T(8,128)S(1)}, u32[]{:S(2)}, u32[]{:S(2)}) collective-permute-start(f32[19,8,128]{2,1,0:T(8,128)S(1)} %get-tuple-element.36.rest_1_), channel_id=1, source_target_pairs={{0,2},{2,0},{1,3},{3,1},{4,6},{6,4},{5,7},{7,5},{8,10},{10,8},{9,1... | collective-permute-start | bytes 233480 | tf_op jit(solution)/shard_map/ppermute | solution.py:762
  12.7 5.2 %collective-permute-start.3 = (f32[3,2,32,256]{3,2,1,0:T(8,128)S(1)}, f32[3,2,32,256]{3,2,1,0:T(8,128)S(1)}, u32[]{:S(2)}, u32[]{:S(2)}) collective-permute-start(f32[3,2,32,256]{3,2,1,0:T(8,128)S(1)} %get-tuple-element.38), channel_id=1, source_target_pairs={{0,1},{1,0},{2,3},{3,2},{4,5},{5,4},{6,7},{7,6},{8,9},{9,8},{10,11... | collective-permute-start | bytes 589832 | tf_op jit(solution)/shard_map/ppermute | solution.py:772
  17.8 1.5 %collective-permute-start.4 = (f32[46,8,128]{2,1,0:T(8,128)S(1)}, f32[46,8,128]{2,1,0:T(8,128)S(1)}, u32[]{:S(2)}, u32[]{:S(2)}) collective-permute-start(f32[46,8,128]{2,1,0:T(8,128)S(1)} %get-tuple-element.39.mine), channel_id=1, source_target_pairs={{0,1},{1,0},{2,3},{3,2},{4,5},{5,4},{6,7},{7,6},{8,9},{9,8},{10,11... | collective-permute-start | bytes 565256 | tf_op jit(solution)/shard_map/ppermute | solution.py:784

commit v4 on v3

--- a/solution.py
+++ b/solution.py
@@ -21,7 +21,7 @@
 
 def call(kernel, outs, ins, scratch=(), any_inputs=(), any_outputs=(), flops=0, moved=0, limit=20, aliases=None):
     specs = [pl.BlockSpec(memory_space=pl.ANY if i in any_inputs else VMEM) for i in range(len(ins))]
-    shapes = [jax.ShapeDtypeStruct(s, jnp.float32) for s in outs]
+    shapes = [s if isinstance(s, jax.ShapeDtypeStruct) else jax.ShapeDtypeStruct(s, jnp.float32) for s in outs]
     return pl.pallas_call(
         kernel,
         out_shape=shapes,
@@ -53,76 +53,6 @@
 
 def even(axis):
     return lax.rem(lax.axis_index(axis), 2) == 0
-
-
-def brick(read, level, fraction, base, layers, q_ref, f_ref, write, extra, unroll):
-    rows, cols = level.shape
-    blank = jnp.zeros((rows, cols), jnp.float32)
-    for c in range(3):
-        for z in (0, 1, layers + 2, layers + 3):
-            q_ref[c, z] = blank
-            f_ref[c, z] = blank
-    cut_gain = fraction * gain
-    scale = 1.0 / (0.5 + fraction)
-
-    def prepare(z, carry):
-        vel = [read(c, z) for c in range(3)]
-        opened = opened_at(level, fraction, (base + z).astype(jnp.float32))
-        for c in range(3):
-            q = opened * vel[c]
-            q_ref[c, z + 2] = q
-            f_ref[c, z + 2] = vel[2] * q
-        return carry
-
-    lax.fori_loop(0, layers, prepare, 0, unroll=4)
-
-    def vertical(c, z):
-        near = f_ref[c, z + 3] - f_ref[c, z + 1]
-        both = q_ref[c, z + 3] + q_ref[c, z + 1]
-        return 6.0 * both - 8.0 * near + (f_ref[c, z + 4] - f_ref[c, z])
-
-    def outside(z):
-        hit = level == (base + z).astype(jnp.float32)
-        found = []
-        for c in range(2):
-            total = blank
-            for offset, weight_f, weight_q in ((1, -8.0, 6.0), (-1, 8.0, 6.0), (2, 1.0, 0.0), (-2, -1.0, 0.0)):
-                at = z + offset
-                if 0 <= at < layers:
-                    total = total + weight_f * f_ref[c, at + 2]
-                    if weight_q:
-                        total = total + weight_q * q_ref[c, at + 2]
-            found.append(jnp.where(hit, cut_gain * total, 0.0))
-        return found
-
-    sums = extra
-    for z in (-2, -1, layers, layers + 1):
-        found = outside(z)
-        sums = [s + f for s, f in zip(sums, found)]
-
-    def update(z, sums):
-        vel = [read(c, z) for c in range(3)]
-        q = [q_ref[c, z + 2] for c in range(3)]
-        layer = (base + z).astype(jnp.float32)
-        opened = opened_at(level, fraction, layer)
-        hit = level == layer
-        weight = gain * opened
-        cross = vel[0] * q[1]
-        along_x = (vel[0] * q[0], cross, f_ref[0, z + 2])
-        along_y = (cross, vel[1] * q[1], f_ref[1, z + 2])
-        sums = list(sums)
-        for c in range(3):
-            b = 6.0 * q[c]
-            total = vertical(c, z) - 6.0 * b
-            total = total + sweep(along_x[c], b, 1) + sweep(along_y[c], b, 0)
-            fresh = vel[c] + weight * total
-            write(c, z, fresh)
-            if c < 2:
-                sums[c] = sums[c] + jnp.where(hit, fresh, 0.0)
-        return tuple(sums)
-
-    sums = lax.fori_loop(0, layers, update, tuple(sums), unroll=unroll)
-    return [s * scale for s in sums]
 
 
 def beyond_terms(tile, level, fraction, base, layers, forward):
@@ -153,7 +83,7 @@
     return found
 
 
-def pack_kernel(layers, bed_in, vel_in, lev_in, frac_in, bed_from, a_ref, b_ref, vel, flat, bed, lev, sems):
+def pack_kernel(layers, bed_in, vel_in, lev_in, frac_in, bed_from, a_ref, b_ref, vel, flat, bed, band_ref, lev, sems):
     _, rows, cols = flat.shape
     wall = lax.axis_index("wall")
     base = wall * layers
@@ -168,6 +98,12 @@
         pieces.append(pltpu.make_async_copy(vel_in.at[:, :, at, :], vel.at[:, :, at, :], sems.at[3 + i]))
     for copy in small + pieces:
         copy.start()
+    tall = iota((cols, cols), 0) - iota((cols, cols), 1)
+    flux_band = jnp.where(tall == 1, -8.0, jnp.where(tall == -1, 8.0, 0.0))
+    flux_band = flux_band + jnp.where(tall == 2, 1.0, jnp.where(tall == -2, -1.0, 0.0))
+    field_band = jnp.where(jnp.abs(tall) == 1, 6.0, jnp.where(tall == 0, -36.0, 0.0))
+    for i, band in enumerate((flux_band, flux_band, field_band, field_band)):
+        band_ref[i * cols : (i + 1) * cols] = band.astype(jnp.bfloat16)
     sub = iota((SUB, cols), 0)
     pair = sub // 2
     is_even = even("plane")
@@ -236,19 +172,13 @@
     return right, left
 
 
-def inner_kernel(layers, comps, vel, flat, *refs):
+def inner_kernel(layers, comps, vel, flat, band_ref, *refs):
     with_shear = 0 in comps
     new_ref = refs[0]
-    q_ref, f_ref, split_ref, band_ref, x_ref = refs[-5:]
+    q_ref, f_ref, split_ref, x_ref = refs[-4:]
     _, rows, cols = flat.shape
     base = lax.axis_index("wall") * layers
     lanes = cols // LANE
-    tall = iota((cols, cols), 0) - iota((cols, cols), 1)
-    flux_band = jnp.where(tall == 1, -8.0, jnp.where(tall == -1, 8.0, 0.0))
-    flux_band = flux_band + jnp.where(tall == 2, 1.0, jnp.where(tall == -2, -1.0, 0.0))
-    field_band = jnp.where(jnp.abs(tall) == 1, 6.0, jnp.where(tall == 0, -36.0, 0.0))
-    for i, band in enumerate((flux_band, flux_band, field_band, field_band)):
-        band_ref[i * cols : (i + 1) * cols] = band.astype(jnp.bfloat16)
     blank = jnp.zeros((rows, cols), jnp.float32)
     for n in range(len(comps)):
         for z in (0, 1, layers + 2, layers + 3):
@@ -278,6 +208,18 @@
     lax.fori_loop(0, layers, prepare, 0)
     for n in range(len(comps)):
         x_ref[n] = jnp.dot(split_ref[n], band_ref[...], preferred_element_type=jnp.float32)
+
+    if with_shear:
+        shear_ref, edge_ref = refs[1:3]
+
+        def put(side, n, value):
+            edge_ref[side, n] = value.reshape(rows // SUB, SUB, LANE)
+
+        gather_edges(lambda c, z: vel[c, z], layers, rows, cols, put)
+        for n in range(2):
+            right, left = repeat_edges(flat[n], rows, cols)
+            put(0, 3 + n, right)
+            put(1, 3 + n, left)
 
     def outside(z, c, cut):
         total = jnp.zeros((rows, LANE), jnp.float32)
@@ -322,21 +264,11 @@
     sums = lax.fori_loop(0, layers, update, tuple(sums))
     if not with_shear:
         return
-    shear_ref, edge_ref = refs[1:3]
     for k in range(lanes):
         cut = slice(k * LANE, (k + 1) * LANE)
         scale = 1.0 / (0.5 + flat[1, :, cut])
         for c in range(2):
             shear_ref[c, :, cut] = sums[2 * k + c] * scale
-
-    def put(side, n, value):
-        edge_ref[side, n] = value.reshape(rows // SUB, SUB, LANE)
-
-    gather_edges(lambda c, z: vel[c, z], layers, rows, cols, put)
-    for n in range(2):
-        right, left = repeat_edges(flat[n], rows, cols)
-        put(0, 3 + n, right)
-        put(1, 3 + n, left)
 
 
 def unpack_kernel(layers, bed_in, got_a, got_b, edge, bed, halo_ref, beside_ref, full_ref, far_ref, *messages):
@@ -409,28 +341,87 @@
                 messages[0][used + parts + i * per + j] = tile[:, j * LANE : (j + 1) * LANE]
 
 
-def strip_kernel(layers, vel, flat, halo, beside, top_ref, bottom_ref, shear_ref, z_ref, q_ref, f_ref):
+def strip_kernel(layers, vel, flat, halo, beside, new_z, fix_ref, shear_ref, z_ref, q_ref, f_ref):
     _, rows, cols = flat.shape
     base = lax.axis_index("wall") * layers
-    sub = iota((SUB, cols), 0)
-    for side, new in ((0, top_ref), (1, bottom_ref)):
-        inside = sub < EDGE if side == 0 else sub >= EDGE
-        outer = sub >= SUB - 2 if side == 0 else sub < 2
-        first = 0 if side == 0 else rows - SUB
-        at = slice(first, first + SUB)
-        levels = jnp.where(inside, flat[0, at], beside[0])
-        fraction = jnp.where(inside, flat[1, at], beside[1])
-        extra = [jnp.where(outer, gain * fraction * beside[2 + c], 0.0) for c in range(2)]
-
-        def read(c, z):
-            return jnp.where(inside, vel[c, z, at], halo[c, z])
-
-        def write(c, z, value):
-            new[c, z] = value
-
-        sums = brick(read, levels, fraction, base, layers, q_ref, f_ref, write, extra, 4)
-        shear_ref[side, 0] = sums[0]
-        shear_ref[side, 1] = sums[1]
+    shape = (SUB, cols)
+    sub = iota(shape, 0)
+    low, high = sub < 2, sub >= SUB - 2
+    blank = jnp.zeros(shape, jnp.float32)
+
+    def faces(first, last):
+        return jnp.where(low, first, jnp.where(high, last, 0.0))
+
+    level, fraction = beside[0], beside[1]
+    own_level = faces(flat[0, :SUB], flat[0, rows - SUB :])
+    own_fraction = faces(flat[1, :SUB], flat[1, rows - SUB :])
+    for c in range(2):
+        for z in (0, 1, layers + 2, layers + 3):
+            q_ref[c, z] = blank
+            f_ref[c, z] = blank
+
+    def prepare(z, carry):
+        opened = opened_at(level, fraction, (base + z).astype(jnp.float32))
+        for c in range(2):
+            q = opened * halo[c, z]
+            q_ref[c, z + 2] = q
+            f_ref[c, z + 2] = halo[2, z] * q
+        return carry
+
+    lax.fori_loop(0, layers, prepare, 0, unroll=4)
+    sums = []
+    for c in range(2):
+        found = gain * fraction * beside[2 + c]
+        for z in (-2, -1, layers, layers + 1):
+            total = blank
+            for offset, weight in ((1, -8.0), (-1, 8.0), (2, 1.0), (-2, -1.0)):
+                at = z + offset
+                if 0 <= at < layers:
+                    total = total + weight * f_ref[c, at + 2]
+                    if abs(offset) == 1:
+                        total = total + 6.0 * q_ref[c, at + 2]
+            found = found + jnp.where(level == (base + z).astype(jnp.float32), gain * fraction * total, 0.0)
+        sums.append(found)
+
+    def update(z, sums):
+        sums = list(sums)
+        layer = (base + z).astype(jnp.float32)
+        opened = opened_at(level, fraction, layer)
+        own_opened = opened_at(own_level, own_fraction, layer)
+        weight, own_weight = gain * opened, gain * own_opened
+        hit, own_hit = level == layer, own_level == layer
+        own_y = faces(vel[1, z, :SUB], vel[1, z, rows - SUB :])
+        for c in range(3):
+            q = q_ref[c, z + 2] if c < 2 else opened * halo[2, z]
+            flux = halo[1, z] * q
+            own = own_y if c == 1 else faces(vel[c, z, :SUB], vel[c, z, rows - SUB :])
+            own_q = own_opened * own
+            own_flux = own_y * own_q
+            a, b = 8.0 * flux, 6.0 * q
+            own_a, own_b = 8.0 * own_flux, 6.0 * own_q
+            less_a, less_b, less = a - own_a, b - own_b, flux - own_flux
+            after = jnp.where(sub == 0, less_b - less_a, 0.0) + ahead(jnp.where(low, less, 0.0), 1, 0)
+            before = jnp.where(sub == SUB - 1, less_b + less_a, 0.0) - ahead(jnp.where(high, less, 0.0), -1, 0)
+            fix = own_weight * faces(ahead(before, -1, 0), ahead(after, 1, 0))
+            fix_ref[c, z] = fix
+            if c == 2:
+                continue
+            after = jnp.where(sub == 0, own_b - own_a, b - a) + ahead(jnp.where(low, own_flux, 0.0), 1, 0)
+            before = jnp.where(sub == SUB - 1, own_b + own_a, b + a) - ahead(jnp.where(high, own_flux, 0.0), -1, 0)
+            total = ahead(after, 1, 0) + ahead(before, -1, 0) + sweep(halo[0, z] * q, b, 1) - 6.0 * b
+            near = f_ref[c, z + 3] - f_ref[c, z + 1]
+            both = q_ref[c, z + 3] + q_ref[c, z + 1]
+            total = total + (6.0 * both - 8.0 * near + (f_ref[c, z + 4] - f_ref[c, z]))
+            sums[c] = sums[c] + jnp.where(hit, halo[c, z] + weight * total, 0.0)
+            sums[2 + c] = sums[2 + c] + jnp.where(own_hit, fix, 0.0)
+        return tuple(sums)
+
+    sums = lax.fori_loop(0, layers, update, (sums[0], sums[1], blank, blank), unroll=4)
+    scale = 1.0 / (0.5 + fraction)
+    own_scale = 1.0 / (0.5 + own_fraction)
+    for c in range(2):
+        shear_ref[0, c] = jnp.where(low | high, sums[c] * scale, 0.0)
+        shear_ref[1, c] = sums[2 + c] * own_scale
     start = jnp.where(lax.axis_index("wall") == 0, layers - 2, 0)
     for c in range(3):
         for z in range(2):
@@ -530,14 +521,13 @@
             for k in range(lanes):
                 cut = slice(k * LANE, (k + 1) * LANE)
                 if t == tiles:
-                    piece = jnp.where(sub < EDGE, strips[1, c, :, cut], strips[0, c, :, cut])
-                    piece = jnp.where((sub < 2) | (sub >= SUB - 2), piece, 0.0)
+                    piece = strips[0, c, :, cut]
                 else:
                     piece = shear[c, at, cut]
                     if t == 0:
-                        piece = jnp.where(sub < 2, strips[0, c, :, cut], piece)
+                        piece = piece + jnp.where(sub < 2, strips[1, c, :, cut], 0.0)
                     if t == tiles - 1:
-                        piece = jnp.where(sub >= SUB - 2, strips[1, c, :, cut], piece)
+                        piece = piece + jnp.where(sub >= SUB - 2, strips[1, c, :, cut], 0.0)
                 if k == 0:
                     piece = jnp.where(lane < 2, pltpu.roll(left[at], LANE - EDGE, 1), piece)
                 if k == lanes - 1:
@@ -555,7 +545,7 @@
             out_ref[used + count + i] = got[0][start + i]
 
 
-def merge_kernel(layers, new, new_z, strip_top, strip_bottom, fresh, far, flat, final, out_ref, sems):
+def merge_kernel(layers, new, new_z, fix, fresh, far, flat, final, out_ref, sems):
     _, rows, cols = flat.shape
     lanes = cols // LANE
     wall = lax.axis_index("wall")
@@ -586,9 +576,9 @@
                     cut = slice(k * LANE, (k + 1) * LANE)
                     piece = new[c, z, at, cut] if c < 2 else new_z[0, z, at, cut]
                     if t == 0:
-                        piece = jnp.where(sub < 2, strip_top[c, z, :, cut], piece)
+                        piece = piece + jnp.where(sub < 2, fix[c, z, :, cut], 0.0)
                     if t == rows // SUB - 1:
-                        piece = jnp.where(sub >= SUB - 2, strip_bottom[c, z, :, cut], piece)
+                        piece = piece + jnp.where(sub >= SUB - 2, fix[c, z, :, cut], 0.0)
                     if k == 0:
                         piece = jnp.where(lane < 2, side, piece)
                     if k == lanes - 1:
@@ -721,9 +711,10 @@
     count = 3 * layers // 4 + (2 if bed_in else 1)
     dma = pltpu.SemaphoreType.DMA
     sheet = (3, layers, SUB, cols)
-    send_a, send_b, vel, flat, bed = call(
+    send_a, send_b, vel, flat, bed, band = call(
         functools.partial(pack_kernel, layers, bed_in),
-        [(count, SUB, cols), (count, SUB, cols), velocity.shape, (2, rows, cols), bed_height.shape],
+        [(count, SUB, cols), (count, SUB, cols), velocity.shape, (2, rows, cols), bed_height.shape]
+        + [jax.ShapeDtypeStruct((4 * cols, cols), jnp.bfloat16)],
         [pltpu.with_memory_space_constraint(x, pltpu.HBM) for x in (velocity, levels, fraction, bed_height)],
         [pltpu.VMEM(levels.shape, jnp.int32), dma((6,))],
         any_inputs=(0, 1, 2, 3),
@@ -740,9 +731,9 @@
         return call(
             functools.partial(inner_kernel, layers, comps),
             [(count, layers, rows, cols)] + more,
-            [vel, flat],
+            [vel, flat, band],
             [deep, deep, pltpu.VMEM((count, layers * rows, 4 * cols), jnp.bfloat16)]
-            + [pltpu.VMEM((4 * cols, cols), jnp.bfloat16), pltpu.VMEM((count, layers * rows, cols), jnp.float32)],
+            + [pltpu.VMEM((count, layers * rows, cols), jnp.float32)],
             flops=flops,
             moved=3_000_000,
         )
@@ -760,19 +751,20 @@
     halo, beside, full, far = unpacked[:4]
     messages = unpacked[4:]
     got = [lax.ppermute(m, "span", pairs) for m, pairs in zip(messages, span_lists)]
-    shallow = pltpu.VMEM((3, layers + 4, SUB, cols), jnp.float32)
-    new_top, new_bottom, strip_shear, send_z = call(
+    shallow = pltpu.VMEM((2, layers + 4, SUB, cols), jnp.float32)
+    (new_z,) = inner((2,), [], 10_000_000)
+    fix, strip_shear, send_z = call(
         functools.partial(strip_kernel, layers),
-        [sheet, sheet, (2, 2, SUB, cols), (3, 2, rows, cols)],
-        [vel, flat, halo, beside],
+        [sheet, (2, 2, SUB, cols), (3, 2, rows, cols)],
+        [vel, flat, halo, beside, new_z],
         [shallow, shallow],
+        any_inputs=(4,),
         flops=10_000_000,
         moved=2_000_000,
     )
     got_z = lax.ppermute(send_z, "wall", pairings("wall")[0])
     shear_count = 2 * tall * (lanes + 1)
     out_count = shear_count + (8 * lanes if bed_in else 0)
-    (new_z,) = inner((2,), [], 10_000_000)
     fresh, mine = call(
         functools.partial(side_kernel, layers, len(got), bed_in),
         [(3, rows, LANE), (out_count, SUB, LANE)],
@@ -785,7 +777,7 @@
     (velocity_next,) = call(
         functools.partial(merge_kernel, layers),
         [velocity.shape],
-        [new, new_z, new_top, new_bottom, fresh, got_z, flat],
+        [new, new_z, fix, fresh, got_z, flat],
         [pltpu.VMEM(velocity.shape, jnp.float32), dma((12,))],
         any_outputs=(0,),
         flops=2_000_000,

time: 20.5 us -> 19.6 us (0.956); the launches traced: 20.1 us -> 19.4 us
  Pallas kernels: 12.1 us -> 10.4 us
  waiting for transfers between devices: 0.26 us -> 0.98 us
  starting transfers between devices: 7.06 us -> 7.38 us
    pallas_call x8, Pallas kernels: 12.1 us -> 10.4 us  [call(): pl.pallas_call(kernel, out_shape=shapes, in_specs=specs, out_specs=[pl.Bl...]
    ppermute x1, waiting for transfers between devices: 0.25 us -> 0.97 us  [body(): got_b = lax.ppermute(send_b, 'plane', plane_b)]
    ppermute x1, starting transfers between devices: 0.09 us -> 0.41 us  [body(): theirs = lax.ppermute(mine, 'wall', pairings('wall')[0])]
  transfers between devices with their start and end apart: 5 -> 5, of which waited for: 1 -> 1; matrix products, arithmetic and copies ran while one was open for 0% -> 0% of each run, Pallas kernels for 46% -> 39%
where the time goes in v4:
time: 19.6 us; the launch traced here: 19.4 us
  Pallas kernels  10.4 us (53%)
  starting transfers between devices  7.38 us (38%)
  waiting for transfers between devices  0.98 us (5%)
  between operations  0.7 us (4%)
    pallas_call x8, Pallas kernels, call(): pl.pallas_call(kernel, out_shape=shapes, in_specs=specs, out_specs=[pl.Bl...  10.4 us
    ppermute x1, starting transfers between devices, body(): got_z = lax.ppermute(send_z, 'wall', pairings('wall')[0])  2.45 us
    ppermute x1, starting transfers between devices, body(): got_b = lax.ppermute(send_b, 'plane', plane_b)  1.91 us
    ppermute x1, starting transfers between devices, body(): got_a = lax.ppermute(send_a, 'plane', plane_a)  1.36 us
    ppermute x1, starting transfers between devices, body(): lax.ppermute(m, 'span', pairs)  1.26 us
    ppermute x1, waiting for transfers between devices, body(): got_b = lax.ppermute(send_b, 'plane', plane_b)  0.97 us
    ppermute x1, starting transfers between devices, body(): theirs = lax.ppermute(mine, 'wall', pairings('wall')[0])  0.41 us
  transfers between devices with their start and end apart: 5, of which 1 were waited for; matrix products, arithmetic and copies ran while one was open for 0% of the time, Pallas kernels for 39%

profile of v4, /device:TPU:17, one launch (start us, length us, event | category | flops | bytes accessed | tf_op | source)
XLA Modules:
  0.0 19.4 jit_solution(5592986492147142448)
XLA Ops:
  0.6 1.5 %shard_map.59 = (f32[14,8,256]{2,1,0:T(8,128)S(1)}, f32[14,8,256]{2,1,0:T(8,128)S(1)}, f32[3,16,32,256]{3,2,1,0:T(8,128)S(1)}, f32[2,32,256]{2,1,0:T(8,128)S(1)}...) custom-call(f32[3,16,32,256]{3,2,1,0:T(8,128)} %vel_in.1, s32[32,256]{1,0:T(8,128)} %lev_in.1, f32[32,256]{1,0:T(8,128)} %frac_in.1, ...), custom_call_target="tpu_custom_call" | custom-call | bytes 1000000 | tf_op jit(solution)/shard_map/pallas_call | solution.py:25
  2.1 1.4 %collective-permute-start = (f32[14,8,256]{2,1,0:T(8,128)S(1)}, f32[14,8,256]{2,1,0:T(8,128)S(1)}, u32[]{:S(2)}, u32[]{:S(2)}) collective-permute-start(f32[14,8,256]{2,1,0:T(8,128)S(1)} %get-tuple-element.25), channel_id=1, source_target_pairs={{0,4},{4,0},{8,12},{12,8},{1,5},{5,1},{9,13},{13,9},{2,6},{6,2},{1... | collective-permute-start | bytes 344072 | tf_op jit(solution)/shard_map/ppermute | solution.py:726
  3.5 1.9 %collective-permute-start.1 = (f32[14,8,256]{2,1,0:T(8,128)S(1)}, f32[14,8,256]{2,1,0:T(8,128)S(1)}, u32[]{:S(2)}, u32[]{:S(2)}) collective-permute-start(f32[14,8,256]{2,1,0:T(8,128)S(1)} %get-tuple-element.26), channel_id=1, source_target_pairs={{4,8},{8,4},{5,9},{9,5},{6,10},{10,6},{7,11},{11,7},{20,24},{24,20... | collective-permute-start | bytes 344072 | tf_op jit(solution)/shard_map/ppermute | solution.py:725
  5.4 2.6 %shard_map.60 = (f32[2,16,32,256]{3,2,1,0:T(8,128)S(1)}, f32[2,32,256]{2,1,0:T(8,128)S(1)}, f32[2,5,4,8,128]{4,3,2,1,0:T(8,128)S(1)}) custom-call(f32[3,16,32,256]{3,2,1,0:T(8,128)S(1)} %get-tuple-element.21.vel, f32[2,32,256]{2,1,0:T(8,128)S(1)} %get-tuple-element.22.flat, bf16[1024,256]{1,0:T(8,128)(2,1)S(1)} %get-tuple-element.23.band_ref), custom_call_target="tpu_custom_call" | custom-call | flops 20000000 | bytes 3000000 | tf_op jit(solution)/shard_map/pallas_call | solution.py:25
  8.1 0.0 collective-permute-done.got_a
  8.1 1.0 %collective-permute-done.1.got_b = f32[14,8,256]{2,1,0:T(8,128)S(1)} collective-permute-done((f32[14,8,256]{2,1,0:T(8,128)S(1)}, f32[14,8,256]{2,1,0:T(8,128)S(1)}, u32[]{:S(2)}, u32[]{:S(2)}) %collective-permute-start.1) | collective-permute-done | bytes 114720 | tf_op jit(solution)/shard_map/ppermute | solution.py:725
  9.0 0.4 %shard_map.62 = (f32[3,16,8,256]{3,2,1,0:T(8,128)S(1)}, f32[4,8,256]{2,1,0:T(8,128)S(1)}, f32[2,25,8,128]{3,2,1,0:T(8,128)S(1)}, f32[2,8,128]{2,1,0:T(8,128)S(1)}, f32[19,8,128]{2,1,0:T(8,128)S(1)}) custom-call(f32[14,8,256]{2,1,0:T(8,128)S(1)} %collective-permute-done.got_a, f32[14,8,256]{2,1,0:T(8,128)S(1)} %collective-permute-done.1.got_b, ...), custom_call_target="tpu_custom_call" | custom-call | bytes 1000000 | tf_op jit(solution)/shard_map/pallas_call | solution.py:25
  9.4 1.3 %collective-permute-start.2 = (f32[19,8,128]{2,1,0:T(8,128)S(1)}, f32[19,8,128]{2,1,0:T(8,128)S(1)}, u32[]{:S(2)}, u32[]{:S(2)}) collective-permute-start(f32[19,8,128]{2,1,0:T(8,128)S(1)} %get-tuple-element.36.rest_1_), channel_id=1, source_target_pairs={{0,2},{2,0},{1,3},{3,1},{4,6},{6,4},{5,7},{7,5},{8,10},{10,8},{9,1... | collective-permute-start | bytes 233480 | tf_op jit(solution)/shard_map/ppermute | solution.py:753
  10.7 1.5 %shard_map.61.new_z.rest_2_ = f32[1,16,32,256]{3,2,1,0:T(8,128)S(1)} custom-call(f32[3,16,32,256]{3,2,1,0:T(8,128)S(1)} %get-tuple-element.21.vel, f32[2,32,256]{2,1,0:T(8,128)S(1)} %get-tuple-element.22.flat, bf16[1024,256]{1,0:T(8,128)(2,1)S(1)} %get-tuple-element.23.band_ref), custom_call_target="tpu_custom_call" | custom-call | flops 10000000 | bytes 3000000 | tf_op jit(solution)/shard_map/pallas_call | solution.py:25
  12.2 1.0 %shard_map.63 = (f32[3,16,8,256]{3,2,1,0:T(8,128)S(1)}, f32[2,2,8,256]{3,2,1,0:T(8,128)S(1)}, f32[3,2,32,256]{3,2,1,0:T(8,128)S(1)}) custom-call(f32[3,16,32,256]{3,2,1,0:T(8,128)S(1)} %get-tuple-element.21.vel, f32[2,32,256]{2,1,0:T(8,128)S(1)} %get-tuple-element.22.flat, f32[3,16,8,256]{3,2,1,0:T(8,128)S(1)} %get-tuple-element.29.halo, ...), custom_call_target="tpu_custom_call" | custom-call | flops 10000000 | bytes 2000000 | tf_op jit(solution)/shard_map/pallas_call | solution.py:25
  13.2 2.5 %collective-permute-start.3 = (f32[3,2,32,256]{3,2,1,0:T(8,128)S(1)}, f32[3,2,32,256]{3,2,1,0:T(8,128)S(1)}, u32[]{:S(2)}, u32[]{:S(2)}) collective-permute-start(f32[3,2,32,256]{3,2,1,0:T(8,128)S(1)} %get-tuple-element.38), channel_id=1, source_target_pairs={{0,1},{1,0},{2,3},{3,2},{4,5},{5,4},{6,7},{7,6},{8,9},{9,8},{10,11... | collective-permute-start | bytes 589832 | tf_op jit(solution)/shard_map/ppermute | solution.py:765
  15.6 0.0 collective-permute-done.2.rest_0_
  15.7 1.1 %shard_map.64 = (f32[3,32,128]{2,1,0:T(8,128)S(1)}, f32[46,8,128]{2,1,0:T(8,128)S(1)}) custom-call(f32[2,25,8,128]{3,2,1,0:T(8,128)S(1)} %get-tuple-element.32.full, f32[2,8,128]{2,1,0:T(8,128)S(1)} %get-tuple-element.33.far, f32[2,32,256]{2,1,0:T(8,128)S(1)} %get-tuple-element.34.shear, f32[2,2,8,256]{3,2,1,0:T(8,128)S(1)} %get-tuple-element.35.strips, ...), custom_call_target="tpu_custom_call" | custom-call | bytes 1000000 | tf_op jit(solution)/shard_map/pallas_call | solution.py:25
  16.8 0.4 %collective-permute-start.4 = (f32[46,8,128]{2,1,0:T(8,128)S(1)}, f32[46,8,128]{2,1,0:T(8,128)S(1)}, u32[]{:S(2)}, u32[]{:S(2)}) collective-permute-start(f32[46,8,128]{2,1,0:T(8,128)S(1)} %get-tuple-element.39.mine), channel_id=1, source_target_pairs={{0,1},{1,0},{2,3},{3,2},{4,5},{5,4},{6,7},{7,6},{8,9},{9,8},{10,11... | collective-permute-start | bytes 565256 | tf_op jit(solution)/shard_map/ppermute | solution.py:776
  17.2 0.0 collective-permute-done.3.far
  17.2 1.4 %shard_map.65 = f32[3,16,32,256]{3,2,1,0:T(8,128)} custom-call(f32[2,16,32,256]{3,2,1,0:T(8,128)S(1)} %get-tuple-element.24.new, f32[1,16,32,256]{3,2,1,0:T(8,128)S(1)} %shard_map.61.new_z.rest_2_, f32[3,16,8,256]{3,2,1,0:T(8,128)S(1)} %get-tuple-element.31.fix, f32[3,32,128]{2,1,0:T(8,128)S(1)} %get-tuple-element.37.fresh, ...), custom_call_target="tpu_custom_call" | custom-call | flops 2000000 | bytes 4000000 | tf_op jit(solution)/shard_map/pallas_call | solution.py:25
  18.6 0.0 collective-permute-done.4.theirs
  18.6 0.9 %shard_map.66 = f32[32,256]{1,0:T(8,128)} custom-call(f32[46,8,128]{2,1,0:T(8,128)S(1)} %get-tuple-element.39.mine, f32[46,8,128]{2,1,0:T(8,128)S(1)} %collective-permute-done.4.theirs), custom_call_target="tpu_custom_call" | custom-call | bytes 1000000 | tf_op jit(solution)/shard_map/pallas_call | solution.py:25
Async XLA Ops:
  2.1 5.9 %collective-permute-start = (f32[14,8,256]{2,1,0:T(8,128)S(1)}, f32[14,8,256]{2,1,0:T(8,128)S(1)}, u32[]{:S(2)}, u32[]{:S(2)}) collective-permute-start(f32[14,8,256]{2,1,0:T(8,128)S(1)} %get-tuple-element.25), channel_id=1, source_target_pairs={{0,4},{4,0},{8,12},{12,8},{1,5},{5,1},{9,13},{13,9},{2,6},{6,2},{1... | collective-permute-start | bytes 344072 | tf_op jit(solution)/shard_map/ppermute | solution.py:726
  3.5 5.5 %collective-permute-start.1 = (f32[14,8,256]{2,1,0:T(8,128)S(1)}, f32[14,8,256]{2,1,0:T(8,128)S(1)}, u32[]{:S(2)}, u32[]{:S(2)}) collective-permute-start(f32[14,8,256]{2,1,0:T(8,128)S(1)} %get-tuple-element.26), channel_id=1, source_target_pairs={{4,8},{8,4},{5,9},{9,5},{6,10},{10,6},{7,11},{11,7},{20,24},{24,20... | collective-permute-start | bytes 344072 | tf_op jit(solution)/shard_map/ppermute | solution.py:725
  9.4 6.2 %collective-permute-start.2 = (f32[19,8,128]{2,1,0:T(8,128)S(1)}, f32[19,8,128]{2,1,0:T(8,128)S(1)}, u32[]{:S(2)}, u32[]{:S(2)}) collective-permute-start(f32[19,8,128]{2,1,0:T(8,128)S(1)} %get-tuple-element.36.rest_1_), channel_id=1, source_target_pairs={{0,2},{2,0},{1,3},{3,1},{4,6},{6,4},{5,7},{7,5},{8,10},{10,8},{9,1... | collective-permute-start | bytes 233480 | tf_op jit(solution)/shard_map/ppermute | solution.py:753
  13.2 4.0 %collective-permute-start.3 = (f32[3,2,32,256]{3,2,1,0:T(8,128)S(1)}, f32[3,2,32,256]{3,2,1,0:T(8,128)S(1)}, u32[]{:S(2)}, u32[]{:S(2)}) collective-permute-start(f32[3,2,32,256]{3,2,1,0:T(8,128)S(1)} %get-tuple-element.38), channel_id=1, source_target_pairs={{0,1},{1,0},{2,3},{3,2},{4,5},{5,4},{6,7},{7,6},{8,9},{9,8},{10,11... | collective-permute-start | bytes 589832 | tf_op jit(solution)/shard_map/ppermute | solution.py:765
  16.8 1.8 %collective-permute-start.4 = (f32[46,8,128]{2,1,0:T(8,128)S(1)}, f32[46,8,128]{2,1,0:T(8,128)S(1)}, u32[]{:S(2)}, u32[]{:S(2)}) collective-permute-start(f32[46,8,128]{2,1,0:T(8,128)S(1)} %get-tuple-element.39.mine), channel_id=1, source_target_pairs={{0,1},{1,0},{2,3},{3,2},{4,5},{5,4},{6,7},{7,6},{8,9},{9,8},{10,11... | collective-permute-start | bytes 565256 | tf_op jit(solution)/shard_map/ppermute | solution.py:776

commit v5 on v4

--- a/solution.py
+++ b/solution.py
@@ -278,9 +278,13 @@
     sub = iota((SUB, cols), 0)
     is_even = even("plane")
 
+    plane = lax.axis_index("plane")
+    has_after, has_before = plane < lax.axis_size("plane") - 1, plane > 0
+
     def sides(n):
         one, two = got_a[n], got_b[n]
-        return jnp.where(is_even, one, two), jnp.where(is_even, two, one)
+        after, before = jnp.where(is_even, one, two), jnp.where(is_even, two, one)
+        return jnp.where(has_after, after, 0.0), jnp.where(has_before, before, 0.0)
 
     def spread(n, fields):
         low, high = sides(n)
@@ -685,6 +689,20 @@
     return lists
 
 
+def everyone(axis, lists):
+    walls = lax.axis_size("wall")
+    full = []
+    for pairs in lists:
+        target = dict(pairs)
+        found = []
+        for i in range(lax.axis_size(axis)):
+            for w in range(walls):
+                to = target[i] * walls + w if i in target else i * walls + walls - 1 - w
+                found.append((i * walls + w, to))
+        full.append(found)
+    return full
+
+
 def bed_around(bed_height, rows, cols):
     spans = lax.axis_size("span")
     whole = lax.all_gather(bed_height, ("span", "wall"), axis=0, tiled=True)
@@ -721,9 +739,9 @@
         moved=1_000_000,
         limit=10,
     )
-    plane_a, plane_b = pairings("plane")
-    got_b = lax.ppermute(send_b, "plane", plane_b)
-    got_a = lax.ppermute(send_a, "plane", plane_a)
+    plane_a, plane_b = everyone("plane", pairings("plane"))
+    got_b = lax.ppermute(send_b, ("plane", "wall"), plane_b)
+    got_a = lax.ppermute(send_a, ("plane", "wall"), plane_a)
 
     def inner(comps, more, flops):
         count = len(comps)

time: 19.6 us -> 17.7 us (0.903)
  starting transfers between devices: 7.38 us -> 5.25 us
  waiting for transfers between devices: 0.98 us -> 1.25 us
    ppermute x2, starting transfers between devices: 3.27 us -> 1.36 us  [the longest x1 1.36 us: body(): got_a = lax.ppermute(send_a, ('plane', 'wall'), plane_a)]
    ppermute x2, waiting for transfers between devices: 0.97 us -> 1.24 us  [the longest x1 1.15 us: body(): got_b = lax.ppermute(send_b, ('plane', 'wall'), plane_b)]
    ppermute x1, starting transfers between devices: 2.45 us -> 2.22 us  [body(): got_z = lax.ppermute(send_z, 'wall', pairings('wall')[0])]
  transfers between devices with their start and end apart: 5 -> 5, of which waited for: 1 -> 2; matrix products, arithmetic and copies ran while one was open for 0% -> 0% of each run, Pallas kernels for 39% -> 43%
where the time goes in v5:
time: 17.7 us; the launch traced here: 17.6 us
  Pallas kernels  10.4 us (59%)
  starting transfers between devices  5.25 us (30%)
  waiting for transfers between devices  1.25 us (7%)
  between operations  0.69 us (4%)
    pallas_call x8, Pallas kernels, call(): pl.pallas_call(kernel, out_shape=shapes, in_specs=specs, out_specs=[pl.Bl...  10.4 us
    ppermute x1, starting transfers between devices, body(): got_z = lax.ppermute(send_z, 'wall', pairings('wall')[0])  2.22 us
    ppermute x1, starting transfers between devices, body(): got_a = lax.ppermute(send_a, ('plane', 'wall'), plane_a)  1.36 us
    ppermute x1, starting transfers between devices, body(): lax.ppermute(m, 'span', pairs)  1.26 us
    ppermute x1, waiting for transfers between devices, body(): got_b = lax.ppermute(send_b, ('plane', 'wall'), plane_b)  1.15 us
    ppermute x1, starting transfers between devices, body(): theirs = lax.ppermute(mine, 'wall', pairings('wall')[0])  0.41 us
  transfers between devices with their start and end apart: 5, of which 2 were waited for; matrix products, arithmetic and copies ran while one was open for 0% of the time, Pallas kernels for 43%

profile of v5, /device:TPU:17, one launch (start us, length us, event | category | flops | bytes accessed | tf_op | source)
XLA Modules:
  0.0 17.6 jit_solution(16487935660284598283)
XLA Ops:
  0.6 1.5 %shard_map.59 = (f32[14,8,256]{2,1,0:T(8,128)S(1)}, f32[14,8,256]{2,1,0:T(8,128)S(1)}, f32[3,16,32,256]{3,2,1,0:T(8,128)S(1)}, f32[2,32,256]{2,1,0:T(8,128)S(1)}...) custom-call(f32[3,16,32,256]{3,2,1,0:T(8,128)} %vel_in.1, s32[32,256]{1,0:T(8,128)} %lev_in.1, f32[32,256]{1,0:T(8,128)} %frac_in.1, ...), custom_call_target="tpu_custom_call" | custom-call | bytes 1000000 | tf_op jit(solution)/shard_map/pallas_call | solution.py:25
  2.1 1.4 %collective-permute-start = (f32[14,8,256]{2,1,0:T(8,128)S(1)}, f32[14,8,256]{2,1,0:T(8,128)S(1)}, u32[]{:S(2)}, u32[]{:S(2)}) collective-permute-start(f32[14,8,256]{2,1,0:T(8,128)S(1)} %get-tuple-element.25), channel_id=1, source_target_pairs={{0,4},{1,5},{4,0},{5,1},{8,12},{9,13},{12,8},{13,9},{2,6},{3,7},{6... | collective-permute-start | bytes 344072 | tf_op jit(solution)/shard_map/ppermute | solution.py:744
  3.5 0.0 collective-permute-start.1
  3.5 2.6 %shard_map.60 = (f32[2,16,32,256]{3,2,1,0:T(8,128)S(1)}, f32[2,32,256]{2,1,0:T(8,128)S(1)}, f32[2,5,4,8,128]{4,3,2,1,0:T(8,128)S(1)}) custom-call(f32[3,16,32,256]{3,2,1,0:T(8,128)S(1)} %get-tuple-element.21.vel, f32[2,32,256]{2,1,0:T(8,128)S(1)} %get-tuple-element.22.flat, bf16[1024,256]{1,0:T(8,128)(2,1)S(1)} %get-tuple-element.23.band_ref), custom_call_target="tpu_custom_call" | custom-call | flops 20000000 | bytes 3000000 | tf_op jit(solution)/shard_map/pallas_call | solution.py:25
  6.1 0.1 collective-permute-done.got_a
  6.2 1.2 %collective-permute-done.1.got_b = f32[14,8,256]{2,1,0:T(8,128)S(1)} collective-permute-done((f32[14,8,256]{2,1,0:T(8,128)S(1)}, f32[14,8,256]{2,1,0:T(8,128)S(1)}, u32[]{:S(2)}, u32[]{:S(2)}) %collective-permute-start.1) | collective-permute-done | bytes 114720 | tf_op jit(solution)/shard_map/ppermute | solution.py:743
  7.4 0.4 %shard_map.62 = (f32[3,16,8,256]{3,2,1,0:T(8,128)S(1)}, f32[4,8,256]{2,1,0:T(8,128)S(1)}, f32[2,25,8,128]{3,2,1,0:T(8,128)S(1)}, f32[2,8,128]{2,1,0:T(8,128)S(1)}, f32[19,8,128]{2,1,0:T(8,128)S(1)}) custom-call(f32[14,8,256]{2,1,0:T(8,128)S(1)} %collective-permute-done.got_a, f32[14,8,256]{2,1,0:T(8,128)S(1)} %collective-permute-done.1.got_b, ...), custom_call_target="tpu_custom_call" | custom-call | bytes 1000000 | tf_op jit(solution)/shard_map/pallas_call | solution.py:25
  7.8 1.3 %collective-permute-start.2 = (f32[19,8,128]{2,1,0:T(8,128)S(1)}, f32[19,8,128]{2,1,0:T(8,128)S(1)}, u32[]{:S(2)}, u32[]{:S(2)}) collective-permute-start(f32[19,8,128]{2,1,0:T(8,128)S(1)} %get-tuple-element.36.rest_1_), channel_id=1, source_target_pairs={{0,2},{2,0},{1,3},{3,1},{4,6},{6,4},{5,7},{7,5},{8,10},{10,8},{9,1... | collective-permute-start | bytes 233480 | tf_op jit(solution)/shard_map/ppermute | solution.py:771
  9.1 1.5 %shard_map.61.new_z.rest_2_ = f32[1,16,32,256]{3,2,1,0:T(8,128)S(1)} custom-call(f32[3,16,32,256]{3,2,1,0:T(8,128)S(1)} %get-tuple-element.21.vel, f32[2,32,256]{2,1,0:T(8,128)S(1)} %get-tuple-element.22.flat, bf16[1024,256]{1,0:T(8,128)(2,1)S(1)} %get-tuple-element.23.band_ref), custom_call_target="tpu_custom_call" | custom-call | flops 10000000 | bytes 3000000 | tf_op jit(solution)/shard_map/pallas_call | solution.py:25
  10.5 1.0 %shard_map.63 = (f32[3,16,8,256]{3,2,1,0:T(8,128)S(1)}, f32[2,2,8,256]{3,2,1,0:T(8,128)S(1)}, f32[3,2,32,256]{3,2,1,0:T(8,128)S(1)}) custom-call(f32[3,16,32,256]{3,2,1,0:T(8,128)S(1)} %get-tuple-element.21.vel, f32[2,32,256]{2,1,0:T(8,128)S(1)} %get-tuple-element.22.flat, f32[3,16,8,256]{3,2,1,0:T(8,128)S(1)} %get-tuple-element.29.halo, ...), custom_call_target="tpu_custom_call" | custom-call | flops 10000000 | bytes 2000000 | tf_op jit(solution)/shard_map/pallas_call | solution.py:25
  11.5 2.2 %collective-permute-start.3 = (f32[3,2,32,256]{3,2,1,0:T(8,128)S(1)}, f32[3,2,32,256]{3,2,1,0:T(8,128)S(1)}, u32[]{:S(2)}, u32[]{:S(2)}) collective-permute-start(f32[3,2,32,256]{3,2,1,0:T(8,128)S(1)} %get-tuple-element.38), channel_id=1, source_target_pairs={{0,1},{1,0},{2,3},{3,2},{4,5},{5,4},{6,7},{7,6},{8,9},{9,8},{10,11... | collective-permute-start | bytes 589832 | tf_op jit(solution)/shard_map/ppermute | solution.py:783
  13.8 0.0 collective-permute-done.2.rest_0_
  13.8 1.1 %shard_map.64 = (f32[3,32,128]{2,1,0:T(8,128)S(1)}, f32[46,8,128]{2,1,0:T(8,128)S(1)}) custom-call(f32[2,25,8,128]{3,2,1,0:T(8,128)S(1)} %get-tuple-element.32.full, f32[2,8,128]{2,1,0:T(8,128)S(1)} %get-tuple-element.33.far, f32[2,32,256]{2,1,0:T(8,128)S(1)} %get-tuple-element.34.shear, f32[2,2,8,256]{3,2,1,0:T(8,128)S(1)} %get-tuple-element.35.strips, ...), custom_call_target="tpu_custom_call" | custom-call | bytes 1000000 | tf_op jit(solution)/shard_map/pallas_call | solution.py:25
  14.9 0.4 %collective-permute-start.4 = (f32[46,8,128]{2,1,0:T(8,128)S(1)}, f32[46,8,128]{2,1,0:T(8,128)S(1)}, u32[]{:S(2)}, u32[]{:S(2)}) collective-permute-start(f32[46,8,128]{2,1,0:T(8,128)S(1)} %get-tuple-element.39.mine), channel_id=1, source_target_pairs={{0,1},{1,0},{2,3},{3,2},{4,5},{5,4},{6,7},{7,6},{8,9},{9,8},{10,11... | collective-permute-start | bytes 565256 | tf_op jit(solution)/shard_map/ppermute | solution.py:794
  15.3 0.0 collective-permute-done.3.far
  15.3 1.4 %shard_map.65 = f32[3,16,32,256]{3,2,1,0:T(8,128)} custom-call(f32[2,16,32,256]{3,2,1,0:T(8,128)S(1)} %get-tuple-element.24.new, f32[1,16,32,256]{3,2,1,0:T(8,128)S(1)} %shard_map.61.new_z.rest_2_, f32[3,16,8,256]{3,2,1,0:T(8,128)S(1)} %get-tuple-element.31.fix, f32[3,32,128]{2,1,0:T(8,128)S(1)} %get-tuple-element.37.fresh, ...), custom_call_target="tpu_custom_call" | custom-call | flops 2000000 | bytes 4000000 | tf_op jit(solution)/shard_map/pallas_call | solution.py:25
  16.7 0.0 collective-permute-done.4.theirs
  16.7 0.9 %shard_map.66 = f32[32,256]{1,0:T(8,128)} custom-call(f32[46,8,128]{2,1,0:T(8,128)S(1)} %get-tuple-element.39.mine, f32[46,8,128]{2,1,0:T(8,128)S(1)} %collective-permute-done.4.theirs), custom_call_target="tpu_custom_call" | custom-call | bytes 1000000 | tf_op jit(solution)/shard_map/pallas_call | solution.py:25
Async XLA Ops:
  2.1 4.1 %collective-permute-start = (f32[14,8,256]{2,1,0:T(8,128)S(1)}, f32[14,8,256]{2,1,0:T(8,128)S(1)}, u32[]{:S(2)}, u32[]{:S(2)}) collective-permute-start(f32[14,8,256]{2,1,0:T(8,128)S(1)} %get-tuple-element.25), channel_id=1, source_target_pairs={{0,4},{1,5},{4,0},{5,1},{8,12},{9,13},{12,8},{13,9},{2,6},{3,7},{6... | collective-permute-start | bytes 344072 | tf_op jit(solution)/shard_map/ppermute | solution.py:744
  3.5 3.9 %collective-permute-start.1 = (f32[14,8,256]{2,1,0:T(8,128)S(1)}, f32[14,8,256]{2,1,0:T(8,128)S(1)}, u32[]{:S(2)}, u32[]{:S(2)}) collective-permute-start(f32[14,8,256]{2,1,0:T(8,128)S(1)} %get-tuple-element.26), channel_id=1, source_target_pairs={{0,1},{1,0},{4,8},{5,9},{8,4},{9,5},{12,13},{13,12},{2,3},{3,2},{6... | collective-permute-start | bytes 344072 | tf_op jit(solution)/shard_map/ppermute | solution.py:743
  7.8 6.0 %collective-permute-start.2 = (f32[19,8,128]{2,1,0:T(8,128)S(1)}, f32[19,8,128]{2,1,0:T(8,128)S(1)}, u32[]{:S(2)}, u32[]{:S(2)}) collective-permute-start(f32[19,8,128]{2,1,0:T(8,128)S(1)} %get-tuple-element.36.rest_1_), channel_id=1, source_target_pairs={{0,2},{2,0},{1,3},{3,1},{4,6},{6,4},{5,7},{7,5},{8,10},{10,8},{9,1... | collective-permute-start | bytes 233480 | tf_op jit(solution)/shard_map/ppermute | solution.py:771
  11.5 3.7 %collective-permute-start.3 = (f32[3,2,32,256]{3,2,1,0:T(8,128)S(1)}, f32[3,2,32,256]{3,2,1,0:T(8,128)S(1)}, u32[]{:S(2)}, u32[]{:S(2)}) collective-permute-start(f32[3,2,32,256]{3,2,1,0:T(8,128)S(1)} %get-tuple-element.38), channel_id=1, source_target_pairs={{0,1},{1,0},{2,3},{3,2},{4,5},{5,4},{6,7},{7,6},{8,9},{9,8},{10,11... | collective-permute-start | bytes 589832 | tf_op jit(solution)/shard_map/ppermute | solution.py:783
  14.9 1.8 %collective-permute-start.4 = (f32[46,8,128]{2,1,0:T(8,128)S(1)}, f32[46,8,128]{2,1,0:T(8,128)S(1)}, u32[]{:S(2)}, u32[]{:S(2)}) collective-permute-start(f32[46,8,128]{2,1,0:T(8,128)S(1)} %get-tuple-element.39.mine), channel_id=1, source_target_pairs={{0,1},{1,0},{2,3},{3,2},{4,5},{5,4},{6,7},{7,6},{8,9},{9,8},{10,11... | collective-permute-start | bytes 565256 | tf_op jit(solution)/shard_map/ppermute | solution.py:794

commit v6 on v5

--- a/solution.py
+++ b/solution.py
@@ -127,17 +127,16 @@
     if bed_in:
         halves = [bed[:, i * cols : (i + 1) * cols] for i in range(bed.shape[1] // cols)]
         put(count + 1, stack(halves, 2), stack(halves, 0))
-    for copy in pieces[:2]:
-        copy.wait()
     top = vel.at[:, :, pl.ds(0, SUB), :]
     bottom = vel.at[:, :, pl.ds(rows - SUB, SUB), :]
-    for c in range(3):
-        for k in range(layers // 4):
-            low = stack([bottom[c, 4 * k + i] for i in range(4)], 2)
-            high = stack([top[c, 4 * k + i] for i in range(4)], 0)
-            put(c * (layers // 4) + k, low, high)
+    quads = [(c, k) for c in range(3) for k in range(layers // 4)]
+    pieces[0].wait()
+    high = [stack([top[c, 4 * k + i] for i in range(4)], 0) for c, k in quads]
+    high_far = beyond_terms(top, high_lev, high_frac, base, layers, False)
+    pieces[1].wait()
+    for n, (c, k) in enumerate(quads):
+        put(n, stack([bottom[c, 4 * k + i] for i in range(4)], 2), high[n])
     low_far = beyond_terms(bottom, low_lev, low_frac, base, layers, True)
-    high_far = beyond_terms(top, high_lev, high_frac, base, layers, False)
     put(count, stack([low_lev, low_frac] + low_far, 2), stack([high_lev, high_frac] + high_far, 0))
     pieces[2].wait()
 
@@ -160,16 +159,19 @@
         put(1, c, jnp.where(column >= EDGE, left, 0.0))
 
 
+def over_groups(x):
+    step = 2 * EDGE
+    while step < LANE:
+        x = x + pltpu.roll(x, step, 1) + (pltpu.roll(x, 2 * step, 1) + pltpu.roll(x, 3 * step, 1))
+        step *= 4
+    return x
+
+
 def repeat_edges(field, rows, cols):
     lane = iota((rows, LANE), 1)
     right = jnp.where(lane < EDGE, pltpu.roll(field[:, cols - LANE :], EDGE, 1), 0.0)
     left = pltpu.roll(jnp.where(lane < EDGE, field[:, :LANE], 0.0), EDGE, 1)
-    step = 2 * EDGE
-    while step < LANE:
-        right = right + pltpu.roll(right, step, 1)
-        left = left + pltpu.roll(left, step, 1)
-        step *= 2
-    return right, left
+    return over_groups(right), over_groups(left)
 
 
 def inner_kernel(layers, comps, vel, flat, band_ref, *refs):
@@ -326,7 +328,7 @@
     for side, shift in ((0, EDGE), (1, LANE - EDGE)):
         for t in range(tall):
             u, v, w, level, fraction = [full_ref[side, n * tall + t] for n in range(5)]
-            last = jnp.where(group == 0, level, jnp.where(group == 1, fraction, 0.0))
+            last = jnp.where(lax.rem(group, 2) == 0, level, fraction)
             packed.append(u + pltpu.roll(v, shift, 1))
             packed.append(w + pltpu.roll(last, shift, 1))
     for i, message in enumerate(messages):
@@ -461,23 +463,11 @@
             up = jnp.where(here < 1, minus, 0.0) - jnp.where(here < 2, minus_far, 0.0)
             part = jnp.where(hit, value, 0.0)
             part = part + gain * fraction * (jnp.where(hit_down, down, 0.0) + jnp.where(hit_up, up, 0.0))
-            step = LANE // 2
-            while step >= width:
-                part = part + pltpu.roll(part, step, 1)
-                step //= 2
+            part = over_groups(part)
             more = extra if c == 0 else ahead(extra, width, 1)
             more = jnp.concatenate([jnp.zeros((shape[0] - SUB, LANE), jnp.float32), more], axis=0)
             shear.append((part + gain * fraction * more) * scale)
     return fresh, shear
-
-
-def everywhere(x):
-    step = 2 * EDGE
-    x = jnp.where(iota(x.shape, 1) < step, x, 0.0)
-    while step < LANE:
-        x = x + pltpu.roll(x, step, 1)
-        step *= 2
-    return x
 
 
 def side_kernel(layers, spans, bed_in, full, far, shear, strips, *rest):
@@ -492,6 +482,7 @@
     right_first = even("span")
     results = []
     column = lax.rem(iota((tall * SUB, LANE), 1), 2 * EDGE)
+    alternate = lax.rem(iota((tall * SUB, LANE), 1) // (2 * EDGE), 2)
     fresh_sides = []
     for side in range(2):
         first = right_first if side == 0 else jnp.logical_not(right_first)
@@ -504,7 +495,8 @@
         both = [jnp.concatenate([other(2 * t + i) for t in range(tall)], axis=0) for i in range(2)]
         turned = [jnp.where(given, pltpu.roll(b, back, 1), 0.0) for b in both]
         theirs = [jnp.where(given, both[0], 0.0), turned[0], jnp.where(given, both[1], 0.0)]
-        theirs += [everywhere(turned[1]), everywhere(ahead(turned[1], 2 * EDGE, 1))]
+        theirs.append(jnp.where(alternate == 0, turned[1], pltpu.roll(turned[1], 2 * EDGE, 1)))
+        theirs.append(jnp.where(alternate == 1, turned[1], ahead(turned[1], 2 * EDGE, 1)))
         fields = []
         for n in range(5):
             own = full[side, n * tall : (n + 1) * tall].reshape(tall * SUB, LANE)
@@ -571,33 +563,43 @@
     far_gain = gain * opened_at(levels, fraction, (base + far_to).astype(jnp.float32))
     near_w, far_w = far[2, near_from], far[2, far_from]
     copies = []
+    part = layers // 4
+
+    def merge(c, z):
+        for t in range(rows // SUB):
+            at = slice(t * SUB, (t + 1) * SUB)
+            side = pltpu.roll(fresh[c, at], (LANE - EDGE - 2 * EDGE * z) % LANE, 1)
+            for k in range(lanes):
+                cut = slice(k * LANE, (k + 1) * LANE)
+                piece = new[c, z, at, cut] if c < 2 else new_z[0, z, at, cut]
+                if t == 0:
+                    piece = piece + jnp.where(sub < 2, fix[c, z, :, cut], 0.0)
+                if t == rows // SUB - 1:
+                    piece = piece + jnp.where(sub >= SUB - 2, fix[c, z, :, cut], 0.0)
+                if k == 0:
+                    piece = jnp.where(lane < 2, side, piece)
+                if k == lanes - 1:
+                    piece = jnp.where(lane >= LANE - 2, side, piece)
+                out_ref[c, z, at, cut] = piece
+
+    def send(c, i):
+        at = pl.ds(i * part, part)
+        copies.append(pltpu.make_async_copy(out_ref.at[c, at], final.at[c, at], sems.at[4 * c + i]))
+        copies[-1].start()
+
     for c in range(3):
-        for z in range(layers):
-            for t in range(rows // SUB):
-                at = slice(t * SUB, (t + 1) * SUB)
-                side = pltpu.roll(fresh[c, at], (LANE - EDGE - 2 * EDGE * z) % LANE, 1)
-                for k in range(lanes):
-                    cut = slice(k * LANE, (k + 1) * LANE)
-                    piece = new[c, z, at, cut] if c < 2 else new_z[0, z, at, cut]
-                    if t == 0:
-                        piece = piece + jnp.where(sub < 2, fix[c, z, :, cut], 0.0)
-                    if t == rows // SUB - 1:
-                        piece = piece + jnp.where(sub >= SUB - 2, fix[c, z, :, cut], 0.0)
-                    if k == 0:
-                        piece = jnp.where(lane < 2, side, piece)
-                    if k == lanes - 1:
-                        piece = jnp.where(lane >= LANE - 2, side, piece)
-                    out_ref[c, z, at, cut] = piece
-        near_q = near_open * far[c, near_from]
-        near_f = sign * (near_w * near_q)
-        far_f = sign * (far_w * (far_open * far[c, far_from]))
-        out_ref[c, near_to] = out_ref[c, near_to] + near_gain * (6.0 * near_q + 8.0 * near_f - far_f)
-        out_ref[c, far_to] = out_ref[c, far_to] - far_gain * near_f
-        part = layers // 4
-        for i in range(4):
-            at = pl.ds(i * part, part)
-            copies.append(pltpu.make_async_copy(out_ref.at[c, at], final.at[c, at], sems.at[4 * c + i]))
-            copies[-1].start()
+        for i in (0, 3, 1, 2):
+            for z in range(i * part, (i + 1) * part):
+                merge(c, z)
+            if i == 3:
+                near_q = near_open * far[c, near_from]
+                near_f = sign * (near_w * near_q)
+                far_f = sign * (far_w * (far_open * far[c, far_from]))
+                out_ref[c, near_to] = out_ref[c, near_to] + near_gain * (6.0 * near_q + 8.0 * near_f - far_f)
+                out_ref[c, far_to] = out_ref[c, far_to] - far_gain * near_f
+                send(c, 0)
+            if i > 0:
+                send(c, i)
     for copy in copies:
         copy.wait()
 

time: 17.7 us -> 17.2 us (0.972)
  Pallas kernels: 10.4 us -> 9.9 us
    pallas_call x8, Pallas kernels: 10.4 us -> 9.9 us  [call(): pl.pallas_call(kernel, out_shape=shapes, in_specs=specs, out_specs=[pl.Bl...]
  transfers between devices with their start and end apart: 5 -> 5, of which waited for: 2 -> 1; matrix products, arithmetic and copies ran while one was open for 0% -> 0% of each run, Pallas kernels for 43% -> 42%
where the time goes in v6:
time: 17.2 us; the launch traced here: 17 us
  Pallas kernels  9.9 us (58%)
  starting transfers between devices  5.26 us (31%)
  waiting for transfers between devices  1.17 us (7%)
  between operations  0.68 us (4%)
    pallas_call x8, Pallas kernels, call(): pl.pallas_call(kernel, out_shape=shapes, in_specs=specs, out_specs=[pl.Bl...  9.9 us
    ppermute x1, starting transfers between devices, body(): got_z = lax.ppermute(send_z, 'wall', pairings('wall')[0])  2.22 us
    ppermute x1, starting transfers between devices, body(): got_a = lax.ppermute(send_a, ('plane', 'wall'), plane_a)  1.36 us
    ppermute x1, starting transfers between devices, body(): lax.ppermute(m, 'span', pairs)  1.28 us
    ppermute x1, waiting for transfers between devices, body(): got_b = lax.ppermute(send_b, ('plane', 'wall'), plane_b)  1.15 us
    ppermute x1, starting transfers between devices, body(): theirs = lax.ppermute(mine, 'wall', pairings('wall')[0])  0.4 us
  transfers between devices with their start and end apart: 5, of which 1 were waited for; matrix products, arithmetic and copies ran while one was open for 0% of the time, Pallas kernels for 42%

profile of v6, /device:TPU:17, one launch (start us, length us, event | category | flops | bytes accessed | tf_op | source)
XLA Modules:
  0.0 17.0 jit_solution(17809106131423703824)
XLA Ops:
  0.6 1.5 %shard_map.59 = (f32[14,8,256]{2,1,0:T(8,128)S(1)}, f32[14,8,256]{2,1,0:T(8,128)S(1)}, f32[3,16,32,256]{3,2,1,0:T(8,128)S(1)}, f32[2,32,256]{2,1,0:T(8,128)S(1)}...) custom-call(f32[3,16,32,256]{3,2,1,0:T(8,128)} %vel_in.1, s32[32,256]{1,0:T(8,128)} %lev_in.1, f32[32,256]{1,0:T(8,128)} %frac_in.1, ...), custom_call_target="tpu_custom_call" | custom-call | bytes 1000000 | tf_op jit(solution)/shard_map/pallas_call | solution.py:25
  2.1 1.4 %collective-permute-start = (f32[14,8,256]{2,1,0:T(8,128)S(1)}, f32[14,8,256]{2,1,0:T(8,128)S(1)}, u32[]{:S(2)}, u32[]{:S(2)}) collective-permute-start(f32[14,8,256]{2,1,0:T(8,128)S(1)} %get-tuple-element.25), channel_id=1, source_target_pairs={{0,4},{1,5},{4,0},{5,1},{8,12},{9,13},{12,8},{13,9},{2,6},{3,7},{6... | collective-permute-start | bytes 344072 | tf_op jit(solution)/shard_map/ppermute | solution.py:746
  3.5 0.0 collective-permute-start.1
  3.5 2.7 %shard_map.60 = (f32[2,16,32,256]{3,2,1,0:T(8,128)S(1)}, f32[2,32,256]{2,1,0:T(8,128)S(1)}, f32[2,5,4,8,128]{4,3,2,1,0:T(8,128)S(1)}) custom-call(f32[3,16,32,256]{3,2,1,0:T(8,128)S(1)} %get-tuple-element.21.vel, f32[2,32,256]{2,1,0:T(8,128)S(1)} %get-tuple-element.22.flat, bf16[1024,256]{1,0:T(8,128)(2,1)S(1)} %get-tuple-element.23.band_ref), custom_call_target="tpu_custom_call" | custom-call | flops 20000000 | bytes 3000000 | tf_op jit(solution)/shard_map/pallas_call | solution.py:25
  6.2 0.0 collective-permute-done.got_a
  6.2 1.2 %collective-permute-done.1.got_b = f32[14,8,256]{2,1,0:T(8,128)S(1)} collective-permute-done((f32[14,8,256]{2,1,0:T(8,128)S(1)}, f32[14,8,256]{2,1,0:T(8,128)S(1)}, u32[]{:S(2)}, u32[]{:S(2)}) %collective-permute-start.1) | collective-permute-done | bytes 114720 | tf_op jit(solution)/shard_map/ppermute | solution.py:745
  7.4 0.3 %shard_map.62 = (f32[3,16,8,256]{3,2,1,0:T(8,128)S(1)}, f32[4,8,256]{2,1,0:T(8,128)S(1)}, f32[2,25,8,128]{3,2,1,0:T(8,128)S(1)}, f32[2,8,128]{2,1,0:T(8,128)S(1)}, f32[19,8,128]{2,1,0:T(8,128)S(1)}) custom-call(f32[14,8,256]{2,1,0:T(8,128)S(1)} %collective-permute-done.got_a, f32[14,8,256]{2,1,0:T(8,128)S(1)} %collective-permute-done.1.got_b, ...), custom_call_target="tpu_custom_call" | custom-call | bytes 1000000 | tf_op jit(solution)/shard_map/pallas_call | solution.py:25
  7.7 1.3 %collective-permute-start.2 = (f32[19,8,128]{2,1,0:T(8,128)S(1)}, f32[19,8,128]{2,1,0:T(8,128)S(1)}, u32[]{:S(2)}, u32[]{:S(2)}) collective-permute-start(f32[19,8,128]{2,1,0:T(8,128)S(1)} %get-tuple-element.36.rest_1_), channel_id=1, source_target_pairs={{0,2},{2,0},{1,3},{3,1},{4,6},{6,4},{5,7},{7,5},{8,10},{10,8},{9,1... | collective-permute-start | bytes 233480 | tf_op jit(solution)/shard_map/ppermute | solution.py:773
  9.0 1.5 %shard_map.61.new_z.rest_2_ = f32[1,16,32,256]{3,2,1,0:T(8,128)S(1)} custom-call(f32[3,16,32,256]{3,2,1,0:T(8,128)S(1)} %get-tuple-element.21.vel, f32[2,32,256]{2,1,0:T(8,128)S(1)} %get-tuple-element.22.flat, bf16[1024,256]{1,0:T(8,128)(2,1)S(1)} %get-tuple-element.23.band_ref), custom_call_target="tpu_custom_call" | custom-call | flops 10000000 | bytes 3000000 | tf_op jit(solution)/shard_map/pallas_call | solution.py:25
  10.4 1.0 %shard_map.63 = (f32[3,16,8,256]{3,2,1,0:T(8,128)S(1)}, f32[2,2,8,256]{3,2,1,0:T(8,128)S(1)}, f32[3,2,32,256]{3,2,1,0:T(8,128)S(1)}) custom-call(f32[3,16,32,256]{3,2,1,0:T(8,128)S(1)} %get-tuple-element.21.vel, f32[2,32,256]{2,1,0:T(8,128)S(1)} %get-tuple-element.22.flat, f32[3,16,8,256]{3,2,1,0:T(8,128)S(1)} %get-tuple-element.29.halo, ...), custom_call_target="tpu_custom_call" | custom-call | flops 10000000 | bytes 2000000 | tf_op jit(solution)/shard_map/pallas_call | solution.py:25
  11.5 2.2 %collective-permute-start.3 = (f32[3,2,32,256]{3,2,1,0:T(8,128)S(1)}, f32[3,2,32,256]{3,2,1,0:T(8,128)S(1)}, u32[]{:S(2)}, u32[]{:S(2)}) collective-permute-start(f32[3,2,32,256]{3,2,1,0:T(8,128)S(1)} %get-tuple-element.38), channel_id=1, source_target_pairs={{0,1},{1,0},{2,3},{3,2},{4,5},{5,4},{6,7},{7,6},{8,9},{9,8},{10,11... | collective-permute-start | bytes 589832 | tf_op jit(solution)/shard_map/ppermute | solution.py:785
  13.7 0.0 collective-permute-done.2.rest_0_
  13.7 0.7 %shard_map.64 = (f32[3,32,128]{2,1,0:T(8,128)S(1)}, f32[46,8,128]{2,1,0:T(8,128)S(1)}) custom-call(f32[2,25,8,128]{3,2,1,0:T(8,128)S(1)} %get-tuple-element.32.full, f32[2,8,128]{2,1,0:T(8,128)S(1)} %get-tuple-element.33.far, f32[2,32,256]{2,1,0:T(8,128)S(1)} %get-tuple-element.34.shear, f32[2,2,8,256]{3,2,1,0:T(8,128)S(1)} %get-tuple-element.35.strips, ...), custom_call_target="tpu_custom_call" | custom-call | bytes 1000000 | tf_op jit(solution)/shard_map/pallas_call | solution.py:25
  14.4 0.4 %collective-permute-start.4 = (f32[46,8,128]{2,1,0:T(8,128)S(1)}, f32[46,8,128]{2,1,0:T(8,128)S(1)}, u32[]{:S(2)}, u32[]{:S(2)}) collective-permute-start(f32[46,8,128]{2,1,0:T(8,128)S(1)} %get-tuple-element.39.mine), channel_id=1, source_target_pairs={{0,1},{1,0},{2,3},{3,2},{4,5},{5,4},{6,7},{7,6},{8,9},{9,8},{10,11... | collective-permute-start | bytes 565256 | tf_op jit(solution)/shard_map/ppermute | solution.py:796
  14.8 0.0 collective-permute-done.3.far
  14.8 1.4 %shard_map.65 = f32[3,16,32,256]{3,2,1,0:T(8,128)} custom-call(f32[2,16,32,256]{3,2,1,0:T(8,128)S(1)} %get-tuple-element.24.new, f32[1,16,32,256]{3,2,1,0:T(8,128)S(1)} %shard_map.61.new_z.rest_2_, f32[3,16,8,256]{3,2,1,0:T(8,128)S(1)} %get-tuple-element.31.fix, f32[3,32,128]{2,1,0:T(8,128)S(1)} %get-tuple-element.37.fresh, ...), custom_call_target="tpu_custom_call" | custom-call | flops 2000000 | bytes 4000000 | tf_op jit(solution)/shard_map/pallas_call | solution.py:25
  16.1 0.0 collective-permute-done.4.theirs
  16.2 0.9 %shard_map.66 = f32[32,256]{1,0:T(8,128)} custom-call(f32[46,8,128]{2,1,0:T(8,128)S(1)} %get-tuple-element.39.mine, f32[46,8,128]{2,1,0:T(8,128)S(1)} %collective-permute-done.4.theirs), custom_call_target="tpu_custom_call" | custom-call | bytes 1000000 | tf_op jit(solution)/shard_map/pallas_call | solution.py:25
Async XLA Ops:
  2.1 4.1 %collective-permute-start = (f32[14,8,256]{2,1,0:T(8,128)S(1)}, f32[14,8,256]{2,1,0:T(8,128)S(1)}, u32[]{:S(2)}, u32[]{:S(2)}) collective-permute-start(f32[14,8,256]{2,1,0:T(8,128)S(1)} %get-tuple-element.25), channel_id=1, source_target_pairs={{0,4},{1,5},{4,0},{5,1},{8,12},{9,13},{12,8},{13,9},{2,6},{3,7},{6... | collective-permute-start | bytes 344072 | tf_op jit(solution)/shard_map/ppermute | solution.py:746
  3.5 3.9 %collective-permute-start.1 = (f32[14,8,256]{2,1,0:T(8,128)S(1)}, f32[14,8,256]{2,1,0:T(8,128)S(1)}, u32[]{:S(2)}, u32[]{:S(2)}) collective-permute-start(f32[14,8,256]{2,1,0:T(8,128)S(1)} %get-tuple-element.26), channel_id=1, source_target_pairs={{0,1},{1,0},{4,8},{5,9},{8,4},{9,5},{12,13},{13,12},{2,3},{3,2},{6... | collective-permute-start | bytes 344072 | tf_op jit(solution)/shard_map/ppermute | solution.py:745
  7.7 6.0 %collective-permute-start.2 = (f32[19,8,128]{2,1,0:T(8,128)S(1)}, f32[19,8,128]{2,1,0:T(8,128)S(1)}, u32[]{:S(2)}, u32[]{:S(2)}) collective-permute-start(f32[19,8,128]{2,1,0:T(8,128)S(1)} %get-tuple-element.36.rest_1_), channel_id=1, source_target_pairs={{0,2},{2,0},{1,3},{3,1},{4,6},{6,4},{5,7},{7,5},{8,10},{10,8},{9,1... | collective-permute-start | bytes 233480 | tf_op jit(solution)/shard_map/ppermute | solution.py:773
  11.5 3.3 %collective-permute-start.3 = (f32[3,2,32,256]{3,2,1,0:T(8,128)S(1)}, f32[3,2,32,256]{3,2,1,0:T(8,128)S(1)}, u32[]{:S(2)}, u32[]{:S(2)}) collective-permute-start(f32[3,2,32,256]{3,2,1,0:T(8,128)S(1)} %get-tuple-element.38), channel_id=1, source_target_pairs={{0,1},{1,0},{2,3},{3,2},{4,5},{5,4},{6,7},{7,6},{8,9},{9,8},{10,11... | collective-permute-start | bytes 589832 | tf_op jit(solution)/shard_map/ppermute | solution.py:785
  14.4 1.8 %collective-permute-start.4 = (f32[46,8,128]{2,1,0:T(8,128)S(1)}, f32[46,8,128]{2,1,0:T(8,128)S(1)}, u32[]{:S(2)}, u32[]{:S(2)}) collective-permute-start(f32[46,8,128]{2,1,0:T(8,128)S(1)} %get-tuple-element.39.mine), channel_id=1, source_target_pairs={{0,1},{1,0},{2,3},{3,2},{4,5},{5,4},{6,7},{7,6},{8,9},{9,8},{10,11... | collective-permute-start | bytes 565256 | tf_op jit(solution)/shard_map/ppermute | solution.py:796

commit v7 on v6

--- a/solution.py
+++ b/solution.py
@@ -207,7 +207,7 @@
                     split_ref[n, at, i * cols + k * LANE : i * cols + (k + 1) * LANE] = part
         return carry
 
-    lax.fori_loop(0, layers, prepare, 0)
+    lax.fori_loop(0, layers, prepare, 0, unroll=2)
     for n in range(len(comps)):
         x_ref[n] = jnp.dot(split_ref[n], band_ref[...], preferred_element_type=jnp.float32)
 
@@ -263,7 +263,7 @@
                     sums[2 * k + c] = sums[2 * k + c] + jnp.where(hit, fresh, 0.0)
         return tuple(sums)
 
-    sums = lax.fori_loop(0, layers, update, tuple(sums))
+    sums = lax.fori_loop(0, layers, update, tuple(sums), unroll=1 if with_shear else 2)
     if not with_shear:
         return
     for k in range(lanes):
@@ -273,7 +273,15 @@
             shear_ref[c, :, cut] = sums[2 * k + c] * scale
 
 
-def unpack_kernel(layers, bed_in, got_a, got_b, edge, bed, halo_ref, beside_ref, full_ref, far_ref, *messages):
+def bed_window(tiles, first):
+    lane = iota((SUB, LANE), 1)
+    inside = [jnp.where(first, tiles[k], tiles[2 + k]) for k in range(2)]
+    after = jnp.where(lane < 2, tiles[2], 0.0)
+    before = jnp.where(lane >= LANE - 2, tiles[1], 0.0)
+    return inside + [jnp.where(first, after, before)]
+
+
+def unpack_kernel(layers, bed_in, got_a, got_b, edge, bed, halo_ref, beside_ref, full_ref, far_ref, bed_ref, *messages):
     cols = halo_ref.shape[3]
     tiles = edge.shape[2]
     tall = tiles + 1
@@ -338,13 +346,23 @@
         message[2 * tall] = jnp.where(is_right, far_ref[0], far_ref[1])
     if bed_in:
         used = 2 * tall + 1
-        parts = bed.shape[1] // LANE
-        for i in range(parts):
-            messages[0][used + i] = bed[:, i * LANE : (i + 1) * LANE]
-        per = cols // LANE
-        for i, tile in enumerate(spread(count + 1, bed.shape[1] // cols)):
-            for j in range(per):
-                messages[0][used + parts + i * per + j] = tile[:, j * LANE : (j + 1) * LANE]
+        first = lax.axis_index("span") == 0
+        own = [bed[:, i * LANE : (i + 1) * LANE] for i in range(4)]
+        past = [tile[:, k * LANE : (k + 1) * LANE] for tile in spread(count + 1, 2) for k in range(2)]
+        for i, tile in enumerate(bed_window(own, first) + bed_window(past, first)):
+            bed_ref[i] = tile
+        there = jnp.logical_not(first)
+        one, two, three = bed_window(own, there)
+        four, five, six = bed_window(past, there)
+        row = iota((SUB, LANE), 0)
+        messages[0][used] = one
+        messages[0][used + 1] = two
+        moved = jnp.where(row < EDGE, pltpu.roll(five, 2, 0), pltpu.roll(five, SUB - 2, 0))
+        messages[0][used + 2] = jnp.where((row < 2) | (row >= SUB - 2), four, moved)
+        rest = pltpu.roll(three, LANE // 4, 1) + pltpu.roll(six, LANE // 2, 1)
+        messages[0][used - 1] = jnp.where(first, far_ref[0], far_ref[1]) + rest
+    else:
+        bed_ref[0] = jnp.zeros((SUB, LANE), jnp.float32)
 
 
 def strip_kernel(layers, vel, flat, halo, beside, new_z, fix_ref, shear_ref, z_ref, q_ref, f_ref):
@@ -422,7 +440,7 @@
             sums[2 + c] = sums[2 + c] + jnp.where(own_hit, fix, 0.0)
         return tuple(sums)
 
-    sums = lax.fori_loop(0, layers, update, (sums[0], sums[1], blank, blank), unroll=4)
+    sums = lax.fori_loop(0, layers, update, (sums[0], sums[1], blank, blank), unroll=8)
     scale = 1.0 / (0.5 + fraction)
     own_scale = 1.0 / (0.5 + own_fraction)
     for c in range(2):
@@ -473,7 +491,7 @@
 def side_kernel(layers, spans, bed_in, full, far, shear, strips, *rest):
     got = rest[:spans]
     rest = rest[spans:]
-    own_message = rest[0]
+    own_bed = rest[0]
     fresh_ref, out_ref = rest[2:]
     _, rows, cols = shear.shape
     tiles = rows // SUB
@@ -535,10 +553,16 @@
     if bed_in:
         used = 2 * tall * (lanes + 1)
         start = 2 * tall + 1
-        count = own_message.shape[0] - start
-        for i in range(count):
-            out_ref[used + i] = own_message[start + i]
-            out_ref[used + count + i] = got[0][start + i]
+        beyond = (lane < 2) | (lane >= LANE - 2)
+        outer = (sub < 2) | (sub >= SUB - 2)
+        rest, pack = got[0][start - 1], got[0][start + 2]
+        moved = jnp.where(sub < EDGE, pltpu.roll(pack, SUB - 2, 0), pltpu.roll(pack, 2, 0))
+        theirs = [got[0][start], got[0][start + 1], jnp.where(beyond, pltpu.roll(rest, LANE - LANE // 4, 1), 0.0)]
+        theirs += [jnp.where(outer, pack, 0.0), jnp.where(outer, moved, 0.0)]
+        theirs.append(jnp.where(beyond, pltpu.roll(rest, LANE // 2, 1), 0.0))
+        for i in range(6):
+            out_ref[used + i] = own_bed[i]
+            out_ref[used + 6 + i] = theirs[i]
 
 
 def merge_kernel(layers, new, new_z, fix, fresh, far, flat, final, out_ref, sems):
@@ -624,28 +648,18 @@
     shear_x, shear_y = sheared(0), sheared(1)
     if bed_in:
         used = 2 * tall * (lanes + 1)
-        parts = 2 * lanes
 
         def tile_of(s, w, which):
             pieces = []
-            for k in range(parts):
-                own = used + which * parts + k
-                across = own + 2 * parts
-                from_mine = jnp.where(span == s, mine[own], mine[across])
-                from_theirs = jnp.where(span == s, theirs[own], theirs[across])
+            for k in range(lanes + 1):
+                own = used + 3 * which + k
+                from_mine = jnp.where(span == s, mine[own], mine[own + 6])
+                from_theirs = jnp.where(span == s, theirs[own], theirs[own + 6])
                 pieces.append(jnp.where(wall == w, from_mine, from_theirs))
             return pieces
 
         def window(pieces):
-            lane = iota((SUB, LANE), 1)
-            low = span == 0
-            inside = [jnp.where(low, pieces[k], pieces[lanes + k]) for k in range(lanes)]
-            beyond = jnp.where(
-                low,
-                jnp.where(lane < LANE // 2, pieces[lanes], 0.0),
-                jnp.where(lane < LANE // 2, 0.0, pieces[lanes - 1]),
-            )
-            return jnp.concatenate(inside + [beyond], axis=1)
+            return jnp.concatenate(pieces, axis=1)
 
         sub = iota((SUB, LANE), 0)
         whole = [window(tile_of(s, w, 0)) for s in range(2) for w in range(2)]
@@ -727,7 +741,7 @@
     spans = lax.axis_size("span")
     walls = lax.axis_size("wall")
     assert walls == 2 and layers * 2 * EDGE == LANE
-    bed_in = spans == 2 and bed_height.shape == (SUB, 2 * cols)
+    bed_in = spans == 2 and lanes == 2 and bed_height.shape == (SUB, 2 * cols)
     count = 3 * layers // 4 + (2 if bed_in else 1)
     dma = pltpu.SemaphoreType.DMA
     sheet = (3, layers, SUB, cols)
@@ -760,16 +774,17 @@
 
     new, shear, edge = inner((0, 1), [(2, rows, cols), (2, 5, tiles, SUB, LANE)], 20_000_000)
     span_lists = [p for p in pairings("span") if p]
-    message = (2 * tall + 1 + (4 * lanes if bed_in else 0), SUB, LANE)
+    message = (2 * tall + 1 + (3 if bed_in else 0), SUB, LANE)
     unpacked = call(
         functools.partial(unpack_kernel, layers, bed_in),
-        [sheet, (4, SUB, cols), (2, 5 * tall, SUB, LANE), (2, SUB, LANE)] + [message] * len(span_lists),
+        [sheet, (4, SUB, cols), (2, 5 * tall, SUB, LANE), (2, SUB, LANE), (6, SUB, LANE)]
+        + [message] * len(span_lists),
         [got_a, got_b, edge, bed],
         moved=1_000_000,
         limit=10,
     )
-    halo, beside, full, far = unpacked[:4]
-    messages = unpacked[4:]
+    halo, beside, full, far, own_bed = unpacked[:5]
+    messages = unpacked[5:]
     got = [lax.ppermute(m, "span", pairs) for m, pairs in zip(messages, span_lists)]
     shallow = pltpu.VMEM((2, layers + 4, SUB, cols), jnp.float32)
     (new_z,) = inner((2,), [], 10_000_000)
@@ -784,11 +799,11 @@
     )
     got_z = lax.ppermute(send_z, "wall", pairings("wall")[0])
     shear_count = 2 * tall * (lanes + 1)
-    out_count = shear_count + (8 * lanes if bed_in else 0)
+    out_count = shear_count + (12 if bed_in else 0)
     fresh, mine = call(
         functools.partial(side_kernel, layers, len(got), bed_in),
         [(3, rows, LANE), (out_count, SUB, LANE)],
-        [full, far, shear, strip_shear] + got + [messages[0], new_z],
+        [full, far, shear, strip_shear] + got + [own_bed, new_z],
         any_inputs=(5 + len(got),),
         moved=1_000_000,
         limit=10,

time: 17.2 us -> 17 us (0.988)
  transfers between devices with their start and end apart: 5 -> 5, of which waited for: 1 -> 3; matrix products, arithmetic and copies ran while one was open for 0% -> 0% of each run, Pallas kernels for 42% -> 42%
where the time goes in v7:
time: 17 us; the launch traced here: 16.9 us
  Pallas kernels  9.74 us (57%)
  starting transfers between devices  5.15 us (30%)
  waiting for transfers between devices  1.3 us (8%)
  between operations  0.68 us (4%)
    pallas_call x8, Pallas kernels, call(): pl.pallas_call(kernel, out_shape=shapes, in_specs=specs, out_specs=[pl.Bl...  9.74 us
    ppermute x1, starting transfers between devices, body(): got_z = lax.ppermute(send_z, 'wall', pairings('wall')[0])  2.23 us
    ppermute x1, starting transfers between devices, body(): got_a = lax.ppermute(send_a, ('plane', 'wall'), plane_a)  1.36 us
    ppermute x1, starting transfers between devices, body(): lax.ppermute(m, 'span', pairs)  1.25 us
    ppermute x1, waiting for transfers between devices, body(): got_b = lax.ppermute(send_b, ('plane', 'wall'), plane_b)  1.15 us
  transfers between devices with their start and end apart: 5, of which 3 were waited for; matrix products, arithmetic and copies ran while one was open for 0% of the time, Pallas kernels for 42%

profile of v7, /device:TPU:17, one launch (start us, length us, event | category | flops | bytes accessed | tf_op | source)
XLA Modules:
  0.0 16.9 jit_solution(3337328760355477653)
XLA Ops:
  0.6 1.5 %shard_map.59 = (f32[14,8,256]{2,1,0:T(8,128)S(1)}, f32[14,8,256]{2,1,0:T(8,128)S(1)}, f32[3,16,32,256]{3,2,1,0:T(8,128)S(1)}, f32[2,32,256]{2,1,0:T(8,128)S(1)}...) custom-call(f32[3,16,32,256]{3,2,1,0:T(8,128)} %vel_in.1, s32[32,256]{1,0:T(8,128)} %lev_in.1, f32[32,256]{1,0:T(8,128)} %frac_in.1, ...), custom_call_target="tpu_custom_call" | custom-call | bytes 1000000 | tf_op jit(solution)/shard_map/pallas_call | solution.py:25
  2.1 1.4 %collective-permute-start = (f32[14,8,256]{2,1,0:T(8,128)S(1)}, f32[14,8,256]{2,1,0:T(8,128)S(1)}, u32[]{:S(2)}, u32[]{:S(2)}) collective-permute-start(f32[14,8,256]{2,1,0:T(8,128)S(1)} %get-tuple-element.26), channel_id=1, source_target_pairs={{0,4},{1,5},{4,0},{5,1},{8,12},{9,13},{12,8},{13,9},{2,6},{3,7},{6... | collective-permute-start | bytes 344072 | tf_op jit(solution)/shard_map/ppermute | solution.py:760
  3.5 0.0 collective-permute-start.1
  3.5 2.6 %shard_map.60 = (f32[2,16,32,256]{3,2,1,0:T(8,128)S(1)}, f32[2,32,256]{2,1,0:T(8,128)S(1)}, f32[2,5,4,8,128]{4,3,2,1,0:T(8,128)S(1)}) custom-call(f32[3,16,32,256]{3,2,1,0:T(8,128)S(1)} %get-tuple-element.22.vel, f32[2,32,256]{2,1,0:T(8,128)S(1)} %get-tuple-element.23.flat, bf16[1024,256]{1,0:T(8,128)(2,1)S(1)} %get-tuple-element.24.band_ref), custom_call_target="tpu_custom_call" | custom-call | flops 20000000 | bytes 3000000 | tf_op jit(solution)/shard_map/pallas_call | solution.py:25
  6.1 0.1 collective-permute-done.got_a
  6.2 1.2 %collective-permute-done.1.got_b = f32[14,8,256]{2,1,0:T(8,128)S(1)} collective-permute-done((f32[14,8,256]{2,1,0:T(8,128)S(1)}, f32[14,8,256]{2,1,0:T(8,128)S(1)}, u32[]{:S(2)}, u32[]{:S(2)}) %collective-permute-start.1) | collective-permute-done | bytes 114720 | tf_op jit(solution)/shard_map/ppermute | solution.py:759
  7.4 0.4 %shard_map.62 = (f32[3,16,8,256]{3,2,1,0:T(8,128)S(1)}, f32[4,8,256]{2,1,0:T(8,128)S(1)}, f32[2,25,8,128]{3,2,1,0:T(8,128)S(1)}, f32[2,8,128]{2,1,0:T(8,128)S(1)...) custom-call(f32[14,8,256]{2,1,0:T(8,128)S(1)} %collective-permute-done.got_a, ...), custom_call_target="tpu_custom_call" | custom-call | bytes 1000000 | tf_op jit(solution)/shard_map/pallas_call | solution.py:25
  7.7 1.3 %collective-permute-start.2 = (f32[14,8,128]{2,1,0:T(8,128)S(1)}, f32[14,8,128]{2,1,0:T(8,128)S(1)}, u32[]{:S(2)}, u32[]{:S(2)}) collective-permute-start(f32[14,8,128]{2,1,0:T(8,128)S(1)} %get-tuple-element.37), channel_id=1, source_target_pairs={{0,2},{2,0},{1,3},{3,1},{4,6},{6,4},{5,7},{7,5},{8,10},{10,8},{9,1... | collective-permute-start | bytes 172040 | tf_op jit(solution)/shard_map/ppermute | solution.py:788
  9.0 1.4 %shard_map.61.new_z.rest_2_ = f32[1,16,32,256]{3,2,1,0:T(8,128)S(1)} custom-call(f32[3,16,32,256]{3,2,1,0:T(8,128)S(1)} %get-tuple-element.22.vel, f32[2,32,256]{2,1,0:T(8,128)S(1)} %get-tuple-element.23.flat, bf16[1024,256]{1,0:T(8,128)(2,1)S(1)} %get-tuple-element.24.band_ref), custom_call_target="tpu_custom_call" | custom-call | flops 10000000 | bytes 3000000 | tf_op jit(solution)/shard_map/pallas_call | solution.py:25
  10.4 1.0 %shard_map.63 = (f32[3,16,8,256]{3,2,1,0:T(8,128)S(1)}, f32[2,2,8,256]{3,2,1,0:T(8,128)S(1)}, f32[3,2,32,256]{3,2,1,0:T(8,128)S(1)}) custom-call(f32[3,16,32,256]{3,2,1,0:T(8,128)S(1)} %get-tuple-element.22.vel, f32[2,32,256]{2,1,0:T(8,128)S(1)} %get-tuple-element.23.flat, f32[3,16,8,256]{3,2,1,0:T(8,128)S(1)} %get-tuple-element.30.halo, ...), custom_call_target="tpu_custom_call" | custom-call | flops 10000000 | bytes 2000000 | tf_op jit(solution)/shard_map/pallas_call | solution.py:25
  11.3 2.2 %collective-permute-start.3 = (f32[3,2,32,256]{3,2,1,0:T(8,128)S(1)}, f32[3,2,32,256]{3,2,1,0:T(8,128)S(1)}, u32[]{:S(2)}, u32[]{:S(2)}) collective-permute-start(f32[3,2,32,256]{3,2,1,0:T(8,128)S(1)} %get-tuple-element.40), channel_id=1, source_target_pairs={{0,1},{1,0},{2,3},{3,2},{4,5},{5,4},{6,7},{7,6},{8,9},{9,8},{10,11... | collective-permute-start | bytes 589832 | tf_op jit(solution)/shard_map/ppermute | solution.py:800
  13.6 0.0 collective-permute-done.2.rest_0_
  13.6 0.7 %shard_map.64 = (f32[3,32,128]{2,1,0:T(8,128)S(1)}, f32[42,8,128]{2,1,0:T(8,128)S(1)}) custom-call(f32[2,25,8,128]{3,2,1,0:T(8,128)S(1)} %get-tuple-element.33.full, f32[2,8,128]{2,1,0:T(8,128)S(1)} %get-tuple-element.34.far, f32[2,32,256]{2,1,0:T(8,128)S(1)} %get-tuple-element.35.shear, f32[2,2,8,256]{3,2,1,0:T(8,128)S(1)} %get-tuple-element.36.strips, ...), custom_call_target="tpu_custom_call" | custom-call | bytes 1000000 | tf_op jit(solution)/shard_map/pallas_call | solution.py:25
  14.3 0.3 %collective-permute-start.4 = (f32[42,8,128]{2,1,0:T(8,128)S(1)}, f32[42,8,128]{2,1,0:T(8,128)S(1)}, u32[]{:S(2)}, u32[]{:S(2)}) collective-permute-start(f32[42,8,128]{2,1,0:T(8,128)S(1)} %get-tuple-element.41.mine), channel_id=1, source_target_pairs={{0,1},{1,0},{2,3},{3,2},{4,5},{5,4},{6,7},{7,6},{8,9},{9,8},{10,11... | collective-permute-start | bytes 516104 | tf_op jit(solution)/shard_map/ppermute | solution.py:811
  14.6 0.1 collective-permute-done.3.far
  14.7 1.3 %shard_map.65 = f32[3,16,32,256]{3,2,1,0:T(8,128)} custom-call(f32[2,16,32,256]{3,2,1,0:T(8,128)S(1)} %get-tuple-element.25.new, f32[1,16,32,256]{3,2,1,0:T(8,128)S(1)} %shard_map.61.new_z.rest_2_, f32[3,16,8,256]{3,2,1,0:T(8,128)S(1)} %get-tuple-element.32.fix, f32[3,32,128]{2,1,0:T(8,128)S(1)} %get-tuple-element.39.fresh, ...), custom_call_target="tpu_custom_call" | custom-call | flops 2000000 | bytes 4000000 | tf_op jit(solution)/shard_map/pallas_call | solution.py:25
  16.0 0.0 collective-permute-done.4.theirs
  16.0 0.9 %shard_map.66 = f32[32,256]{1,0:T(8,128)} custom-call(f32[42,8,128]{2,1,0:T(8,128)S(1)} %get-tuple-element.41.mine, f32[42,8,128]{2,1,0:T(8,128)S(1)} %collective-permute-done.4.theirs), custom_call_target="tpu_custom_call" | custom-call | bytes 1000000 | tf_op jit(solution)/shard_map/pallas_call | solution.py:25
Async XLA Ops:
  2.1 4.1 %collective-permute-start = (f32[14,8,256]{2,1,0:T(8,128)S(1)}, f32[14,8,256]{2,1,0:T(8,128)S(1)}, u32[]{:S(2)}, u32[]{:S(2)}) collective-permute-start(f32[14,8,256]{2,1,0:T(8,128)S(1)} %get-tuple-element.26), channel_id=1, source_target_pairs={{0,4},{1,5},{4,0},{5,1},{8,12},{9,13},{12,8},{13,9},{2,6},{3,7},{6... | collective-permute-start | bytes 344072 | tf_op jit(solution)/shard_map/ppermute | solution.py:760
  3.5 3.9 %collective-permute-start.1 = (f32[14,8,256]{2,1,0:T(8,128)S(1)}, f32[14,8,256]{2,1,0:T(8,128)S(1)}, u32[]{:S(2)}, u32[]{:S(2)}) collective-permute-start(f32[14,8,256]{2,1,0:T(8,128)S(1)} %get-tuple-element.27), channel_id=1, source_target_pairs={{0,1},{1,0},{4,8},{5,9},{8,4},{9,5},{12,13},{13,12},{2,3},{3,2},{6... | collective-permute-start | bytes 344072 | tf_op jit(solution)/shard_map/ppermute | solution.py:759
  7.7 5.9 %collective-permute-start.2 = (f32[14,8,128]{2,1,0:T(8,128)S(1)}, f32[14,8,128]{2,1,0:T(8,128)S(1)}, u32[]{:S(2)}, u32[]{:S(2)}) collective-permute-start(f32[14,8,128]{2,1,0:T(8,128)S(1)} %get-tuple-element.37), channel_id=1, source_target_pairs={{0,2},{2,0},{1,3},{3,1},{4,6},{6,4},{5,7},{7,5},{8,10},{10,8},{9,1... | collective-permute-start | bytes 172040 | tf_op jit(solution)/shard_map/ppermute | solution.py:788
  11.3 3.3 %collective-permute-start.3 = (f32[3,2,32,256]{3,2,1,0:T(8,128)S(1)}, f32[3,2,32,256]{3,2,1,0:T(8,128)S(1)}, u32[]{:S(2)}, u32[]{:S(2)}) collective-permute-start(f32[3,2,32,256]{3,2,1,0:T(8,128)S(1)} %get-tuple-element.40), channel_id=1, source_target_pairs={{0,1},{1,0},{2,3},{3,2},{4,5},{5,4},{6,7},{7,6},{8,9},{9,8},{10,11... | collective-permute-start | bytes 589832 | tf_op jit(solution)/shard_map/ppermute | solution.py:800
  14.3 1.7 %collective-permute-start.4 = (f32[42,8,128]{2,1,0:T(8,128)S(1)}, f32[42,8,128]{2,1,0:T(8,128)S(1)}, u32[]{:S(2)}, u32[]{:S(2)}) collective-permute-start(f32[42,8,128]{2,1,0:T(8,128)S(1)} %get-tuple-element.41.mine), channel_id=1, source_target_pairs={{0,1},{1,0},{2,3},{3,2},{4,5},{5,4},{6,7},{7,6},{8,9},{9,8},{10,11... | collective-permute-start | bytes 516104 | tf_op jit(solution)/shard_map/ppermute | solution.py:811

commit v8 on v7

--- a/solution.py
+++ b/solution.py
@@ -174,18 +174,44 @@
     return over_groups(right), over_groups(left)
 
 
-def inner_kernel(layers, comps, vel, flat, band_ref, *refs):
-    with_shear = 0 in comps
-    new_ref = refs[0]
-    q_ref, f_ref, split_ref, x_ref = refs[-4:]
+def inner_change(z, cut, vel_y, q_ref, f_ref, x_ref):
+    q = q_ref[z + 2, :, cut]
+    rows = q.shape[0]
+    total = x_ref[pl.ds(pl.multiple_of(z * rows, rows), rows), cut] + sweep(vel_y * q, 6.0 * q, 0)
+    near = f_ref[z + 3, :, cut] - f_ref[z + 1, :, cut]
+    both = q_ref[z + 3, :, cut] + q_ref[z + 1, :, cut]
+    return total + (6.0 * both - 8.0 * near + (f_ref[z + 4, :, cut] - f_ref[z, :, cut]))
+
+
+def third_kernel(layers, vel, flat, q_ref, f_ref, x_ref, new_ref):
+    _, rows, cols = flat.shape
+    base = lax.axis_index("wall") * layers
+
+    def update(z, carry):
+        layer = (base + z).astype(jnp.float32)
+        for k in range(cols // LANE):
+            cut = slice(k * LANE, (k + 1) * LANE)
+            weight = gain * opened_at(flat[0, :, cut], flat[1, :, cut], layer)
+            change = inner_change(z, cut, vel[1, z, :, cut], q_ref, f_ref, x_ref)
+            new_ref[0, z, :, cut] = vel[2, z, :, cut] + weight * change
+        return carry
+
+    lax.fori_loop(0, layers, update, 0, unroll=2)
+
+
+def inner_kernel(layers, vel, flat, band_ref, new_ref, shear_ref, edge_ref, third_q, third_f, third_x, *scratch):
+    q_pair, f_pair, split_ref, x_pair = scratch
+    q_ref = [q_pair.at[0], q_pair.at[1], third_q]
+    f_ref = [f_pair.at[0], f_pair.at[1], third_f]
+    x_ref = [x_pair.at[0], x_pair.at[1], third_x]
     _, rows, cols = flat.shape
     base = lax.axis_index("wall") * layers
     lanes = cols // LANE
     blank = jnp.zeros((rows, cols), jnp.float32)
-    for n in range(len(comps)):
+    for c in range(3):
         for z in (0, 1, layers + 2, layers + 3):
-            q_ref[n, z] = blank
-            f_ref[n, z] = blank
+            q_ref[c][z] = blank
+            f_ref[c][z] = blank
 
     def halves(x):
         high = x.astype(jnp.bfloat16)
@@ -198,74 +224,62 @@
             cut = slice(k * LANE, (k + 1) * LANE)
             opened = opened_at(flat[0, :, cut], flat[1, :, cut], layer)
             vel_x, vel_z = vel[0, z, :, cut], vel[2, z, :, cut]
-            for n, c in enumerate(comps):
+            for c in range(3):
                 q = opened * vel[c, z, :, cut]
-                q_ref[n, z + 2, :, cut] = q
-                f_ref[n, z + 2, :, cut] = vel_z * q
+                q_ref[c][z + 2, :, cut] = q
+                f_ref[c][z + 2, :, cut] = vel_z * q
                 parts = halves(vel_x * q) + halves(q)
                 for i, part in enumerate(parts):
-                    split_ref[n, at, i * cols + k * LANE : i * cols + (k + 1) * LANE] = part
+                    split_ref[c, at, i * cols + k * LANE : i * cols + (k + 1) * LANE] = part
         return carry
 
     lax.fori_loop(0, layers, prepare, 0, unroll=2)
-    for n in range(len(comps)):
-        x_ref[n] = jnp.dot(split_ref[n], band_ref[...], preferred_element_type=jnp.float32)
-
-    if with_shear:
-        shear_ref, edge_ref = refs[1:3]
-
-        def put(side, n, value):
-            edge_ref[side, n] = value.reshape(rows // SUB, SUB, LANE)
-
-        gather_edges(lambda c, z: vel[c, z], layers, rows, cols, put)
-        for n in range(2):
-            right, left = repeat_edges(flat[n], rows, cols)
-            put(0, 3 + n, right)
-            put(1, 3 + n, left)
+    for c in range(3):
+        x_ref[c][...] = jnp.dot(split_ref[c], band_ref[...], preferred_element_type=jnp.float32)
+
+    def put(side, n, value):
+        edge_ref[side, n] = value.reshape(rows // SUB, SUB, LANE)
+
+    gather_edges(lambda c, z: vel[c, z], layers, rows, cols, put)
+    for n in range(2):
+        right, left = repeat_edges(flat[n], rows, cols)
+        put(0, 3 + n, right)
+        put(1, 3 + n, left)
 
     def outside(z, c, cut):
         total = jnp.zeros((rows, LANE), jnp.float32)
         for offset, weight in ((1, -8.0), (-1, 8.0), (2, 1.0), (-2, -1.0)):
             at = z + offset
             if 0 <= at < layers:
-                total = total + weight * f_ref[c, at + 2, :, cut]
+                total = total + weight * f_ref[c][at + 2, :, cut]
                 if abs(offset) == 1:
-                    total = total + 6.0 * q_ref[c, at + 2, :, cut]
+                    total = total + 6.0 * q_ref[c][at + 2, :, cut]
         hit = flat[0, :, cut] == (base + z).astype(jnp.float32)
         return jnp.where(hit, gain * flat[1, :, cut] * total, 0.0)
 
     sums = []
-    if with_shear:
-        for k in range(lanes):
-            cut = slice(k * LANE, (k + 1) * LANE)
-            for c in range(2):
-                sums.append(sum(outside(z, c, cut) for z in (-2, -1, layers, layers + 1)))
+    for k in range(lanes):
+        cut = slice(k * LANE, (k + 1) * LANE)
+        for c in range(2):
+            sums.append(sum(outside(z, c, cut) for z in (-2, -1, layers, layers + 1)))
 
     def update(z, sums):
         sums = list(sums)
         layer = (base + z).astype(jnp.float32)
-        at = pl.ds(pl.multiple_of(z * rows, rows), rows)
         for k in range(lanes):
             cut = slice(k * LANE, (k + 1) * LANE)
             level = flat[0, :, cut]
             weight = gain * opened_at(level, flat[1, :, cut], layer)
             hit = level == layer
             vel_y = vel[1, z, :, cut]
-            for n, c in enumerate(comps):
-                q = q_ref[n, z + 2, :, cut]
-                total = x_ref[n, at, cut] + sweep(vel_y * q, 6.0 * q, 0)
-                near = f_ref[n, z + 3, :, cut] - f_ref[n, z + 1, :, cut]
-                both = q_ref[n, z + 3, :, cut] + q_ref[n, z + 1, :, cut]
-                total = total + (6.0 * both - 8.0 * near + (f_ref[n, z + 4, :, cut] - f_ref[n, z, :, cut]))
-                fresh = vel[c, z, :, cut] + weight * total
-                new_ref[n, z, :, cut] = fresh
-                if with_shear:
-                    sums[2 * k + c] = sums[2 * k + c] + jnp.where(hit, fresh, 0.0)
+            for c in range(2):
+                change = inner_change(z, cut, vel_y, q_ref[c], f_ref[c], x_ref[c])
+                fresh = vel[c, z, :, cut] + weight * change
+                new_ref[c, z, :, cut] = fresh
+                sums[2 * k + c] = sums[2 * k + c] + jnp.where(hit, fresh, 0.0)
         return tuple(sums)
 
-    sums = lax.fori_loop(0, layers, update, tuple(sums), unroll=1 if with_shear else 2)
-    if not with_shear:
-        return
+    sums = lax.fori_loop(0, layers, update, tuple(sums))
     for k in range(lanes):
         cut = slice(k * LANE, (k + 1) * LANE)
         scale = 1.0 / (0.5 + flat[1, :, cut])
@@ -759,20 +773,17 @@
     got_b = lax.ppermute(send_b, ("plane", "wall"), plane_b)
     got_a = lax.ppermute(send_a, ("plane", "wall"), plane_a)
 
-    def inner(comps, more, flops):
-        count = len(comps)
-        deep = pltpu.VMEM((count, layers + 4, rows, cols), jnp.float32)
-        return call(
-            functools.partial(inner_kernel, layers, comps),
-            [(count, layers, rows, cols)] + more,
-            [vel, flat, band],
-            [deep, deep, pltpu.VMEM((count, layers * rows, 4 * cols), jnp.bfloat16)]
-            + [pltpu.VMEM((count, layers * rows, cols), jnp.float32)],
-            flops=flops,
-            moved=3_000_000,
-        )
-
-    new, shear, edge = inner((0, 1), [(2, rows, cols), (2, 5, tiles, SUB, LANE)], 20_000_000)
+    deep = (layers + 4, rows, cols)
+    flat_rows = (layers * rows, cols)
+    new, shear, edge, third_q, third_f, third_x = call(
+        functools.partial(inner_kernel, layers),
+        [(2, layers, rows, cols), (2, rows, cols), (2, 5, tiles, SUB, LANE), deep, deep, flat_rows],
+        [vel, flat, band],
+        [pltpu.VMEM((2,) + deep, jnp.float32)] * 2
+        + [pltpu.VMEM((3, layers * rows, 4 * cols), jnp.bfloat16), pltpu.VMEM((2,) + flat_rows, jnp.float32)],
+        flops=20_000_000,
+        moved=3_000_000,
+    )
     span_lists = [p for p in pairings("span") if p]
     message = (2 * tall + 1 + (3 if bed_in else 0), SUB, LANE)
     unpacked = call(
@@ -787,7 +798,13 @@
     messages = unpacked[5:]
     got = [lax.ppermute(m, "span", pairs) for m, pairs in zip(messages, span_lists)]
     shallow = pltpu.VMEM((2, layers + 4, SUB, cols), jnp.float32)
-    (new_z,) = inner((2,), [], 10_000_000)
+    (new_z,) = call(
+        functools.partial(third_kernel, layers),
+        [(1, layers, rows, cols)],
+        [vel, flat, third_q, third_f, third_x],
+        flops=5_000_000,
+        moved=2_000_000,
+    )
     fix, strip_shear, send_z = call(
         functools.partial(strip_kernel, layers),
         [sheet, (2, 2, SUB, cols), (3, 2, rows, cols)],

time: 17 us -> 17 us (level)
  starting transfers between devices: 5.15 us -> 5.92 us
  waiting for transfers between devices: 1.3 us -> 0.76 us
  Pallas kernels: 9.74 us -> 9.45 us
    ppermute x1, starting transfers between devices: 0.3 us -> 1.08 us  [body(): theirs = lax.ppermute(mine, 'wall', pairings('wall')[0])]
    ppermute x1, waiting for transfers between devices: 1.15 us -> 0.75 us  [body(): got_b = lax.ppermute(send_b, ('plane', 'wall'), plane_b)]
    pallas_call x8, Pallas kernels: 9.74 us -> 9.45 us  [call(): pl.pallas_call(kernel, out_shape=shapes, in_specs=specs, out_specs=[pl.Bl...]
  transfers between devices with their start and end apart: 5 -> 5, of which waited for: 3 -> 1; matrix products, arithmetic and copies ran while one was open for 0% -> 0% of each run, Pallas kernels for 42% -> 40%
where the time goes in v8:
time: 17 us; the launch traced here: 16.8 us
  Pallas kernels  9.45 us (56%)
  starting transfers between devices  5.92 us (35%)
  waiting for transfers between devices  0.76 us (4%)
  between operations  0.68 us (4%)
    pallas_call x8, Pallas kernels, call(): pl.pallas_call(kernel, out_shape=shapes, in_specs=specs, out_specs=[pl.Bl...  9.45 us
    ppermute x1, starting transfers between devices, body(): got_z = lax.ppermute(send_z, 'wall', pairings('wall')[0])  2.22 us
    ppermute x1, starting transfers between devices, body(): got_a = lax.ppermute(send_a, ('plane', 'wall'), plane_a)  1.36 us
    ppermute x1, starting transfers between devices, body(): lax.ppermute(m, 'span', pairs)  1.25 us
    ppermute x1, starting transfers between devices, body(): theirs = lax.ppermute(mine, 'wall', pairings('wall')[0])  1.08 us
    ppermute x1, waiting for transfers between devices, body(): got_b = lax.ppermute(send_b, ('plane', 'wall'), plane_b)  0.75 us
  transfers between devices with their start and end apart: 5, of which 1 were waited for; matrix products, arithmetic and copies ran while one was open for 0% of the time, Pallas kernels for 40%

profile of v8, /device:TPU:17, one launch (start us, length us, event | category | flops | bytes accessed | tf_op | source)
XLA Modules:
  0.0 16.8 jit_solution(1942293291662196096)
XLA Ops:
  0.6 1.5 %shard_map.59 = (f32[14,8,256]{2,1,0:T(8,128)S(1)}, f32[14,8,256]{2,1,0:T(8,128)S(1)}, f32[3,16,32,256]{3,2,1,0:T(8,128)S(1)}, f32[2,32,256]{2,1,0:T(8,128)S(1)}...) custom-call(f32[3,16,32,256]{3,2,1,0:T(8,128)} %vel_in.1, s32[32,256]{1,0:T(8,128)} %lev_in.1, f32[32,256]{1,0:T(8,128)} %frac_in.1, ...), custom_call_target="tpu_custom_call" | custom-call | bytes 1000000 | tf_op jit(solution)/shard_map/pallas_call | solution.py:25
  2.1 1.4 %collective-permute-start = (f32[14,8,256]{2,1,0:T(8,128)S(1)}, f32[14,8,256]{2,1,0:T(8,128)S(1)}, u32[]{:S(2)}, u32[]{:S(2)}) collective-permute-start(f32[14,8,256]{2,1,0:T(8,128)S(1)} %get-tuple-element.32), channel_id=1, source_target_pairs={{0,4},{1,5},{4,0},{5,1},{8,12},{9,13},{12,8},{13,9},{2,6},{3,7},{6... | collective-permute-start | bytes 344072 | tf_op jit(solution)/shard_map/ppermute | solution.py:774
  3.5 0.0 collective-permute-start.1
  3.5 3.1 %shard_map.60 = (f32[2,16,32,256]{3,2,1,0:T(8,128)S(1)}, f32[2,32,256]{2,1,0:T(8,128)S(1)}, f32[2,5,4,8,128]{4,3,2,1,0:T(8,128)S(1)}, f32[20,32,256]{2,1,0:T(8,1...) custom-call(f32[3,16,32,256]{3,2,1,0:T(8,128)S(1)} %get-tuple-element.25.vel, ...), custom_call_target="tpu_custom_call" | custom-call | flops 20000000 | bytes 3000000 | tf_op jit(solution)/shard_map/pallas_call | solution.py:25
  6.6 0.0 collective-permute-done.got_a
  6.6 0.7 %collective-permute-done.1.got_b = f32[14,8,256]{2,1,0:T(8,128)S(1)} collective-permute-done((f32[14,8,256]{2,1,0:T(8,128)S(1)}, f32[14,8,256]{2,1,0:T(8,128)S(1)}, u32[]{:S(2)}, u32[]{:S(2)}) %collective-permute-start.1) | collective-permute-done | bytes 114720 | tf_op jit(solution)/shard_map/ppermute | solution.py:773
  7.4 0.4 %shard_map.62 = (f32[3,16,8,256]{3,2,1,0:T(8,128)S(1)}, f32[4,8,256]{2,1,0:T(8,128)S(1)}, f32[2,25,8,128]{3,2,1,0:T(8,128)S(1)}, f32[2,8,128]{2,1,0:T(8,128)S(1)...) custom-call(f32[14,8,256]{2,1,0:T(8,128)S(1)} %collective-permute-done.got_a, ...), custom_call_target="tpu_custom_call" | custom-call | bytes 1000000 | tf_op jit(solution)/shard_map/pallas_call | solution.py:25
  7.7 1.3 %collective-permute-start.2 = (f32[14,8,128]{2,1,0:T(8,128)S(1)}, f32[14,8,128]{2,1,0:T(8,128)S(1)}, u32[]{:S(2)}, u32[]{:S(2)}) collective-permute-start(f32[14,8,128]{2,1,0:T(8,128)S(1)} %get-tuple-element.43), channel_id=1, source_target_pairs={{0,2},{2,0},{1,3},{3,1},{4,6},{6,4},{5,7},{7,5},{8,10},{10,8},{9,1... | collective-permute-start | bytes 172040 | tf_op jit(solution)/shard_map/ppermute | solution.py:799
  9.0 0.6 %shard_map.61.new_z.rest_2_ = f32[1,16,32,256]{3,2,1,0:T(8,128)S(1)} custom-call(f32[3,16,32,256]{3,2,1,0:T(8,128)S(1)} %get-tuple-element.25.vel, f32[2,32,256]{2,1,0:T(8,128)S(1)} %get-tuple-element.26.flat, f32[20,32,256]{2,1,0:T(8,128)S(1)} %get-tuple-element.29.q_ref, f32[20,32,256]{2,1,0:T(8,128)S(1)} %get-tuple-element.30.f_ref, ...), custom_call_target="tpu_custom_call" | custom-call | flops 5000000 | bytes 2000000 | tf_op jit(solution)/shard_map/pallas_call | solution.py:25
  9.6 1.0 %shard_map.63 = (f32[3,16,8,256]{3,2,1,0:T(8,128)S(1)}, f32[2,2,8,256]{3,2,1,0:T(8,128)S(1)}, f32[3,2,32,256]{3,2,1,0:T(8,128)S(1)}) custom-call(f32[3,16,32,256]{3,2,1,0:T(8,128)S(1)} %get-tuple-element.25.vel, f32[2,32,256]{2,1,0:T(8,128)S(1)} %get-tuple-element.26.flat, f32[3,16,8,256]{3,2,1,0:T(8,128)S(1)} %get-tuple-element.36.halo, ...), custom_call_target="tpu_custom_call" | custom-call | flops 10000000 | bytes 2000000 | tf_op jit(solution)/shard_map/pallas_call | solution.py:25
  10.6 2.2 %collective-permute-start.3 = (f32[3,2,32,256]{3,2,1,0:T(8,128)S(1)}, f32[3,2,32,256]{3,2,1,0:T(8,128)S(1)}, u32[]{:S(2)}, u32[]{:S(2)}) collective-permute-start(f32[3,2,32,256]{3,2,1,0:T(8,128)S(1)} %get-tuple-element.46), channel_id=1, source_target_pairs={{0,1},{1,0},{2,3},{3,2},{4,5},{5,4},{6,7},{7,6},{8,9},{9,8},{10,11... | collective-permute-start | bytes 589832 | tf_op jit(solution)/shard_map/ppermute | solution.py:817
  12.8 0.0 collective-permute-done.2.rest_0_
  12.8 0.7 %shard_map.64 = (f32[3,32,128]{2,1,0:T(8,128)S(1)}, f32[42,8,128]{2,1,0:T(8,128)S(1)}) custom-call(f32[2,25,8,128]{3,2,1,0:T(8,128)S(1)} %get-tuple-element.39.full, f32[2,8,128]{2,1,0:T(8,128)S(1)} %get-tuple-element.40.far, f32[2,32,256]{2,1,0:T(8,128)S(1)} %get-tuple-element.41.shear, f32[2,2,8,256]{3,2,1,0:T(8,128)S(1)} %get-tuple-element.42.strips, ...), custom_call_target="tpu_custom_call" | custom-call | bytes 1000000 | tf_op jit(solution)/shard_map/pallas_call | solution.py:25
  13.5 1.1 %collective-permute-start.4 = (f32[42,8,128]{2,1,0:T(8,128)S(1)}, f32[42,8,128]{2,1,0:T(8,128)S(1)}, u32[]{:S(2)}, u32[]{:S(2)}) collective-permute-start(f32[42,8,128]{2,1,0:T(8,128)S(1)} %get-tuple-element.47.mine), channel_id=1, source_target_pairs={{0,1},{1,0},{2,3},{3,2},{4,5},{5,4},{6,7},{7,6},{8,9},{9,8},{10,11... | collective-permute-start | bytes 516104 | tf_op jit(solution)/shard_map/ppermute | solution.py:828
  14.6 0.0 collective-permute-done.3.far
  14.6 1.4 %shard_map.65 = f32[3,16,32,256]{3,2,1,0:T(8,128)} custom-call(f32[2,16,32,256]{3,2,1,0:T(8,128)S(1)} %get-tuple-element.28.new, f32[1,16,32,256]{3,2,1,0:T(8,128)S(1)} %shard_map.61.new_z.rest_2_, f32[3,16,8,256]{3,2,1,0:T(8,128)S(1)} %get-tuple-element.38.fix, f32[3,32,128]{2,1,0:T(8,128)S(1)} %get-tuple-element.45.fresh, ...), custom_call_target="tpu_custom_call" | custom-call | flops 2000000 | bytes 4000000 | tf_op jit(solution)/shard_map/pallas_call | solution.py:25
  15.9 0.0 collective-permute-done.4.theirs
  15.9 0.9 %shard_map.66 = f32[32,256]{1,0:T(8,128)} custom-call(f32[42,8,128]{2,1,0:T(8,128)S(1)} %get-tuple-element.47.mine, f32[42,8,128]{2,1,0:T(8,128)S(1)} %collective-permute-done.4.theirs), custom_call_target="tpu_custom_call" | custom-call | bytes 1000000 | tf_op jit(solution)/shard_map/pallas_call | solution.py:25
Async XLA Ops:
  2.1 4.5 %collective-permute-start = (f32[14,8,256]{2,1,0:T(8,128)S(1)}, f32[14,8,256]{2,1,0:T(8,128)S(1)}, u32[]{:S(2)}, u32[]{:S(2)}) collective-permute-start(f32[14,8,256]{2,1,0:T(8,128)S(1)} %get-tuple-element.32), channel_id=1, source_target_pairs={{0,4},{1,5},{4,0},{5,1},{8,12},{9,13},{12,8},{13,9},{2,6},{3,7},{6... | collective-permute-start | bytes 344072 | tf_op jit(solution)/shard_map/ppermute | solution.py:774
  3.5 3.9 %collective-permute-start.1 = (f32[14,8,256]{2,1,0:T(8,128)S(1)}, f32[14,8,256]{2,1,0:T(8,128)S(1)}, u32[]{:S(2)}, u32[]{:S(2)}) collective-permute-start(f32[14,8,256]{2,1,0:T(8,128)S(1)} %get-tuple-element.33), channel_id=1, source_target_pairs={{0,1},{1,0},{4,8},{5,9},{8,4},{9,5},{12,13},{13,12},{2,3},{3,2},{6... | collective-permute-start | bytes 344072 | tf_op jit(solution)/shard_map/ppermute | solution.py:773
  7.7 5.1 %collective-permute-start.2 = (f32[14,8,128]{2,1,0:T(8,128)S(1)}, f32[14,8,128]{2,1,0:T(8,128)S(1)}, u32[]{:S(2)}, u32[]{:S(2)}) collective-permute-start(f32[14,8,128]{2,1,0:T(8,128)S(1)} %get-tuple-element.43), channel_id=1, source_target_pairs={{0,2},{2,0},{1,3},{3,1},{4,6},{6,4},{5,7},{7,5},{8,10},{10,8},{9,1... | collective-permute-start | bytes 172040 | tf_op jit(solution)/shard_map/ppermute | solution.py:799
  10.6 4.0 %collective-permute-start.3 = (f32[3,2,32,256]{3,2,1,0:T(8,128)S(1)}, f32[3,2,32,256]{3,2,1,0:T(8,128)S(1)}, u32[]{:S(2)}, u32[]{:S(2)}) collective-permute-start(f32[3,2,32,256]{3,2,1,0:T(8,128)S(1)} %get-tuple-element.46), channel_id=1, source_target_pairs={{0,1},{1,0},{2,3},{3,2},{4,5},{5,4},{6,7},{7,6},{8,9},{9,8},{10,11... | collective-permute-start | bytes 589832 | tf_op jit(solution)/shard_map/ppermute | solution.py:817
  13.5 2.4 %collective-permute-start.4 = (f32[42,8,128]{2,1,0:T(8,128)S(1)}, f32[42,8,128]{2,1,0:T(8,128)S(1)}, u32[]{:S(2)}, u32[]{:S(2)}) collective-permute-start(f32[42,8,128]{2,1,0:T(8,128)S(1)} %get-tuple-element.47.mine), channel_id=1, source_target_pairs={{0,1},{1,0},{2,3},{3,2},{4,5},{5,4},{6,7},{7,6},{8,9},{9,8},{10,11... | collective-permute-start | bytes 516104 | tf_op jit(solution)/shard_map/ppermute | solution.py:828

commit v9 on v8

--- a/solution.py
+++ b/solution.py
@@ -295,7 +295,11 @@
     return inside + [jnp.where(first, after, before)]
 
 
-def unpack_kernel(layers, bed_in, got_a, got_b, edge, bed, halo_ref, beside_ref, full_ref, far_ref, bed_ref, *messages):
+def unpack_kernel(layers, bed_in, got_a, got_b, edge, bed, vel, halo_ref, beside_ref, full_ref, far_ref, bed_ref, z_ref, *messages):
+    start = jnp.where(lax.axis_index("wall") == 0, layers - 2, 0)
+    for c in range(3):
+        for z in range(2):
+            z_ref[c, z] = vel[c, start + z]
     cols = halo_ref.shape[3]
     tiles = edge.shape[2]
     tall = tiles + 1
@@ -379,7 +383,7 @@
         bed_ref[0] = jnp.zeros((SUB, LANE), jnp.float32)
 
 
-def strip_kernel(layers, vel, flat, halo, beside, new_z, fix_ref, shear_ref, z_ref, q_ref, f_ref):
+def strip_kernel(layers, spans, vel, flat, halo, beside, full, far, new_z, fix_ref, shear_ref, face_ref, q_ref, f_ref):
     _, rows, cols = flat.shape
     base = lax.axis_index("wall") * layers
     shape = (SUB, cols)
@@ -460,10 +464,12 @@
     for c in range(2):
         shear_ref[0, c] = jnp.where(low | high, sums[c] * scale, 0.0)
         shear_ref[1, c] = sums[2 + c] * own_scale
-    start = jnp.where(lax.axis_index("wall") == 0, layers - 2, 0)
-    for c in range(3):
-        for z in range(2):
-            z_ref[c, z] = vel[c, start + z]
+    if spans == 1:
+        fresh, shear = face_strip(full, far, jnp.logical_not(even("span")), None, base, layers)
+        for n, value in enumerate(fresh + shear):
+            face_ref[n] = value
+    else:
+        face_ref[...] = jnp.zeros(face_ref.shape, jnp.float32)
 
 
 def column_strip(vel, levels, fraction, extra, base, layers):
@@ -502,7 +508,35 @@
     return fresh, shear
 
 
-def side_kernel(layers, spans, bed_in, full, far, shear, strips, *rest):
+def side_columns(shape, right):
+    column = lax.rem(iota(shape, 1), 2 * EDGE)
+    return jnp.where(right, column, 2 * EDGE - 1 - column)
+
+
+def face_strip(full, far, right, got, base, layers):
+    tall = full.shape[1] // 5
+    shape = (tall * SUB, LANE)
+
+    def own(n):
+        return jnp.where(right, full[0, n], full[1, n])
+
+    fields = [jnp.concatenate([own(n * tall + t) for t in range(tall)], axis=0) for n in range(5)]
+    extra = jnp.where(right, far[0], far[1])
+    if got is not None:
+        given = side_columns(shape, right) >= EDGE
+        alternate = lax.rem(iota(shape, 1) // (2 * EDGE), 2)
+        both = [jnp.concatenate([got[2 * t + i] for t in range(tall)], axis=0) for i in range(2)]
+        turned = [jnp.where(right, pltpu.roll(b, EDGE, 1), pltpu.roll(b, LANE - EDGE, 1)) for b in both]
+        turned = [jnp.where(given, b, 0.0) for b in turned]
+        theirs = [jnp.where(given, both[0], 0.0), turned[0], jnp.where(given, both[1], 0.0)]
+        theirs.append(jnp.where(alternate == 0, turned[1], pltpu.roll(turned[1], 2 * EDGE, 1)))
+        theirs.append(jnp.where(alternate == 1, turned[1], ahead(turned[1], 2 * EDGE, 1)))
+        fields = [a + b for a, b in zip(fields, theirs)]
+        extra = extra + got[2 * tall]
+    return column_strip(fields[:3], fields[3], fields[4], extra, base, layers)
+
+
+def side_kernel(layers, spans, bed_in, full, far, shear, strips, face, *rest):
     got = rest[:spans]
     rest = rest[spans:]
     own_bed = rest[0]
@@ -512,33 +546,18 @@
     tall = tiles + 1
     base = lax.axis_index("wall") * layers
     right_first = even("span")
-    results = []
-    column = lax.rem(iota((tall * SUB, LANE), 1), 2 * EDGE)
-    alternate = lax.rem(iota((tall * SUB, LANE), 1) // (2 * EDGE), 2)
-    fresh_sides = []
-    for side in range(2):
-        first = right_first if side == 0 else jnp.logical_not(right_first)
-
-        def other(n):
-            return jnp.where(first, got[0][n], got[1][n] if spans > 1 else 0.0)
-
-        given = column >= EDGE if side == 0 else column < EDGE
-        back = EDGE if side == 0 else LANE - EDGE
-        both = [jnp.concatenate([other(2 * t + i) for t in range(tall)], axis=0) for i in range(2)]
-        turned = [jnp.where(given, pltpu.roll(b, back, 1), 0.0) for b in both]
-        theirs = [jnp.where(given, both[0], 0.0), turned[0], jnp.where(given, both[1], 0.0)]
-        theirs.append(jnp.where(alternate == 0, turned[1], pltpu.roll(turned[1], 2 * EDGE, 1)))
-        theirs.append(jnp.where(alternate == 1, turned[1], ahead(turned[1], 2 * EDGE, 1)))
-        fields = []
-        for n in range(5):
-            own = full[side, n * tall : (n + 1) * tall].reshape(tall * SUB, LANE)
-            fields.append(own + theirs[n])
-        extra = far[side] + other(2 * tall)
-        fresh, edge_shear = column_strip(fields[:3], fields[3], fields[4], extra, base, layers)
-        fresh_sides.append(fresh)
-        results.append(edge_shear)
+    fresh, first = face_strip(full, far, right_first, got[0], base, layers)
+    if spans > 1:
+        other_fresh, second = face_strip(full, far, jnp.logical_not(right_first), got[1], base, layers)
+    else:
+        other_fresh, second = [face[n] for n in range(3)], [face[3], face[4]]
+    is_first = side_columns((tall * SUB, LANE), right_first) < EDGE
     for c in range(3):
-        fresh_ref[c] = jnp.where(column < EDGE, fresh_sides[0][c], fresh_sides[1][c])[:rows]
+        fresh_ref[c] = jnp.where(is_first, fresh[c], other_fresh[c])[:rows]
+    results = [
+        [jnp.where(right_first, a, b) for a, b in zip(first, second)],
+        [jnp.where(right_first, b, a) for a, b in zip(first, second)],
+    ]
     lane = iota((SUB, LANE), 1)
     sub = iota((SUB, LANE), 0)
     lanes = cols // LANE
@@ -788,14 +807,14 @@
     message = (2 * tall + 1 + (3 if bed_in else 0), SUB, LANE)
     unpacked = call(
         functools.partial(unpack_kernel, layers, bed_in),
-        [sheet, (4, SUB, cols), (2, 5 * tall, SUB, LANE), (2, SUB, LANE), (6, SUB, LANE)]
+        [sheet, (4, SUB, cols), (2, 5 * tall, SUB, LANE), (2, SUB, LANE), (6, SUB, LANE), (3, 2, rows, cols)]
         + [message] * len(span_lists),
-        [got_a, got_b, edge, bed],
+        [got_a, got_b, edge, bed, vel],
         moved=1_000_000,
         limit=10,
     )
-    halo, beside, full, far, own_bed = unpacked[:5]
-    messages = unpacked[5:]
+    halo, beside, full, far, own_bed, send_z = unpacked[:6]
+    messages = unpacked[6:]
     got = [lax.ppermute(m, "span", pairs) for m, pairs in zip(messages, span_lists)]
     shallow = pltpu.VMEM((2, layers + 4, SUB, cols), jnp.float32)
     (new_z,) = call(
@@ -805,12 +824,12 @@
         flops=5_000_000,
         moved=2_000_000,
     )
-    fix, strip_shear, send_z = call(
-        functools.partial(strip_kernel, layers),
-        [sheet, (2, 2, SUB, cols), (3, 2, rows, cols)],
-        [vel, flat, halo, beside, new_z],
+    fix, strip_shear, face = call(
+        functools.partial(strip_kernel, layers, len(span_lists)),
+        [sheet, (2, 2, SUB, cols), (5, tall * SUB, LANE)],
+        [vel, flat, halo, beside, full, far, new_z],
         [shallow, shallow],
-        any_inputs=(4,),
+        any_inputs=(6,),
         flops=10_000_000,
         moved=2_000_000,
     )
@@ -820,8 +839,8 @@
     fresh, mine = call(
         functools.partial(side_kernel, layers, len(got), bed_in),
         [(3, rows, LANE), (out_count, SUB, LANE)],
-        [full, far, shear, strip_shear] + got + [own_bed, new_z],
-        any_inputs=(5 + len(got),),
+        [full, far, shear, strip_shear, face] + got + [own_bed, new_z],
+        any_inputs=(6 + len(got),),
         moved=1_000_000,
         limit=10,
     )

time: 17 us -> 16.9 us (level)
  starting transfers between devices: 5.92 us -> 5.52 us
  Pallas kernels: 9.45 us -> 9.74 us
    ppermute x1, starting transfers between devices: 1.08 us -> 0.75 us  [body(): theirs = lax.ppermute(mine, 'wall', pairings('wall')[0])]
    pallas_call x8, Pallas kernels: 9.45 us -> 9.74 us  [call(): pl.pallas_call(kernel, out_shape=shapes, in_specs=specs, out_specs=[pl.Bl...]
  transfers between devices with their start and end apart: 5 -> 5, of which waited for: 1 -> 1; matrix products, arithmetic and copies ran while one was open for 0% -> 0% of each run, Pallas kernels for 40% -> 42%
where the time goes in v9:
time: 16.9 us; the launch traced here: 16.7 us
  Pallas kernels  9.74 us (58%)
  starting transfers between devices  5.52 us (33%)
  waiting for transfers between devices  0.76 us (4%)
  between operations  0.7 us (4%)
    pallas_call x8, Pallas kernels, call(): pl.pallas_call(kernel, out_shape=shapes, in_specs=specs, out_specs=[pl.Bl...  9.74 us
    ppermute x1, starting transfers between devices, body(): got_z = lax.ppermute(send_z, 'wall', pairings('wall')[0])  2.16 us
    ppermute x1, starting transfers between devices, body(): got_a = lax.ppermute(send_a, ('plane', 'wall'), plane_a)  1.36 us
    ppermute x1, starting transfers between devices, body(): lax.ppermute(m, 'span', pairs)  1.25 us
    ppermute x1, waiting for transfers between devices, body(): got_b = lax.ppermute(send_b, ('plane', 'wall'), plane_b)  0.75 us
    ppermute x1, starting transfers between devices, body(): theirs = lax.ppermute(mine, 'wall', pairings('wall')[0])  0.75 us
  transfers between devices with their start and end apart: 5, of which 1 were waited for; matrix products, arithmetic and copies ran while one was open for 0% of the time, Pallas kernels for 42%

profile of v9, /device:TPU:17, one launch (start us, length us, event | category | flops | bytes accessed | tf_op | source)
XLA Modules:
  0.0 16.7 jit_solution(8385155372899786029)
XLA Ops:
  0.6 1.5 %shard_map.59 = (f32[14,8,256]{2,1,0:T(8,128)S(1)}, f32[14,8,256]{2,1,0:T(8,128)S(1)}, f32[3,16,32,256]{3,2,1,0:T(8,128)S(1)}, f32[2,32,256]{2,1,0:T(8,128)S(1)}...) custom-call(f32[3,16,32,256]{3,2,1,0:T(8,128)} %vel_in.1, s32[32,256]{1,0:T(8,128)} %lev_in.1, f32[32,256]{1,0:T(8,128)} %frac_in.1, ...), custom_call_target="tpu_custom_call" | custom-call | bytes 1000000 | tf_op jit(solution)/shard_map/pallas_call | solution.py:25
  2.1 1.4 %collective-permute-start = (f32[14,8,256]{2,1,0:T(8,128)S(1)}, f32[14,8,256]{2,1,0:T(8,128)S(1)}, u32[]{:S(2)}, u32[]{:S(2)}) collective-permute-start(f32[14,8,256]{2,1,0:T(8,128)S(1)} %get-tuple-element.33), channel_id=1, source_target_pairs={{0,4},{1,5},{4,0},{5,1},{8,12},{9,13},{12,8},{13,9},{2,6},{3,7},{6... | collective-permute-start | bytes 344072 | tf_op jit(solution)/shard_map/ppermute | solution.py:793
  3.5 0.0 collective-permute-start.1
  3.5 3.1 %shard_map.60 = (f32[2,16,32,256]{3,2,1,0:T(8,128)S(1)}, f32[2,32,256]{2,1,0:T(8,128)S(1)}, f32[2,5,4,8,128]{4,3,2,1,0:T(8,128)S(1)}, f32[20,32,256]{2,1,0:T(8,1...) custom-call(f32[3,16,32,256]{3,2,1,0:T(8,128)S(1)} %get-tuple-element.26.vel, ...), custom_call_target="tpu_custom_call" | custom-call | flops 20000000 | bytes 3000000 | tf_op jit(solution)/shard_map/pallas_call | solution.py:25
  6.6 0.0 collective-permute-done.got_a
  6.6 0.7 %collective-permute-done.1.got_b = f32[14,8,256]{2,1,0:T(8,128)S(1)} collective-permute-done((f32[14,8,256]{2,1,0:T(8,128)S(1)}, f32[14,8,256]{2,1,0:T(8,128)S(1)}, u32[]{:S(2)}, u32[]{:S(2)}) %collective-permute-start.1) | collective-permute-done | bytes 114720 | tf_op jit(solution)/shard_map/ppermute | solution.py:792
  7.4 0.4 %shard_map.62 = (f32[3,16,8,256]{3,2,1,0:T(8,128)S(1)}, f32[4,8,256]{2,1,0:T(8,128)S(1)}, f32[2,25,8,128]{3,2,1,0:T(8,128)S(1)}, f32[2,8,128]{2,1,0:T(8,128)S(1)...) custom-call(f32[14,8,256]{2,1,0:T(8,128)S(1)} %collective-permute-done.got_a, ...), custom_call_target="tpu_custom_call" | custom-call | bytes 1000000 | tf_op jit(solution)/shard_map/pallas_call | solution.py:25
  7.7 1.3 %collective-permute-start.2 = (f32[14,8,128]{2,1,0:T(8,128)S(1)}, f32[14,8,128]{2,1,0:T(8,128)S(1)}, u32[]{:S(2)}, u32[]{:S(2)}) collective-permute-start(f32[14,8,128]{2,1,0:T(8,128)S(1)} %get-tuple-element.45), channel_id=1, source_target_pairs={{0,2},{2,0},{1,3},{3,1},{4,6},{6,4},{5,7},{7,5},{8,10},{10,8},{9,1... | collective-permute-start | bytes 172040 | tf_op jit(solution)/shard_map/ppermute | solution.py:818
  9.0 2.2 %collective-permute-start.3 = (f32[3,2,32,256]{3,2,1,0:T(8,128)S(1)}, f32[3,2,32,256]{3,2,1,0:T(8,128)S(1)}, u32[]{:S(2)}, u32[]{:S(2)}) collective-permute-start(f32[3,2,32,256]{3,2,1,0:T(8,128)S(1)} %get-tuple-element.48), channel_id=1, source_target_pairs={{0,1},{1,0},{2,3},{3,2},{4,5},{5,4},{6,7},{7,6},{8,9},{9,8},{10,11... | collective-permute-start | bytes 589832 | tf_op jit(solution)/shard_map/ppermute | solution.py:836
  11.1 0.6 %shard_map.61.new_z.rest_2_ = f32[1,16,32,256]{3,2,1,0:T(8,128)S(1)} custom-call(f32[3,16,32,256]{3,2,1,0:T(8,128)S(1)} %get-tuple-element.26.vel, f32[2,32,256]{2,1,0:T(8,128)S(1)} %get-tuple-element.27.flat, f32[20,32,256]{2,1,0:T(8,128)S(1)} %get-tuple-element.30.q_ref, f32[20,32,256]{2,1,0:T(8,128)S(1)} %get-tuple-element.31.f_ref, ...), custom_call_target="tpu_custom_call" | custom-call | flops 5000000 | bytes 2000000 | tf_op jit(solution)/shard_map/pallas_call | solution.py:25
  11.8 1.4 %shard_map.63 = (f32[3,16,8,256]{3,2,1,0:T(8,128)S(1)}, f32[2,2,8,256]{3,2,1,0:T(8,128)S(1)}, f32[5,40,128]{2,1,0:T(8,128)S(1)}) custom-call(f32[3,16,32,256]{3,2,1,0:T(8,128)S(1)} %get-tuple-element.26.vel, f32[2,32,256]{2,1,0:T(8,128)S(1)} %get-tuple-element.27.flat, f32[3,16,8,256]{3,2,1,0:T(8,128)S(1)} %get-tuple-element.37.halo, ...), custom_call_target="tpu_custom_call" | custom-call | flops 10000000 | bytes 2000000 | tf_op jit(solution)/shard_map/pallas_call | solution.py:25
  13.1 0.0 collective-permute-done.2.rest_0_
  13.1 0.6 %shard_map.64 = (f32[3,32,128]{2,1,0:T(8,128)S(1)}, f32[42,8,128]{2,1,0:T(8,128)S(1)}) custom-call(f32[2,25,8,128]{3,2,1,0:T(8,128)S(1)} %get-tuple-element.39.full, f32[2,8,128]{2,1,0:T(8,128)S(1)} %get-tuple-element.40.far, f32[2,32,256]{2,1,0:T(8,128)S(1)} %get-tuple-element.42.shear, f32[2,2,8,256]{3,2,1,0:T(8,128)S(1)} %get-tuple-element.43.strips, ...), custom_call_target="tpu_custom_call" | custom-call | bytes 1000000 | tf_op jit(solution)/shard_map/pallas_call | solution.py:25
  13.7 0.7 %collective-permute-start.4 = (f32[42,8,128]{2,1,0:T(8,128)S(1)}, f32[42,8,128]{2,1,0:T(8,128)S(1)}, u32[]{:S(2)}, u32[]{:S(2)}) collective-permute-start(f32[42,8,128]{2,1,0:T(8,128)S(1)} %get-tuple-element.49.mine), channel_id=1, source_target_pairs={{0,1},{1,0},{2,3},{3,2},{4,5},{5,4},{6,7},{7,6},{8,9},{9,8},{10,11... | collective-permute-start | bytes 516104 | tf_op jit(solution)/shard_map/ppermute | solution.py:847
  14.5 0.0 collective-permute-done.3.far
  14.5 1.4 %shard_map.65 = f32[3,16,32,256]{3,2,1,0:T(8,128)} custom-call(f32[2,16,32,256]{3,2,1,0:T(8,128)S(1)} %get-tuple-element.29.new, f32[1,16,32,256]{3,2,1,0:T(8,128)S(1)} %shard_map.61.new_z.rest_2_, f32[3,16,8,256]{3,2,1,0:T(8,128)S(1)} %get-tuple-element.41.fix, f32[3,32,128]{2,1,0:T(8,128)S(1)} %get-tuple-element.47.fresh, ...), custom_call_target="tpu_custom_call" | custom-call | flops 2000000 | bytes 4000000 | tf_op jit(solution)/shard_map/pallas_call | solution.py:25
  15.9 0.0 collective-permute-done.4.theirs
  15.9 0.9 %shard_map.66 = f32[32,256]{1,0:T(8,128)} custom-call(f32[42,8,128]{2,1,0:T(8,128)S(1)} %get-tuple-element.49.mine, f32[42,8,128]{2,1,0:T(8,128)S(1)} %collective-permute-done.4.theirs), custom_call_target="tpu_custom_call" | custom-call | bytes 1000000 | tf_op jit(solution)/shard_map/pallas_call | solution.py:25
Async XLA Ops:
  2.1 4.5 %collective-permute-start = (f32[14,8,256]{2,1,0:T(8,128)S(1)}, f32[14,8,256]{2,1,0:T(8,128)S(1)}, u32[]{:S(2)}, u32[]{:S(2)}) collective-permute-start(f32[14,8,256]{2,1,0:T(8,128)S(1)} %get-tuple-element.33), channel_id=1, source_target_pairs={{0,4},{1,5},{4,0},{5,1},{8,12},{9,13},{12,8},{13,9},{2,6},{3,7},{6... | collective-permute-start | bytes 344072 | tf_op jit(solution)/shard_map/ppermute | solution.py:793
  3.5 3.9 %collective-permute-start.1 = (f32[14,8,256]{2,1,0:T(8,128)S(1)}, f32[14,8,256]{2,1,0:T(8,128)S(1)}, u32[]{:S(2)}, u32[]{:S(2)}) collective-permute-start(f32[14,8,256]{2,1,0:T(8,128)S(1)} %get-tuple-element.34), channel_id=1, source_target_pairs={{0,1},{1,0},{4,8},{5,9},{8,4},{9,5},{12,13},{13,12},{2,3},{3,2},{6... | collective-permute-start | bytes 344072 | tf_op jit(solution)/shard_map/ppermute | solution.py:792
  7.7 5.4 %collective-permute-start.2 = (f32[14,8,128]{2,1,0:T(8,128)S(1)}, f32[14,8,128]{2,1,0:T(8,128)S(1)}, u32[]{:S(2)}, u32[]{:S(2)}) collective-permute-start(f32[14,8,128]{2,1,0:T(8,128)S(1)} %get-tuple-element.45), channel_id=1, source_target_pairs={{0,2},{2,0},{1,3},{3,1},{4,6},{6,4},{5,7},{7,5},{8,10},{10,8},{9,1... | collective-permute-start | bytes 172040 | tf_op jit(solution)/shard_map/ppermute | solution.py:818
  9.0 5.5 %collective-permute-start.3 = (f32[3,2,32,256]{3,2,1,0:T(8,128)S(1)}, f32[3,2,32,256]{3,2,1,0:T(8,128)S(1)}, u32[]{:S(2)}, u32[]{:S(2)}) collective-permute-start(f32[3,2,32,256]{3,2,1,0:T(8,128)S(1)} %get-tuple-element.48), channel_id=1, source_target_pairs={{0,1},{1,0},{2,3},{3,2},{4,5},{5,4},{6,7},{7,6},{8,9},{9,8},{10,11... | collective-permute-start | bytes 589832 | tf_op jit(solution)/shard_map/ppermute | solution.py:836
  13.7 2.1 %collective-permute-start.4 = (f32[42,8,128]{2,1,0:T(8,128)S(1)}, f32[42,8,128]{2,1,0:T(8,128)S(1)}, u32[]{:S(2)}, u32[]{:S(2)}) collective-permute-start(f32[42,8,128]{2,1,0:T(8,128)S(1)} %get-tuple-element.49.mine), channel_id=1, source_target_pairs={{0,1},{1,0},{2,3},{3,2},{4,5},{5,4},{6,7},{7,6},{8,9},{9,8},{10,11... | collective-permute-start | bytes 516104 | tf_op jit(solution)/shard_map/ppermute | solution.py:847

commit v10 on v9

--- a/solution.py
+++ b/solution.py
@@ -59,17 +59,22 @@
     near = pltpu.roll(level, SUB - 1, 0) if forward else pltpu.roll(level, 1, 0)
     far = pltpu.roll(level, SUB - 2, 0) if forward else pltpu.roll(level, 2, 0)
     sign = 1.0 if forward else -1.0
-    one = [jnp.zeros(level.shape, jnp.float32)] * 2
-    two = list(one)
-    for z in range(layers):
+    blank = jnp.zeros(level.shape, jnp.float32)
+
+    def add(z, sums):
+        sums = list(sums)
         layer = (base + z).astype(jnp.float32)
         opened = opened_at(level, fraction, layer)
         near_hit, far_hit = near == layer, far == layer
         for c in range(2):
             q = opened * tile[c, z]
             flux = sign * (tile[1, z] * q)
-            one[c] = one[c] + jnp.where(near_hit, 6.0 * q + 8.0 * flux, 0.0)
-            two[c] = two[c] - jnp.where(far_hit, flux, 0.0)
+            sums[c] = sums[c] + jnp.where(near_hit, 6.0 * q + 8.0 * flux, 0.0)
+            sums[2 + c] = sums[2 + c] - jnp.where(far_hit, flux, 0.0)
+        return tuple(sums)
+
+    sums = lax.fori_loop(0, layers, add, (blank,) * 4, unroll=4)
+    one, two = sums[:2], sums[2:]
     sub = iota(level.shape, 0)
     source = SUB - 3 if forward else 2
     past = source - 1 if forward else source + 1
@@ -183,7 +188,11 @@
     return total + (6.0 * both - 8.0 * near + (f_ref[z + 4, :, cut] - f_ref[z, :, cut]))
 
 
-def third_kernel(layers, vel, flat, q_ref, f_ref, x_ref, new_ref):
+def third_kernel(layers, vel, flat, q_ref, f_ref, x_ref, new_ref, z_ref):
+    start = jnp.where(lax.axis_index("wall") == 0, layers - 2, 0)
+    for c in range(3):
+        for z in range(2):
+            z_ref[c, z] = vel[c, start + z]
     _, rows, cols = flat.shape
     base = lax.axis_index("wall") * layers
 
@@ -295,11 +304,7 @@
     return inside + [jnp.where(first, after, before)]
 
 
-def unpack_kernel(layers, bed_in, got_a, got_b, edge, bed, vel, halo_ref, beside_ref, full_ref, far_ref, bed_ref, z_ref, *messages):
-    start = jnp.where(lax.axis_index("wall") == 0, layers - 2, 0)
-    for c in range(3):
-        for z in range(2):
-            z_ref[c, z] = vel[c, start + z]
+def unpack_kernel(layers, bed_in, got_a, got_b, edge, bed, halo_ref, beside_ref, full_ref, far_ref, bed_ref, *messages):
     cols = halo_ref.shape[3]
     tiles = edge.shape[2]
     tall = tiles + 1
@@ -645,7 +650,7 @@
         copies[-1].start()
 
     for c in range(3):
-        for i in (0, 3, 1, 2):
+        for i in (1, 2, 0, 3):
             for z in range(i * part, (i + 1) * part):
                 merge(c, z)
             if i == 3:
@@ -807,19 +812,19 @@
     message = (2 * tall + 1 + (3 if bed_in else 0), SUB, LANE)
     unpacked = call(
         functools.partial(unpack_kernel, layers, bed_in),
-        [sheet, (4, SUB, cols), (2, 5 * tall, SUB, LANE), (2, SUB, LANE), (6, SUB, LANE), (3, 2, rows, cols)]
+        [sheet, (4, SUB, cols), (2, 5 * tall, SUB, LANE), (2, SUB, LANE), (6, SUB, LANE)]
         + [message] * len(span_lists),
-        [got_a, got_b, edge, bed, vel],
+        [got_a, got_b, edge, bed],
         moved=1_000_000,
         limit=10,
     )
-    halo, beside, full, far, own_bed, send_z = unpacked[:6]
-    messages = unpacked[6:]
+    halo, beside, full, far, own_bed = unpacked[:5]
+    messages = unpacked[5:]
     got = [lax.ppermute(m, "span", pairs) for m, pairs in zip(messages, span_lists)]
     shallow = pltpu.VMEM((2, layers + 4, SUB, cols), jnp.float32)
-    (new_z,) = call(
+    new_z, send_z = call(
         functools.partial(third_kernel, layers),
-        [(1, layers, rows, cols)],
+        [(1, layers, rows, cols), (3, 2, rows, cols)],
         [vel, flat, third_q, third_f, third_x],
         flops=5_000_000,
         moved=2_000_000,

time: 16.9 us -> 16.8 us (level)
  no operation moved by 1% of the time
where the time goes in v10:
time: 16.8 us; the launch traced here: 16.7 us
  Pallas kernels  9.69 us (58%)
  starting transfers between devices  5.53 us (33%)
  waiting for transfers between devices  0.76 us (5%)
  between operations  0.7 us (4%)
    pallas_call x8, Pallas kernels, call(): pl.pallas_call(kernel, out_shape=shapes, in_specs=specs, out_specs=[pl.Bl...  9.69 us
    ppermute x1, starting transfers between devices, body(): got_z = lax.ppermute(send_z, 'wall', pairings('wall')[0])  2.22 us
    ppermute x1, starting transfers between devices, body(): got_a = lax.ppermute(send_a, ('plane', 'wall'), plane_a)  1.36 us
    ppermute x1, starting transfers between devices, body(): lax.ppermute(m, 'span', pairs)  1.25 us
    ppermute x1, waiting for transfers between devices, body(): got_b = lax.ppermute(send_b, ('plane', 'wall'), plane_b)  0.75 us
    ppermute x1, starting transfers between devices, body(): theirs = lax.ppermute(mine, 'wall', pairings('wall')[0])  0.69 us
  transfers between devices with their start and end apart: 5, of which 1 were waited for; matrix products, arithmetic and copies ran while one was open for 0% of the time, Pallas kernels for 42%

profile of v10, /device:TPU:17, one launch (start us, length us, event | category | flops | bytes accessed | tf_op | source)
XLA Modules:
  0.0 16.7 jit_solution(776943238346667832)
XLA Ops:
  0.6 1.5 %shard_map.59 = (f32[14,8,256]{2,1,0:T(8,128)S(1)}, f32[14,8,256]{2,1,0:T(8,128)S(1)}, f32[3,16,32,256]{3,2,1,0:T(8,128)S(1)}, f32[2,32,256]{2,1,0:T(8,128)S(1)}...) custom-call(f32[3,16,32,256]{3,2,1,0:T(8,128)} %vel_in.1, s32[32,256]{1,0:T(8,128)} %lev_in.1, f32[32,256]{1,0:T(8,128)} %frac_in.1, ...), custom_call_target="tpu_custom_call" | custom-call | bytes 1000000 | tf_op jit(solution)/shard_map/pallas_call | solution.py:25
  2.1 1.4 %collective-permute-start = (f32[14,8,256]{2,1,0:T(8,128)S(1)}, f32[14,8,256]{2,1,0:T(8,128)S(1)}, u32[]{:S(2)}, u32[]{:S(2)}) collective-permute-start(f32[14,8,256]{2,1,0:T(8,128)S(1)} %get-tuple-element.35), channel_id=1, source_target_pairs={{0,4},{1,5},{4,0},{5,1},{8,12},{9,13},{12,8},{13,9},{2,6},{3,7},{6... | collective-permute-start | bytes 344072 | tf_op jit(solution)/shard_map/ppermute | solution.py:798
  3.5 0.0 collective-permute-start.1
  3.5 3.1 %shard_map.60 = (f32[2,16,32,256]{3,2,1,0:T(8,128)S(1)}, f32[2,32,256]{2,1,0:T(8,128)S(1)}, f32[2,5,4,8,128]{4,3,2,1,0:T(8,128)S(1)}, f32[20,32,256]{2,1,0:T(8,1...) custom-call(f32[3,16,32,256]{3,2,1,0:T(8,128)S(1)} %get-tuple-element.27.vel, ...), custom_call_target="tpu_custom_call" | custom-call | flops 20000000 | bytes 3000000 | tf_op jit(solution)/shard_map/pallas_call | solution.py:25
  6.6 0.0 collective-permute-done.got_a
  6.6 0.7 %collective-permute-done.1.got_b = f32[14,8,256]{2,1,0:T(8,128)S(1)} collective-permute-done((f32[14,8,256]{2,1,0:T(8,128)S(1)}, f32[14,8,256]{2,1,0:T(8,128)S(1)}, u32[]{:S(2)}, u32[]{:S(2)}) %collective-permute-start.1) | collective-permute-done | bytes 114720 | tf_op jit(solution)/shard_map/ppermute | solution.py:797
  7.4 0.4 %shard_map.62 = (f32[3,16,8,256]{3,2,1,0:T(8,128)S(1)}, f32[4,8,256]{2,1,0:T(8,128)S(1)}, f32[2,25,8,128]{3,2,1,0:T(8,128)S(1)}, f32[2,8,128]{2,1,0:T(8,128)S(1)...) custom-call(f32[14,8,256]{2,1,0:T(8,128)S(1)} %collective-permute-done.got_a, ...), custom_call_target="tpu_custom_call" | custom-call | bytes 1000000 | tf_op jit(solution)/shard_map/pallas_call | solution.py:25
  7.7 1.3 %collective-permute-start.2 = (f32[14,8,128]{2,1,0:T(8,128)S(1)}, f32[14,8,128]{2,1,0:T(8,128)S(1)}, u32[]{:S(2)}, u32[]{:S(2)}) collective-permute-start(f32[14,8,128]{2,1,0:T(8,128)S(1)} %get-tuple-element.47), channel_id=1, source_target_pairs={{0,2},{2,0},{1,3},{3,1},{4,6},{6,4},{5,7},{7,5},{8,10},{10,8},{9,1... | collective-permute-start | bytes 172040 | tf_op jit(solution)/shard_map/ppermute | solution.py:823
  9.0 0.6 %shard_map.61 = (f32[1,16,32,256]{3,2,1,0:T(8,128)S(1)}, f32[3,2,32,256]{3,2,1,0:T(8,128)S(1)}) custom-call(f32[3,16,32,256]{3,2,1,0:T(8,128)S(1)} %get-tuple-element.27.vel, f32[2,32,256]{2,1,0:T(8,128)S(1)} %get-tuple-element.28.flat, f32[20,32,256]{2,1,0:T(8,128)S(1)} %get-tuple-element.31.q_ref, f32[20,32,256]{2,1,0:T(8,128)S(1)} %get-tuple-element.32.f_ref, ...), custom_call_target="tpu_custom_call" | custom-call | flops 5000000 | bytes 2000000 | tf_op jit(solution)/shard_map/pallas_call | solution.py:25
  9.6 2.2 %collective-permute-start.3 = (f32[3,2,32,256]{3,2,1,0:T(8,128)S(1)}, f32[3,2,32,256]{3,2,1,0:T(8,128)S(1)}, u32[]{:S(2)}, u32[]{:S(2)}) collective-permute-start(f32[3,2,32,256]{3,2,1,0:T(8,128)S(1)} %get-tuple-element.50), channel_id=1, source_target_pairs={{0,1},{1,0},{2,3},{3,2},{4,5},{5,4},{6,7},{7,6},{8,9},{9,8},{10,11... | collective-permute-start | bytes 589832 | tf_op jit(solution)/shard_map/ppermute | solution.py:841
  11.8 1.4 %shard_map.63 = (f32[3,16,8,256]{3,2,1,0:T(8,128)S(1)}, f32[2,2,8,256]{3,2,1,0:T(8,128)S(1)}, f32[5,40,128]{2,1,0:T(8,128)S(1)}) custom-call(f32[3,16,32,256]{3,2,1,0:T(8,128)S(1)} %get-tuple-element.27.vel, f32[2,32,256]{2,1,0:T(8,128)S(1)} %get-tuple-element.28.flat, f32[3,16,8,256]{3,2,1,0:T(8,128)S(1)} %get-tuple-element.39.halo, ...), custom_call_target="tpu_custom_call" | custom-call | flops 10000000 | bytes 2000000 | tf_op jit(solution)/shard_map/pallas_call | solution.py:25
  13.2 0.0 collective-permute-done.2.rest_0_
  13.2 0.6 %shard_map.64 = (f32[3,32,128]{2,1,0:T(8,128)S(1)}, f32[42,8,128]{2,1,0:T(8,128)S(1)}) custom-call(f32[2,25,8,128]{3,2,1,0:T(8,128)S(1)} %get-tuple-element.41.full, f32[2,8,128]{2,1,0:T(8,128)S(1)} %get-tuple-element.42.far, f32[2,32,256]{2,1,0:T(8,128)S(1)} %get-tuple-element.44.shear, f32[2,2,8,256]{3,2,1,0:T(8,128)S(1)} %get-tuple-element.45.strips, ...), custom_call_target="tpu_custom_call" | custom-call | bytes 1000000 | tf_op jit(solution)/shard_map/pallas_call | solution.py:25
  13.8 0.7 %collective-permute-start.4 = (f32[42,8,128]{2,1,0:T(8,128)S(1)}, f32[42,8,128]{2,1,0:T(8,128)S(1)}, u32[]{:S(2)}, u32[]{:S(2)}) collective-permute-start(f32[42,8,128]{2,1,0:T(8,128)S(1)} %get-tuple-element.51.mine), channel_id=1, source_target_pairs={{0,1},{1,0},{2,3},{3,2},{4,5},{5,4},{6,7},{7,6},{8,9},{9,8},{10,11... | collective-permute-start | bytes 516104 | tf_op jit(solution)/shard_map/ppermute | solution.py:852
  14.5 0.0 collective-permute-done.3.far
  14.5 1.3 %shard_map.65 = f32[3,16,32,256]{3,2,1,0:T(8,128)} custom-call(f32[2,16,32,256]{3,2,1,0:T(8,128)S(1)} %get-tuple-element.30.new, f32[1,16,32,256]{3,2,1,0:T(8,128)S(1)} %get-tuple-element.34.new_z.rest_2_, f32[3,16,8,256]{3,2,1,0:T(8,128)S(1)} %get-tuple-element.43.fix, f32[3,32,128]{2,1,0:T(8,128)S(1)} %get-tuple-element.49.fresh, ...), custom_call_target="tpu_custom_call" | custom-call | flops 2000000 | bytes 4000000 | tf_op jit(solution)/shard_map/pallas_call | solution.py:25
  15.8 0.0 collective-permute-done.4.theirs
  15.8 0.9 %shard_map.66 = f32[32,256]{1,0:T(8,128)} custom-call(f32[42,8,128]{2,1,0:T(8,128)S(1)} %get-tuple-element.51.mine, f32[42,8,128]{2,1,0:T(8,128)S(1)} %collective-permute-done.4.theirs), custom_call_target="tpu_custom_call" | custom-call | bytes 1000000 | tf_op jit(solution)/shard_map/pallas_call | solution.py:25
Async XLA Ops:
  2.1 4.5 %collective-permute-start = (f32[14,8,256]{2,1,0:T(8,128)S(1)}, f32[14,8,256]{2,1,0:T(8,128)S(1)}, u32[]{:S(2)}, u32[]{:S(2)}) collective-permute-start(f32[14,8,256]{2,1,0:T(8,128)S(1)} %get-tuple-element.35), channel_id=1, source_target_pairs={{0,4},{1,5},{4,0},{5,1},{8,12},{9,13},{12,8},{13,9},{2,6},{3,7},{6... | collective-permute-start | bytes 344072 | tf_op jit(solution)/shard_map/ppermute | solution.py:798
  3.5 3.9 %collective-permute-start.1 = (f32[14,8,256]{2,1,0:T(8,128)S(1)}, f32[14,8,256]{2,1,0:T(8,128)S(1)}, u32[]{:S(2)}, u32[]{:S(2)}) collective-permute-start(f32[14,8,256]{2,1,0:T(8,128)S(1)} %get-tuple-element.36), channel_id=1, source_target_pairs={{0,1},{1,0},{4,8},{5,9},{8,4},{9,5},{12,13},{13,12},{2,3},{3,2},{6... | collective-permute-start | bytes 344072 | tf_op jit(solution)/shard_map/ppermute | solution.py:797
  7.7 5.5 %collective-permute-start.2 = (f32[14,8,128]{2,1,0:T(8,128)S(1)}, f32[14,8,128]{2,1,0:T(8,128)S(1)}, u32[]{:S(2)}, u32[]{:S(2)}) collective-permute-start(f32[14,8,128]{2,1,0:T(8,128)S(1)} %get-tuple-element.47), channel_id=1, source_target_pairs={{0,2},{2,0},{1,3},{3,1},{4,6},{6,4},{5,7},{7,5},{8,10},{10,8},{9,1... | collective-permute-start | bytes 172040 | tf_op jit(solution)/shard_map/ppermute | solution.py:823
  9.6 4.9 %collective-permute-start.3 = (f32[3,2,32,256]{3,2,1,0:T(8,128)S(1)}, f32[3,2,32,256]{3,2,1,0:T(8,128)S(1)}, u32[]{:S(2)}, u32[]{:S(2)}) collective-permute-start(f32[3,2,32,256]{3,2,1,0:T(8,128)S(1)} %get-tuple-element.50), channel_id=1, source_target_pairs={{0,1},{1,0},{2,3},{3,2},{4,5},{5,4},{6,7},{7,6},{8,9},{9,8},{10,11... | collective-permute-start | bytes 589832 | tf_op jit(solution)/shard_map/ppermute | solution.py:841
  13.8 2.0 %collective-permute-start.4 = (f32[42,8,128]{2,1,0:T(8,128)S(1)}, f32[42,8,128]{2,1,0:T(8,128)S(1)}, u32[]{:S(2)}, u32[]{:S(2)}) collective-permute-start(f32[42,8,128]{2,1,0:T(8,128)S(1)} %get-tuple-element.51.mine), channel_id=1, source_target_pairs={{0,1},{1,0},{2,3},{3,2},{4,5},{5,4},{6,7},{7,6},{8,9},{9,8},{10,11... | collective-permute-start | bytes 516104 | tf_op jit(solution)/shard_map/ppermute | solution.py:852

commit v11 on v10

--- a/solution.py
+++ b/solution.py
@@ -242,7 +242,7 @@
                     split_ref[c, at, i * cols + k * LANE : i * cols + (k + 1) * LANE] = part
         return carry
 
-    lax.fori_loop(0, layers, prepare, 0, unroll=2)
+    lax.fori_loop(0, layers, prepare, 0, unroll=4)
     for c in range(3):
         x_ref[c][...] = jnp.dot(split_ref[c], band_ref[...], preferred_element_type=jnp.float32)
 

time: 16.8 us -> 16.9 us (level)
  no operation moved by 1% of the time
where the time goes in v11:
time: 16.9 us; the launch traced here: 16.7 us
  Pallas kernels  9.81 us (58%)
  starting transfers between devices  5.53 us (33%)
  between operations  0.7 us (4%)
  waiting for transfers between devices  0.64 us (4%)
    pallas_call x8, Pallas kernels, call(): pl.pallas_call(kernel, out_shape=shapes, in_specs=specs, out_specs=[pl.Bl...  9.81 us
    ppermute x1, starting transfers between devices, body(): got_z = lax.ppermute(send_z, 'wall', pairings('wall')[0])  2.22 us
    ppermute x1, starting transfers between devices, body(): got_a = lax.ppermute(send_a, ('plane', 'wall'), plane_a)  1.36 us
    ppermute x1, starting transfers between devices, body(): lax.ppermute(m, 'span', pairs)  1.25 us
    ppermute x1, starting transfers between devices, body(): theirs = lax.ppermute(mine, 'wall', pairings('wall')[0])  0.69 us
    ppermute x1, waiting for transfers between devices, body(): got_b = lax.ppermute(send_b, ('plane', 'wall'), plane_b)  0.63 us
  transfers between devices with their start and end apart: 5, of which 1 were waited for; matrix products, arithmetic and copies ran while one was open for 0% of the time, Pallas kernels for 42%

profile of v11, /device:TPU:17, one launch (start us, length us, event | category | flops | bytes accessed | tf_op | source)
XLA Modules:
  0.0 16.7 jit_solution(9124931256844801937)
XLA Ops:
  0.6 1.5 %shard_map.59 = (f32[14,8,256]{2,1,0:T(8,128)S(1)}, f32[14,8,256]{2,1,0:T(8,128)S(1)}, f32[3,16,32,256]{3,2,1,0:T(8,128)S(1)}, f32[2,32,256]{2,1,0:T(8,128)S(1)}...) custom-call(f32[3,16,32,256]{3,2,1,0:T(8,128)} %vel_in.1, s32[32,256]{1,0:T(8,128)} %lev_in.1, f32[32,256]{1,0:T(8,128)} %frac_in.1, ...), custom_call_target="tpu_custom_call" | custom-call | bytes 1000000 | tf_op jit(solution)/shard_map/pallas_call | solution.py:25
  2.1 1.4 %collective-permute-start = (f32[14,8,256]{2,1,0:T(8,128)S(1)}, f32[14,8,256]{2,1,0:T(8,128)S(1)}, u32[]{:S(2)}, u32[]{:S(2)}) collective-permute-start(f32[14,8,256]{2,1,0:T(8,128)S(1)} %get-tuple-element.35), channel_id=1, source_target_pairs={{0,4},{1,5},{4,0},{5,1},{8,12},{9,13},{12,8},{13,9},{2,6},{3,7},{6... | collective-permute-start | bytes 344072 | tf_op jit(solution)/shard_map/ppermute | solution.py:798
  3.5 0.0 collective-permute-start.1
  3.5 3.2 %shard_map.60 = (f32[2,16,32,256]{3,2,1,0:T(8,128)S(1)}, f32[2,32,256]{2,1,0:T(8,128)S(1)}, f32[2,5,4,8,128]{4,3,2,1,0:T(8,128)S(1)}, f32[20,32,256]{2,1,0:T(8,1...) custom-call(f32[3,16,32,256]{3,2,1,0:T(8,128)S(1)} %get-tuple-element.27.vel, ...), custom_call_target="tpu_custom_call" | custom-call | flops 20000000 | bytes 3000000 | tf_op jit(solution)/shard_map/pallas_call | solution.py:25
  6.7 0.0 collective-permute-done.got_a
  6.7 0.6 %collective-permute-done.1.got_b = f32[14,8,256]{2,1,0:T(8,128)S(1)} collective-permute-done((f32[14,8,256]{2,1,0:T(8,128)S(1)}, f32[14,8,256]{2,1,0:T(8,128)S(1)}, u32[]{:S(2)}, u32[]{:S(2)}) %collective-permute-start.1) | collective-permute-done | bytes 114720 | tf_op jit(solution)/shard_map/ppermute | solution.py:797
  7.4 0.4 %shard_map.62 = (f32[3,16,8,256]{3,2,1,0:T(8,128)S(1)}, f32[4,8,256]{2,1,0:T(8,128)S(1)}, f32[2,25,8,128]{3,2,1,0:T(8,128)S(1)}, f32[2,8,128]{2,1,0:T(8,128)S(1)...) custom-call(f32[14,8,256]{2,1,0:T(8,128)S(1)} %collective-permute-done.got_a, ...), custom_call_target="tpu_custom_call" | custom-call | bytes 1000000 | tf_op jit(solution)/shard_map/pallas_call | solution.py:25
  7.7 1.3 %collective-permute-start.2 = (f32[14,8,128]{2,1,0:T(8,128)S(1)}, f32[14,8,128]{2,1,0:T(8,128)S(1)}, u32[]{:S(2)}, u32[]{:S(2)}) collective-permute-start(f32[14,8,128]{2,1,0:T(8,128)S(1)} %get-tuple-element.47), channel_id=1, source_target_pairs={{0,2},{2,0},{1,3},{3,1},{4,6},{6,4},{5,7},{7,5},{8,10},{10,8},{9,1... | collective-permute-start | bytes 172040 | tf_op jit(solution)/shard_map/ppermute | solution.py:823
  9.0 0.6 %shard_map.61 = (f32[1,16,32,256]{3,2,1,0:T(8,128)S(1)}, f32[3,2,32,256]{3,2,1,0:T(8,128)S(1)}) custom-call(f32[3,16,32,256]{3,2,1,0:T(8,128)S(1)} %get-tuple-element.27.vel, f32[2,32,256]{2,1,0:T(8,128)S(1)} %get-tuple-element.28.flat, f32[20,32,256]{2,1,0:T(8,128)S(1)} %get-tuple-element.31.q_ref, f32[20,32,256]{2,1,0:T(8,128)S(1)} %get-tuple-element.32.f_ref, ...), custom_call_target="tpu_custom_call" | custom-call | flops 5000000 | bytes 2000000 | tf_op jit(solution)/shard_map/pallas_call | solution.py:25
  9.6 2.2 %collective-permute-start.3 = (f32[3,2,32,256]{3,2,1,0:T(8,128)S(1)}, f32[3,2,32,256]{3,2,1,0:T(8,128)S(1)}, u32[]{:S(2)}, u32[]{:S(2)}) collective-permute-start(f32[3,2,32,256]{3,2,1,0:T(8,128)S(1)} %get-tuple-element.50), channel_id=1, source_target_pairs={{0,1},{1,0},{2,3},{3,2},{4,5},{5,4},{6,7},{7,6},{8,9},{9,8},{10,11... | collective-permute-start | bytes 589832 | tf_op jit(solution)/shard_map/ppermute | solution.py:841
  11.8 1.4 %shard_map.63 = (f32[3,16,8,256]{3,2,1,0:T(8,128)S(1)}, f32[2,2,8,256]{3,2,1,0:T(8,128)S(1)}, f32[5,40,128]{2,1,0:T(8,128)S(1)}) custom-call(f32[3,16,32,256]{3,2,1,0:T(8,128)S(1)} %get-tuple-element.27.vel, f32[2,32,256]{2,1,0:T(8,128)S(1)} %get-tuple-element.28.flat, f32[3,16,8,256]{3,2,1,0:T(8,128)S(1)} %get-tuple-element.39.halo, ...), custom_call_target="tpu_custom_call" | custom-call | flops 10000000 | bytes 2000000 | tf_op jit(solution)/shard_map/pallas_call | solution.py:25
  13.2 0.0 collective-permute-done.2.rest_0_
  13.2 0.6 %shard_map.64 = (f32[3,32,128]{2,1,0:T(8,128)S(1)}, f32[42,8,128]{2,1,0:T(8,128)S(1)}) custom-call(f32[2,25,8,128]{3,2,1,0:T(8,128)S(1)} %get-tuple-element.41.full, f32[2,8,128]{2,1,0:T(8,128)S(1)} %get-tuple-element.42.far, f32[2,32,256]{2,1,0:T(8,128)S(1)} %get-tuple-element.44.shear, f32[2,2,8,256]{3,2,1,0:T(8,128)S(1)} %get-tuple-element.45.strips, ...), custom_call_target="tpu_custom_call" | custom-call | bytes 1000000 | tf_op jit(solution)/shard_map/pallas_call | solution.py:25
  13.8 0.7 %collective-permute-start.4 = (f32[42,8,128]{2,1,0:T(8,128)S(1)}, f32[42,8,128]{2,1,0:T(8,128)S(1)}, u32[]{:S(2)}, u32[]{:S(2)}) collective-permute-start(f32[42,8,128]{2,1,0:T(8,128)S(1)} %get-tuple-element.51.mine), channel_id=1, source_target_pairs={{0,1},{1,0},{2,3},{3,2},{4,5},{5,4},{6,7},{7,6},{8,9},{9,8},{10,11... | collective-permute-start | bytes 516104 | tf_op jit(solution)/shard_map/ppermute | solution.py:852
  14.5 0.0 collective-permute-done.3.far
  14.5 1.3 %shard_map.65 = f32[3,16,32,256]{3,2,1,0:T(8,128)} custom-call(f32[2,16,32,256]{3,2,1,0:T(8,128)S(1)} %get-tuple-element.30.new, f32[1,16,32,256]{3,2,1,0:T(8,128)S(1)} %get-tuple-element.34.new_z.rest_2_, f32[3,16,8,256]{3,2,1,0:T(8,128)S(1)} %get-tuple-element.43.fix, f32[3,32,128]{2,1,0:T(8,128)S(1)} %get-tuple-element.49.fresh, ...), custom_call_target="tpu_custom_call" | custom-call | flops 2000000 | bytes 4000000 | tf_op jit(solution)/shard_map/pallas_call | solution.py:25
  15.8 0.0 collective-permute-done.4.theirs
  15.8 0.9 %shard_map.66 = f32[32,256]{1,0:T(8,128)} custom-call(f32[42,8,128]{2,1,0:T(8,128)S(1)} %get-tuple-element.51.mine, f32[42,8,128]{2,1,0:T(8,128)S(1)} %collective-permute-done.4.theirs), custom_call_target="tpu_custom_call" | custom-call | bytes 1000000 | tf_op jit(solution)/shard_map/pallas_call | solution.py:25
Async XLA Ops:
  2.1 4.6 %collective-permute-start = (f32[14,8,256]{2,1,0:T(8,128)S(1)}, f32[14,8,256]{2,1,0:T(8,128)S(1)}, u32[]{:S(2)}, u32[]{:S(2)}) collective-permute-start(f32[14,8,256]{2,1,0:T(8,128)S(1)} %get-tuple-element.35), channel_id=1, source_target_pairs={{0,4},{1,5},{4,0},{5,1},{8,12},{9,13},{12,8},{13,9},{2,6},{3,7},{6... | collective-permute-start | bytes 344072 | tf_op jit(solution)/shard_map/ppermute | solution.py:798
  3.5 3.9 %collective-permute-start.1 = (f32[14,8,256]{2,1,0:T(8,128)S(1)}, f32[14,8,256]{2,1,0:T(8,128)S(1)}, u32[]{:S(2)}, u32[]{:S(2)}) collective-permute-start(f32[14,8,256]{2,1,0:T(8,128)S(1)} %get-tuple-element.36), channel_id=1, source_target_pairs={{0,1},{1,0},{4,8},{5,9},{8,4},{9,5},{12,13},{13,12},{2,3},{3,2},{6... | collective-permute-start | bytes 344072 | tf_op jit(solution)/shard_map/ppermute | solution.py:797
  7.7 5.5 %collective-permute-start.2 = (f32[14,8,128]{2,1,0:T(8,128)S(1)}, f32[14,8,128]{2,1,0:T(8,128)S(1)}, u32[]{:S(2)}, u32[]{:S(2)}) collective-permute-start(f32[14,8,128]{2,1,0:T(8,128)S(1)} %get-tuple-element.47), channel_id=1, source_target_pairs={{0,2},{2,0},{1,3},{3,1},{4,6},{6,4},{5,7},{7,5},{8,10},{10,8},{9,1... | collective-permute-start | bytes 172040 | tf_op jit(solution)/shard_map/ppermute | solution.py:823
  9.6 4.9 %collective-permute-start.3 = (f32[3,2,32,256]{3,2,1,0:T(8,128)S(1)}, f32[3,2,32,256]{3,2,1,0:T(8,128)S(1)}, u32[]{:S(2)}, u32[]{:S(2)}) collective-permute-start(f32[3,2,32,256]{3,2,1,0:T(8,128)S(1)} %get-tuple-element.50), channel_id=1, source_target_pairs={{0,1},{1,0},{2,3},{3,2},{4,5},{5,4},{6,7},{7,6},{8,9},{9,8},{10,11... | collective-permute-start | bytes 589832 | tf_op jit(solution)/shard_map/ppermute | solution.py:841
  13.8 2.0 %collective-permute-start.4 = (f32[42,8,128]{2,1,0:T(8,128)S(1)}, f32[42,8,128]{2,1,0:T(8,128)S(1)}, u32[]{:S(2)}, u32[]{:S(2)}) collective-permute-start(f32[42,8,128]{2,1,0:T(8,128)S(1)} %get-tuple-element.51.mine), channel_id=1, source_target_pairs={{0,1},{1,0},{2,3},{3,2},{4,5},{5,4},{6,7},{7,6},{8,9},{9,8},{10,11... | collective-permute-start | bytes 516104 | tf_op jit(solution)/shard_map/ppermute | solution.py:852
